TPU v7x, 512 devices: a whole 4x4x16 slice. The times are simulated.
512 devices in a mesh: dom: 64 (over x, z), orb: 8 (over y, core).
Axes of the slice: x: 4, y: 4, z: 16, core: 2. Of those that a mesh axis runs over, the one named last changes fastest.
Arguments:
- orbitals: bfloat16 [3072, 64, 512], P('dom', 'orb'), may hold values from -6 to 6
- adjoint_source: bfloat16 [3072, 64, 512], P('dom', 'orb'), may hold values from -6 to 6
- eigenvalues: float32 [64], P('orb'), may hold values from -1 to -0.25
- cell_scale: float32 [3072], P('dom'), may hold values from 0.4 to 1.6
- base_potential: float32 [3072, 512], P('dom'), may hold values from 0.5 to 1.5
- stiffness: bfloat16 [512, 512], replicated, may hold values from -1.5 to 1.5, as said below
- face_perm: int32 [3072, 64], P('dom'), may hold values from 0 to 63, each once within a row
- restrict: bfloat16 [512, 64], replicated, may hold values from -0.25 to 0.25
- prolong: bfloat16 [64, 512], replicated, may hold values from -0.75 to 0.75
- owner: int32 [3072, 1], P('dom'), may hold values from 0 to 63; in each aligned block of 48 rows (0 to 47, 48 to 95, ...) at most 2 rows name the same one
- pot_slot: int32 [3072], P('dom'), may hold values from 0 to 63
- potential: float32 [4096, 64], P('dom'), may hold values from -6 to 6
Outputs:
- adjoint: bfloat16 [3072, 64, 512], P('dom', 'orb')
- updated: float32 [4096, 64], P('dom')
- applied: bfloat16 [3072, 64, 512], P('dom', 'orb')
Inputs may be any that keep to these rules, and one draw needn't show every extreme that they name: In the rows of one device no owner is named by more than 2 cells. `face_perm`: each row is a permutation. `stiffness`: symmetric.
All inputs are finite; a program needn't handle non-finite values.
Results may differ from a plain program's by a relative error of at most 0.0027.
Values sent between devices are 32-bit elements; how exact they have to be, the bound alone decides.
No kernel may reach another device: no remote copies, remote signals or barrier semaphores. Data moves between devices by JAX's collectives and lax.ppermute only.
A program may use at most 64 MiB of HBM per device.

v0:
```python
import jax
import jax.numpy as jnp
from jax import lax
from jax.sharding import PartitionSpec as P

ITERS = 4


relax = 0.25
step_rate = 0.1


def padded_2(block, sides, width):
    for axis, dim in sides:
        count = lax.axis_size(axis)
        forward = [(i, i + 1) for i in range(count - 1)]
        backward = [(target, source) for source, target in forward]
        low = lax.ppermute(
            lax.slice_in_dim(block, block.shape[dim] - width, None, axis=dim), axis, forward
        )
        high = lax.ppermute(lax.slice_in_dim(block, 0, width, axis=dim), axis, backward)
        block = jnp.concatenate([low, block, high], axis=dim)
    return block


def local(
    orbitals,
    adjoint_source,
    eigenvalues,
    cell_scale,
    base_potential,
    stiffness,
    face_perm,
    restrict,
    prolong,
    owner,
    pot_slot,
    potential,
):
    nodes = stiffness.shape[0]
    faces = face_perm.shape[1]
    pot_rows = potential.shape[0]
    n_domains = lax.axis_size("dom")
    cell_count = owner.shape[0]
    capacity = 2 * ((cell_count + n_domains - 1) // n_domains)
    onehot = (face_perm[:, :, None] == jnp.arange(faces, dtype=jnp.int32)[None, None, :]).astype(
        jnp.float32
    )

    def assemble_local(partial_sum):
        left_face = partial_sum[:, :, :faces]
        right_face = partial_sum[:, :, nodes - faces :]
        sent_right = jnp.einsum("ckj,cok->coj", onehot, right_face, precision=lax.Precision.HIGHEST)
        boundary = jnp.stack([left_face[0], sent_right[-1]], 0)
        padded = padded_2(boundary, (("dom", 0),), 1)
        left_next = jnp.concatenate([left_face[1:], padded[3][None]], 0)
        add_right = jnp.einsum("ckj,coj->cok", onehot, left_next, precision=lax.Precision.HIGHEST)
        add_left = jnp.concatenate([padded[0][None], sent_right[:-1]], 0)
        return jnp.concatenate(
            [
                left_face + add_left,
                partial_sum[:, :, faces : nodes - faces],
                right_face + add_right,
            ],
            2,
        )

    def operator(values_bf, values_full, shift):
        kinetic = jnp.dot(
            values_bf.reshape(-1, nodes), stiffness, preferred_element_type=jnp.float32
        ).reshape(values_full.shape)
        return assemble_local(cell_scale[:, None, None] * kinetic + shift * values_full)

    source = adjoint_source.astype(jnp.float32)
    shift = base_potential[:, None, :] - eigenvalues[None, :, None]
    iterate = relax * source
    for step_index in range(ITERS):
        image = operator(iterate.astype(jnp.bfloat16), iterate, shift)
        iterate = iterate + relax * (source - image)
    adjoint = iterate.astype(jnp.bfloat16)
    partial_density = jnp.sum(orbitals.astype(jnp.float32) * iterate, axis=1)
    restrict_full = restrict.astype(jnp.float32)
    density_term = lax.psum(partial_density, "orb")
    projected = jnp.dot(density_term, restrict_full, precision=lax.Precision.HIGHEST)
    coarse_cols = projected.shape[1]
    dest_owner = owner[:, 0]
    owner_hot = (dest_owner[:, None] == jnp.arange(n_domains, dtype=jnp.int32)[None, :]).astype(
        jnp.int32
    )
    earlier = jnp.cumsum(owner_hot, axis=0) - owner_hot
    rank_within = jnp.sum(earlier * owner_hot, axis=1)
    slot_index = dest_owner * capacity + rank_within
    send_hot_int = (
        slot_index[None, :] == jnp.arange(n_domains * capacity, dtype=jnp.int32)[:, None]
    ).astype(jnp.int32)
    send_hot = send_hot_int.astype(jnp.float32)
    send_values = jnp.dot(send_hot, projected, precision=lax.Precision.HIGHEST).reshape(
        n_domains, capacity, coarse_cols
    )
    send_ids = (jnp.sum(send_hot_int * (pot_slot + 1)[None, :], axis=1) - 1).reshape(
        n_domains, capacity
    )
    recv_values, recv_ids = (
        lax.all_to_all(send_values, "dom", split_axis=0, concat_axis=0, tiled=True),
        lax.all_to_all(send_ids, "dom", split_axis=0, concat_axis=0, tiled=True),
    )
    recv_hot = (
        recv_ids.reshape(-1)[None, :] == jnp.arange(pot_rows, dtype=jnp.int32)[:, None]
    ).astype(jnp.float32)
    summed = jnp.dot(
        recv_hot, recv_values.reshape(-1, coarse_cols), precision=lax.Precision.HIGHEST
    )
    updated = potential - step_rate * summed
    every_pot = lax.all_gather(updated, "dom", axis=0, tiled=True)
    cell_pot = every_pot[dest_owner * pot_rows + pot_slot]
    node_potential = jnp.dot(cell_pot, prolong.astype(jnp.float32), precision=lax.Precision.HIGHEST)
    shift_new = (base_potential + node_potential)[:, None, :]
    applied = operator(orbitals, orbitals.astype(jnp.float32), shift_new).astype(jnp.bfloat16)
    return (adjoint, updated, applied)


def solution(mesh):
    in_specs = (
        P("dom", "orb", None),
        P("dom", "orb", None),
        P("orb"),
        P("dom"),
        P("dom", None),
        P(),
        P("dom", None),
        P(),
        P(),
        P("dom", None),
        P("dom"),
        P("dom", None),
    )
    out_specs = (P("dom", "orb", None), P("dom", None), P("dom", "orb", None))
    return jax.shard_map(local, mesh=mesh, in_specs=in_specs, out_specs=out_specs, check_vma=False)
```

profile of v0, /device:TPU:6, one launch (start us, length us, event | category | flops | bytes accessed | tf_op | source)
XLA Modules:
  0.0 320.7 jit_solution(6365384118985894531)
XLA Ops:
  8.2 1.6 fusion.10
  9.8 11.7 %collective-permute-start.1 = (f32[1,8,64]{2,1,0:T(8,128)S(1)}, f32[1,8,64]{2,1,0:T(8,128)S(1)}, u32[]{:S(2)}, u32[]{:S(2)}) collective-permute-start(f32[1,8,64]{2,1,0:T(8,128)S(1)} %slice.159), channel_id=1, source_target_pairs={{8,0},{16,8},{24,16},{32,24},{40,32},{48,40},{56,48},{64,56},{72,6... | collective-permute-start | bytes 6152 | tf_op jit(solution)/shard_map/ppermute | solution.py:21
  22.9 1.9 collective-permute-start
  27.1 3.5 %collective-permute-done = f32[1,8,64]{2,1,0:T(8,128)S(1)} collective-permute-done((f32[1,8,64]{2,1,0:T(8,128)S(1)}, f32[1,8,64]{2,1,0:T(8,128)S(1)}, u32[]{:S(2)}, u32[]{:S(2)}) %collective-permute-start) | collective-permute-done | bytes 2080 | tf_op jit(solution)/shard_map/ppermute | solution.py:18
  31.5 2.6 collective-permute-start.3
  35.8 3.3 %collective-permute-start.2 = (f32[1,8,64]{2,1,0:T(8,128)S(1)}, f32[1,8,64]{2,1,0:T(8,128)S(1)}, u32[]{:S(2)}, u32[]{:S(2)}) collective-permute-start(f32[1,8,64]{2,1,0:T(8,128)S(1)} %slice.162), channel_id=1, source_target_pairs={{0,8},{8,16},{16,24},{24,32},{32,40},{40,48},{48,56},{56,64},{64,7... | collective-permute-start | bytes 6152 | tf_op jit(solution)/shard_map/ppermute | solution.py:18
  40.5 2.9 collective-permute-done.2
  44.5 1.9 collective-permute-start.5
  48.1 3.9 %collective-permute-start.4 = (f32[1,8,64]{2,1,0:T(8,128)S(1)}, f32[1,8,64]{2,1,0:T(8,128)S(1)}, u32[]{:S(2)}, u32[]{:S(2)}) collective-permute-start(f32[1,8,64]{2,1,0:T(8,128)S(1)} %slice.169), channel_id=1, source_target_pairs={{0,8},{8,16},{16,24},{24,32},{32,40},{40,48},{48,56},{56,64},{64,7... | collective-permute-start | bytes 6152 | tf_op jit(solution)/shard_map/ppermute | solution.py:18
  53.5 2.3 collective-permute-done.4
  56.6 1.9 collective-permute-start.7
  60.3 3.9 %collective-permute-start.6 = (f32[1,8,64]{2,1,0:T(8,128)S(1)}, f32[1,8,64]{2,1,0:T(8,128)S(1)}, u32[]{:S(2)}, u32[]{:S(2)}) collective-permute-start(f32[1,8,64]{2,1,0:T(8,128)S(1)} %slice.176), channel_id=1, source_target_pairs={{0,8},{8,16},{16,24},{24,32},{32,40},{40,48},{48,56},{56,64},{64,7... | collective-permute-start | bytes 6152 | tf_op jit(solution)/shard_map/ppermute | solution.py:18
  65.6 2.3 collective-permute-done.6
  68.0 2.1 fusion.24
  70.8 5.5 %all-to-all-start = ((s32[64,1,2]{2,1,0:T(1,128)}), s32[64,1,2]{2,1,0:T(1,128)S(1)}, u32[]{:S(2)}, u32[]{:S(2)}) async-start(s32[64,1,2]{2,1,0:T(1,128)} %bitcast.2), calls=%async_computation | async-start | bytes 65536 | tf_op jit(solution)/shard_map/all_to_all | solution.py:105
  76.4 57.9 %all-reduce.2.cloned.1.call-done = f32[48,512]{1,0:T(8,128)} async-done(((f32[48,512]{1,0:T(8,128)}), f32[48,512]{1,0:T(8,128)}) %all-reduce.2.cloned.1.call-update) | async-done | bytes 98320 | tf_op jit(solution)/shard_map/psum | solution.py:83
  136.4 16.1 %all-to-all-start.1 = ((f32[64,1,128]{2,1,0:T(1,128)}), f32[64,1,128]{2,1,0:T(1,128)S(1)}, u32[]{:S(2)}, u32[]{:S(2)}) async-start(f32[64,1,128]{2,1,0:T(1,128)} %reshape.85), calls=%async_computation.1 | async-start | bytes 65536 | tf_op jit(solution)/shard_map/all_to_all | solution.py:104
  154.0 11.0 %all-to-all-done.1 = f32[64,1,128]{2,1,0:T(1,128)S(1)} async-done(((f32[64,1,128]{2,1,0:T(1,128)}), f32[64,1,128]{2,1,0:T(1,128)S(1)}, u32[]{:S(2)}, u32[]{:S(2)}) %all-to-all-start.1) | async-done | bytes 32800 | tf_op jit(solution)/shard_map/all_to_all | solution.py:104
  167.2 128.7 %all-gather.2.cloned.1.call-done = f32[4096,64]{1,0:T(8,128)} async-done(((f32[64,64]{1,0:T(8,128)}), f32[4096,64]{1,0:T(8,128)}) %all-gather.2.cloned.1.call-update) | async-done | bytes 1048592 | tf_op jit(solution)/shard_map/all_gather | solution.py:114
  295.9 2.2 gather_fusion
  298.7 4.9 %collective-permute-start.9 = (f32[1,8,64]{2,1,0:T(8,128)S(1)}, f32[1,8,64]{2,1,0:T(8,128)S(1)}, u32[]{:S(2)}, u32[]{:S(2)}) collective-permute-start(f32[1,8,64]{2,1,0:T(8,128)S(1)} %slice.187), channel_id=1, source_target_pairs={{8,0},{16,8},{24,16},{32,24},{40,32},{48,40},{56,48},{64,56},{72,6... | collective-permute-start | bytes 6152 | tf_op jit(solution)/shard_map/ppermute | solution.py:21
  305.2 1.9 collective-permute-start.8
  307.2 1.6 fusion.20
  308.8 4.1 %collective-permute-done.8 = f32[1,8,64]{2,1,0:T(8,128)S(1)} collective-permute-done((f32[1,8,64]{2,1,0:T(8,128)S(1)}, f32[1,8,64]{2,1,0:T(8,128)S(1)}, u32[]{:S(2)}, u32[]{:S(2)}) %collective-permute-start.8) | collective-permute-done | bytes 2080 | tf_op jit(solution)/shard_map/ppermute | solution.py:18
  (98 shorter events, 26.3 us)
Async XLA Ops:
  7.2 14.3 %copy-start.11 = (s32[48,64]{1,0:T(8,128)S(1)}, s32[48,64]{1,0:T(8,128)}, u32[]{:S(2)}) copy-start(s32[48,64]{1,0:T(8,128)} %param.18) | copy-start | bytes 36868
  7.2 17.7 %copy-start.7 = (s32[48,1]{0,1:T(1,128)S(1)}, s32[48,1]{0,1:T(1,128)}, u32[]{:S(2)}) copy-start(s32[48,1]{0,1:T(1,128)} %param.21) | copy-start | bytes 580
  7.2 18.0 %copy-start.9 = (s32[48]{0:T(128)S(1)}, s32[48]{0:T(128)}, u32[]{:S(2)}) copy-start(s32[48]{0:T(128)} %param.22) | copy-start | bytes 580
  7.2 127.1 %all-reduce.2.cloned.1.call-start = ((), (), s32[]{:S(2)}) async-start(), calls=%async_computation.2 | async-start | bytes 196608 | tf_op jit(solution)/shard_map/psum | solution.py:83
  9.8 15.8 %collective-permute-start.1 = (f32[1,8,64]{2,1,0:T(8,128)S(1)}, f32[1,8,64]{2,1,0:T(8,128)S(1)}, u32[]{:S(2)}, u32[]{:S(2)}) collective-permute-start(f32[1,8,64]{2,1,0:T(8,128)S(1)} %slice.159), channel_id=1, source_target_pairs={{8,0},{16,8},{24,16},{32,24},{40,32},{48,40},{56,48},{64,56},{72,6... | collective-permute-start | bytes 6152 | tf_op jit(solution)/shard_map/ppermute | solution.py:21
  22.9 7.6 %collective-permute-start = (f32[1,8,64]{2,1,0:T(8,128)S(1)}, f32[1,8,64]{2,1,0:T(8,128)S(1)}, u32[]{:S(2)}, u32[]{:S(2)}) collective-permute-start(f32[1,8,64]{2,1,0:T(8,128)S(1)} %slice.155), channel_id=1, source_target_pairs={{0,8},{8,16},{16,24},{24,32},{32,40},{40,48},{48,56},{56,64},{64,7... | collective-permute-start | bytes 6152 | tf_op jit(solution)/shard_map/ppermute | solution.py:18
  25.3 5.3 %copy-start.1 = (bf16[48,8,512]{2,1,0:T(8,128)(2,1)S(1)}, bf16[48,8,512]{2,1,0:T(8,128)(2,1)}, u32[]{:S(2)}) copy-start(bf16[48,8,512]{2,1,0:T(8,128)(2,1)} %param.13) | copy-start | bytes 1179652
  25.3 5.3 %copy-start.3 = (f32[48,512]{1,0:T(8,128)S(1)}, f32[48,512]{1,0:T(8,128)}, u32[]{:S(2)}) copy-start(f32[48,512]{1,0:T(8,128)} %param.16) | copy-start | bytes 294916
  25.4 5.3 %copy-start.8 = (f32[48]{0:T(128)S(1)}, f32[48]{0:T(128)}, u32[]{:S(2)}) copy-start(f32[48]{0:T(128)} %param.15) | copy-start | bytes 580
  31.5 7.6 %collective-permute-start.3 = (f32[1,8,64]{2,1,0:T(8,128)S(1)}, f32[1,8,64]{2,1,0:T(8,128)S(1)}, u32[]{:S(2)}, u32[]{:S(2)}) collective-permute-start(f32[1,8,64]{2,1,0:T(8,128)S(1)} %slice.166), channel_id=1, source_target_pairs={{8,0},{16,8},{24,16},{32,24},{40,32},{48,40},{56,48},{64,56},{72,6... | collective-permute-start | bytes 6152 | tf_op jit(solution)/shard_map/ppermute | solution.py:21
  35.8 7.6 %collective-permute-start.2 = (f32[1,8,64]{2,1,0:T(8,128)S(1)}, f32[1,8,64]{2,1,0:T(8,128)S(1)}, u32[]{:S(2)}, u32[]{:S(2)}) collective-permute-start(f32[1,8,64]{2,1,0:T(8,128)S(1)} %slice.162), channel_id=1, source_target_pairs={{0,8},{8,16},{16,24},{24,32},{32,40},{40,48},{48,56},{56,64},{64,7... | collective-permute-start | bytes 6152 | tf_op jit(solution)/shard_map/ppermute | solution.py:18
  44.5 7.6 %collective-permute-start.5 = (f32[1,8,64]{2,1,0:T(8,128)S(1)}, f32[1,8,64]{2,1,0:T(8,128)S(1)}, u32[]{:S(2)}, u32[]{:S(2)}) collective-permute-start(f32[1,8,64]{2,1,0:T(8,128)S(1)} %slice.173), channel_id=1, source_target_pairs={{8,0},{16,8},{24,16},{32,24},{40,32},{48,40},{56,48},{64,56},{72,6... | collective-permute-start | bytes 6152 | tf_op jit(solution)/shard_map/ppermute | solution.py:21
  48.1 7.6 %collective-permute-start.4 = (f32[1,8,64]{2,1,0:T(8,128)S(1)}, f32[1,8,64]{2,1,0:T(8,128)S(1)}, u32[]{:S(2)}, u32[]{:S(2)}) collective-permute-start(f32[1,8,64]{2,1,0:T(8,128)S(1)} %slice.169), channel_id=1, source_target_pairs={{0,8},{8,16},{16,24},{24,32},{32,40},{40,48},{48,56},{56,64},{64,7... | collective-permute-start | bytes 6152 | tf_op jit(solution)/shard_map/ppermute | solution.py:18
  56.6 7.6 %collective-permute-start.7 = (f32[1,8,64]{2,1,0:T(8,128)S(1)}, f32[1,8,64]{2,1,0:T(8,128)S(1)}, u32[]{:S(2)}, u32[]{:S(2)}) collective-permute-start(f32[1,8,64]{2,1,0:T(8,128)S(1)} %slice.180), channel_id=1, source_target_pairs={{8,0},{16,8},{24,16},{32,24},{40,32},{48,40},{56,48},{64,56},{72,6... | collective-permute-start | bytes 6152 | tf_op jit(solution)/shard_map/ppermute | solution.py:21
  60.0 8.0 %copy-start.2 = (bf16[48,8,512]{2,1,0:T(8,128)(2,1)S(1)}, bf16[48,8,512]{2,1,0:T(8,128)(2,1)}, u32[]{:S(2)}) copy-start(bf16[48,8,512]{2,1,0:T(8,128)(2,1)} %param.12) | copy-start | bytes 1179652
  60.3 7.6 %collective-permute-start.6 = (f32[1,8,64]{2,1,0:T(8,128)S(1)}, f32[1,8,64]{2,1,0:T(8,128)S(1)}, u32[]{:S(2)}, u32[]{:S(2)}) collective-permute-start(f32[1,8,64]{2,1,0:T(8,128)S(1)} %slice.176), channel_id=1, source_target_pairs={{0,8},{8,16},{16,24},{24,32},{32,40},{40,48},{48,56},{56,64},{64,7... | collective-permute-start | bytes 6152 | tf_op jit(solution)/shard_map/ppermute | solution.py:18
  67.9 66.4 %copy-start.4 = (bf16[512,64]{0,1:T(8,128)(2,1)S(1)}, bf16[512,64]{0,1:T(8,128)(2,1)}, u32[]{:S(2)}) copy-start(bf16[512,64]{0,1:T(8,128)(2,1)} %param.19) | copy-start | bytes 196612
  67.9 98.4 %copy-start.6 = (f32[64,64]{1,0:T(8,128)S(1)}, f32[64,64]{1,0:T(8,128)}, u32[]{:S(2)}) copy-start(f32[64,64]{1,0:T(8,128)} %param.23) | copy-start | bytes 49156
  68.0 230.1 %copy-start.5 = (bf16[64,512]{1,0:T(8,128)(2,1)S(1)}, bf16[64,512]{1,0:T(8,128)(2,1)}, u32[]{:S(2)}) copy-start(bf16[64,512]{1,0:T(8,128)(2,1)} %param.20) | copy-start | bytes 196612
  70.8 65.6 %all-to-all-start = ((s32[64,1,2]{2,1,0:T(1,128)}), s32[64,1,2]{2,1,0:T(1,128)S(1)}, u32[]{:S(2)}, u32[]{:S(2)}) async-start(s32[64,1,2]{2,1,0:T(1,128)} %bitcast.2), calls=%async_computation | async-start | bytes 65536 | tf_op jit(solution)/shard_map/all_to_all | solution.py:105
  136.4 28.6 %all-to-all-start.1 = ((f32[64,1,128]{2,1,0:T(1,128)}), f32[64,1,128]{2,1,0:T(1,128)S(1)}, u32[]{:S(2)}, u32[]{:S(2)}) async-start(f32[64,1,128]{2,1,0:T(1,128)} %reshape.85), calls=%async_computation.1 | async-start | bytes 65536 | tf_op jit(solution)/shard_map/all_to_all | solution.py:104
  152.5 143.4 %all-gather.2.cloned.1.call-start = ((), (), s32[]{:S(2)}) async-start(), calls=%async_computation.3 | async-start | bytes 2129920 | tf_op jit(solution)/shard_map/all_gather | solution.py:114
  298.7 8.5 %collective-permute-start.9 = (f32[1,8,64]{2,1,0:T(8,128)S(1)}, f32[1,8,64]{2,1,0:T(8,128)S(1)}, u32[]{:S(2)}, u32[]{:S(2)}) collective-permute-start(f32[1,8,64]{2,1,0:T(8,128)S(1)} %slice.187), channel_id=1, source_target_pairs={{8,0},{16,8},{24,16},{32,24},{40,32},{48,40},{56,48},{64,56},{72,6... | collective-permute-start | bytes 6152 | tf_op jit(solution)/shard_map/ppermute | solution.py:21
  305.2 7.6 %collective-permute-start.8 = (f32[1,8,64]{2,1,0:T(8,128)S(1)}, f32[1,8,64]{2,1,0:T(8,128)S(1)}, u32[]{:S(2)}, u32[]{:S(2)}) collective-permute-start(f32[1,8,64]{2,1,0:T(8,128)S(1)} %slice.183), channel_id=1, source_target_pairs={{0,8},{8,16},{16,24},{24,32},{32,40},{40,48},{48,56},{56,64},{64,7... | collective-permute-start | bytes 6152 | tf_op jit(solution)/shard_map/ppermute | solution.py:18
  (2 other events, 6.3 us)
Sparse Core Ops, SparseCore 0:
  70.2 64.0 all-reduce.1
  167.3 128.5 all-gather.1
where the time goes:
time: 321 us
  waiting for transfers between devices  213 us (66%)
  starting transfers between devices  59.6 us (19%)
  matrix products  20.7 us (6%)
  between operations  14.7 us (5%)
  local copies, waits for them, and re-layouts  7.21 us (2%)
  other arithmetic  5.72 us (2%)
    all_gather x1, waiting for transfers between devices, local(): every_pot = lax.all_gather(updated, 'dom', axis=0, tiled=True)  129 us
    psum x1, waiting for transfers between devices, local(): density_term = lax.psum(partial_density, 'orb')  57.9 us
    ppermute x5, starting transfers between devices, padded_2(): lax.ppermute(lax.slice_in_dim(block, 0, width, axis=dim), axis, backward)  23 us
    all_to_all x1, starting transfers between devices, local(): lax.all_to_all(send_values, 'dom', split_axis=0, concat_axis=0, tiled=True)  16.1 us
    ppermute x5, waiting for transfers between devices, padded_2(): lax.ppermute(lax.slice_in_dim(block, block.shape[dim] - width, None, axis...  15 us
    ppermute x5, starting transfers between devices, padded_2(): lax.ppermute(lax.slice_in_dim(block, block.shape[dim] - width, None, axis...  15 us
    all_to_all x1, waiting for transfers between devices, local(): lax.all_to_all(send_values, 'dom', split_axis=0, concat_axis=0, tiled=True)  11 us
    dot_general x5, matrix products, assemble_local(): jnp.einsum('ckj,coj->cok', onehot, left_next, precision=lax.Precision.HIG...  7.2 us
  transfers between devices with their start and end apart: 14, of which 8 were waited for; matrix products, arithmetic and copies ran while one was open for 6% of the time, Pallas kernels for 0%

commit v1 on v0

v1 whole, which is shorter than its diff:
```python
import jax
import jax.numpy as jnp
import numpy as np
from jax import lax
from jax.experimental import pallas as pl
from jax.experimental.pallas import tpu as pltpu
from jax.sharding import PartitionSpec as P

ITERS = 4
relax = 0.25
step_rate = 0.1

LANES = 128
HALF = 64
NODES = 512
WIDTH = 8
CELLS = 48
HALO = 4
EXT = CELLS + 2 * HALO
F32, BF16 = jnp.float32, jnp.bfloat16


def dot(a, b, contract=((1,), (0,))):
    return lax.dot_general(a, b, (contract, ((), ())), preferred_element_type=F32)


def split(a):
    high = a.astype(BF16)
    return high, (a - high.astype(F32)).astype(BF16)


def lane_below(bound):
    return lax.broadcasted_iota(jnp.int32, (WIDTH, LANES), 1) < bound


SRC_ROWS, ORB_AT, BASE_AT, META_AT, HALO_ROWS = 32, 32, 40, 44, 48
IDX, SCALE, TARGET = slice(0, 128), slice(128, 256), slice(256, 384)


def solve_kernel(edge, src, orb, base, meta, left, right, eig, stiff, restrict_t, group,
                 adjoint_out, projected_out, x, quarter, xb, kin, shifted, factor, index):
    own = slice(HALO * WIDTH, (HALO + CELLS) * WIDTH)
    first, last = slice(0, HALO * WIDTH), slice((HALO + CELLS) * WIDTH, EXT * WIDTH)
    quarter[own] = relax * src[...].astype(F32)
    quarter[first] = relax * left[0:SRC_ROWS]
    quarter[last] = relax * right[0:SRC_ROWS]
    x[...] = quarter[...]
    eig_column = eig[...]
    for e in range(EXT):
        if e < HALO:
            base_row, meta_row = left[BASE_AT + e : BASE_AT + e + 1], left[META_AT + e : META_AT + e + 1]
        elif e < HALO + CELLS:
            base_row, meta_row = base[e - HALO : e - HALO + 1], meta[e - HALO : e - HALO + 1]
        else:
            at = e - HALO - CELLS
            base_row, meta_row = right[BASE_AT + at : BASE_AT + at + 1], right[META_AT + at : META_AT + at + 1]
        rows = slice(e * WIDTH, (e + 1) * WIDTH)
        shifted[rows] = base_row - eig_column
        factor[rows] = jnp.broadcast_to(meta_row[:, SCALE], (WIDTH, LANES))
        index[rows] = jnp.broadcast_to(meta_row[:, IDX].astype(jnp.int32), (WIDTH, LANES))
    low = lane_below(HALF)
    open_left, open_right = edge[0].astype(F32), edge[1].astype(F32)

    def step(_, carry):
        xb[...] = x[...].astype(BF16)
        kin[...] = dot(xb[...], stiff[...])
        part_before = new_before = None
        for e in range(EXT):
            rows = slice(e * WIDTH, (e + 1) * WIDTH)
            scale = factor[rows]
            parts, news = [], []
            for t in range(4):
                cols = slice(t * LANES, (t + 1) * LANES)
                here = x[rows, cols]
                part = scale * kin[rows, cols] + shifted[rows, cols] * here
                parts.append(part)
                news.append(here + quarter[rows, cols] - relax * part)
            if e > 0:
                crossing = jnp.where(low, parts[0], part_before)
                moved = relax * jnp.take_along_axis(
                    crossing, index[(e - 1) * WIDTH : e * WIDTH], axis=1, mode="promise_in_bounds"
                )
                if e == HALO:
                    moved = moved * open_left
                if e == HALO + CELLS:
                    moved = moved * open_right
                news[0] = jnp.where(low, news[0] - moved, news[0])
                x[(e - 1) * WIDTH : e * WIDTH, 3 * LANES :] = jnp.where(low, new_before, new_before - moved)
            for t in range(3):
                x[rows, t * LANES : (t + 1) * LANES] = news[t]
            part_before, new_before = parts[3], news[3]
        x[(EXT - 1) * WIDTH :, 3 * LANES :] = new_before
        return carry

    lax.fori_loop(0, ITERS, step, 0)
    mine = x[own]
    adjoint_out[...] = mine.astype(BF16)
    high, rest = split(orb[...].astype(F32) * mine)
    density = dot(group[...], high) + dot(group[...], rest)
    high, rest = split(density)
    nt = ((1,), (1,))
    projected_out[...] = dot(restrict_t[...], high, nt) + dot(restrict_t[...], rest, nt)


def sum_kernel(gathered, wanted, unpack, out):
    sources = gathered.shape[0] // WIDTH
    values = gathered[...]
    high, rest = split(values)
    ids = dot(high, unpack[...])
    row = lax.broadcasted_iota(jnp.int32, ids.shape, 0) % WIDTH
    lane = lax.broadcasted_iota(jnp.int32, ids.shape, 1)
    ids = jnp.where(lane // 6 == row, ids, 0.0)
    ids = jnp.sum(ids.reshape(sources, WIDTH, LANES), axis=1)
    lane = lax.broadcasted_iota(jnp.int32, ids.shape, 1)
    source = lax.broadcasted_iota(jnp.int32, ids.shape, 0)
    known = (source * HALF + lane - CELLS).astype(F32)
    ids = jnp.where(lane < CELLS, ids, jnp.where(lane < CELLS + HALF, known, -1.0))
    asked = jnp.broadcast_to(wanted[...], (LANES, LANES))
    total = jnp.zeros((2 * WIDTH, LANES), F32)
    for s in range(0, sources, 2):
        hot = [jnp.where(asked == ids[i : i + 1], 1.0, 0.0).astype(BF16) for i in (s, s + 1)]
        both = [
            jnp.concatenate([high[i * WIDTH : (i + 1) * WIDTH], rest[i * WIDTH : (i + 1) * WIDTH]], 0)
            for i in (s, s + 1)
        ]
        total = total + dot(jnp.concatenate(both, 1), jnp.concatenate(hot, 1), ((1,), (1,)))
    result = total[:WIDTH] + total[WIDTH:]
    for r in range(out.shape[0] // WIDTH):
        out[r * WIDTH : (r + 1) * WIDTH] = result


def apply_kernel(edge, columns, orb, base, meta, left, right, stiff, prolong, updated_out, applied_out, ob, kin):
    table = jnp.transpose(columns[...])
    updated_out[...] = table[0:HALF]
    high, rest = split(table[HALF:])
    node = dot(high, prolong[...]) + dot(rest, prolong[...])
    ob[0:16] = jnp.concatenate([left[ORB_AT : ORB_AT + WIDTH], right[ORB_AT : ORB_AT + WIDTH]], 0).astype(BF16)
    ob[16:] = orb[...]
    kin[...] = dot(ob[...], stiff[...])
    low = lane_below(HALF)
    open_left, open_right = edge[0].astype(F32), edge[1].astype(F32)
    part_before = new_before = index_before = None
    finished = []
    for e in range(CELLS + 2):
        if e == 0:
            values, base_row = left[ORB_AT : ORB_AT + WIDTH], left[BASE_AT + HALO - 1 : BASE_AT + HALO]
            meta_row = left[META_AT + HALO - 1 : META_AT + HALO]
            node_row, kin_rows = node[CELLS : CELLS + 1], slice(0, WIDTH)
        elif e <= CELLS:
            c = e - 1
            values = orb[c // 2 * 16 : c // 2 * 16 + 16].astype(F32)[c % 2 * WIDTH : (c % 2 + 1) * WIDTH]
            base_row, meta_row, node_row = base[c : c + 1], meta[c : c + 1], node[c : c + 1]
            kin_rows = slice(16 + c * WIDTH, 16 + (c + 1) * WIDTH)
        else:
            values, base_row = right[ORB_AT : ORB_AT + WIDTH], right[BASE_AT : BASE_AT + 1]
            meta_row = right[META_AT : META_AT + 1]
            node_row, kin_rows = node[CELLS + 1 : CELLS + 2], slice(WIDTH, 2 * WIDTH)
        shift = base_row + node_row
        scale = jnp.broadcast_to(meta_row[:, SCALE], (WIDTH, LANES))
        parts = [
            scale * kin[kin_rows, t * LANES : (t + 1) * LANES]
            + shift[:, t * LANES : (t + 1) * LANES] * values[:, t * LANES : (t + 1) * LANES]
            for t in range(4)
        ]
        if e > 0:
            crossing = jnp.where(low, parts[0], part_before)
            moved = jnp.take_along_axis(crossing, index_before, axis=1, mode="promise_in_bounds")
            if e == 1:
                moved = moved * open_left
            if e == CELLS + 1:
                moved = moved * open_right
            done = jnp.where(low, new_before[3], new_before[3] + moved)
            if e > 1:
                finished.append(jnp.concatenate([*new_before[:3], done], 1))
            news = [jnp.where(low, parts[0] + moved, parts[0]), *parts[1:]]
        else:
            news = parts
        part_before, new_before = parts[3], news
        index_before = jnp.broadcast_to(meta_row[:, IDX].astype(jnp.int32), (WIDTH, LANES))
        if len(finished) == 2:
            c = e - 3
            applied_out[c * WIDTH : (c + 2) * WIDTH] = jnp.concatenate(finished, 0).astype(BF16)
            finished = []


def unpack_table():
    table = np.zeros((LANES, LANES), np.float32)
    for k in range(CELLS):
        table[112 + k % 6, k] = 64.0
        table[118 + k % 6, k] = 1.0
    return table


def group_table():
    table = np.zeros((LANES, CELLS * WIDTH), np.float32)
    for row in range(CELLS * WIDTH):
        table[row // WIDTH, row] = 1.0
    return table


def local(orbitals, adjoint_source, eigenvalues, cell_scale, base_potential, stiffness, face_perm, restrict,
          prolong, owner, pot_slot, potential):
    n_dom, n_orb = lax.axis_size("dom"), lax.axis_size("orb")
    dom, orb_at = lax.axis_index("dom"), lax.axis_index("orb")
    vmem = pl.BlockSpec(memory_space=pltpu.VMEM)
    smem = pl.BlockSpec(memory_space=pltpu.SMEM)

    orb2 = orbitals.reshape(CELLS * WIDTH, NODES)
    src2 = adjoint_source.reshape(CELLS * WIDTH, NODES)
    target = owner[:, 0] * HALF + pot_slot
    faces = jnp.arange(HALF, dtype=jnp.int32)
    inverse = jnp.sum(jnp.where(face_perm[:, :, None] == faces[None, None, :], faces[None, :, None], 0), axis=1)
    meta = jnp.concatenate(
        [
            (HALF + inverse).astype(F32),
            face_perm.astype(F32),
            jnp.broadcast_to(cell_scale[:, None], (CELLS, LANES)),
            jnp.broadcast_to(target.astype(F32)[:, None], (CELLS, 2 * LANES)),
        ],
        1,
    )

    def packed(cells, orb_cell):
        rows = slice(cells.start * WIDTH, cells.stop * WIDTH)
        return jnp.concatenate(
            [
                src2[rows].astype(F32),
                orb2[orb_cell * WIDTH : (orb_cell + 1) * WIDTH].astype(F32),
                base_potential[cells],
                meta[cells],
            ],
            0,
        )

    ahead = [(i, i + 1) for i in range(n_dom - 1)]
    left = lax.ppermute(packed(slice(CELLS - HALO, CELLS), CELLS - 1), "dom", ahead)
    right = lax.ppermute(packed(slice(0, HALO), 0), "dom", [(b, a) for a, b in ahead])

    edge = jnp.stack([dom > 0, dom < n_dom - 1]).astype(jnp.int32)
    pot_columns = lax.dynamic_slice_in_dim(potential, orb_at * WIDTH, WIDTH, 1).T
    static = jnp.concatenate(
        [
            jnp.zeros((WIDTH, CELLS), F32),
            pot_columns,
            owner.reshape(WIDTH, 6).astype(F32),
            pot_slot.reshape(WIDTH, 6).astype(F32),
            jnp.zeros((WIDTH, 4), F32),
        ],
        1,
    )
    group = jnp.asarray(group_table(), BF16)
    unpack = jnp.asarray(unpack_table(), BF16)
    rows = EXT * WIDTH
    adjoint2, projected = pl.pallas_call(
        solve_kernel,
        out_shape=(
            jax.ShapeDtypeStruct((CELLS * WIDTH, NODES), BF16),
            jax.ShapeDtypeStruct((HALF, LANES), F32),
        ),
        in_specs=[smem] + [vmem] * 10,
        out_specs=(vmem, vmem),
        scratch_shapes=[
            pltpu.VMEM((rows, NODES), F32),
            pltpu.VMEM((rows, NODES), F32),
            pltpu.VMEM((rows, NODES), BF16),
            pltpu.VMEM((rows, NODES), F32),
            pltpu.VMEM((rows, NODES), F32),
            pltpu.VMEM((rows, LANES), F32),
            pltpu.VMEM((rows, LANES), jnp.int32),
        ],
        compiler_params=pltpu.CompilerParams(vmem_limit_bytes=32 * 2**20),
    )(edge, src2, orb2, base_potential, meta, left, right, eigenvalues[:, None], stiffness, restrict.T, group)

    mine = lax.all_to_all(projected.reshape(n_orb, WIDTH, LANES), "orb", split_axis=0, concat_axis=0, tiled=True)
    payload = static - step_rate * jnp.sum(mine, axis=0)
    gathered = lax.all_to_all(
        jnp.broadcast_to(payload[None], (n_dom, WIDTH, LANES)), "dom", split_axis=0, concat_axis=0, tiled=True
    )
    halo_ids = jnp.stack([left[META_AT + HALO - 1, 256], right[META_AT, 256]])
    wanted = jnp.concatenate(
        [
            (dom * HALF + faces).astype(F32),
            target.astype(F32),
            halo_ids,
            jnp.full((LANES - HALF - CELLS - 2,), -2.0, F32),
        ]
    )[:, None]
    columns = pl.pallas_call(
        sum_kernel,
        out_shape=jax.ShapeDtypeStruct((n_orb * WIDTH, LANES), F32),
        in_specs=[vmem] * 3,
        out_specs=vmem,
        compiler_params=pltpu.CompilerParams(vmem_limit_bytes=32 * 2**20),
    )(gathered.reshape(n_dom * WIDTH, LANES), wanted, unpack)
    columns = lax.all_to_all(columns.reshape(n_orb, WIDTH, LANES), "orb", split_axis=0, concat_axis=0, tiled=True)
    updated, applied2 = pl.pallas_call(
        apply_kernel,
        out_shape=(
            jax.ShapeDtypeStruct((HALF, HALF), F32),
            jax.ShapeDtypeStruct((CELLS * WIDTH, NODES), BF16),
        ),
        in_specs=[smem] + [vmem] * 8,
        out_specs=(vmem, vmem),
        scratch_shapes=[
            pltpu.VMEM(((CELLS + 2) * WIDTH, NODES), BF16),
            pltpu.VMEM(((CELLS + 2) * WIDTH, NODES), F32),
        ],
        compiler_params=pltpu.CompilerParams(vmem_limit_bytes=32 * 2**20),
    )(edge, columns.reshape(n_orb * WIDTH, LANES), orb2, base_potential, meta, left, right, stiffness, prolong)
    return adjoint2.reshape(orbitals.shape), updated, applied2.reshape(orbitals.shape)


def solution(mesh):
    in_specs = (
        P("dom", "orb", None),
        P("dom", "orb", None),
        P("orb"),
        P("dom"),
        P("dom", None),
        P(),
        P("dom", None),
        P(),
        P(),
        P("dom", None),
        P("dom"),
        P("dom", None),
    )
    out_specs = (P("dom", "orb", None), P("dom", None), P("dom", "orb", None))
    return jax.shard_map(local, mesh=mesh, in_specs=in_specs, out_specs=out_specs, check_vma=False)
```

time: 321 us -> 84.1 us (0.26)
  the two profiles are of different devices: /device:TPU:6 before, /device:TPU:1 now
where the time goes in v1:
time: 84.1 us; the launch traced here: 83.5 us
  starting transfers between devices  30.4 us (36%)
  waiting for transfers between devices  24.8 us (29%)
  blocking collectives  10.1 us (12%)
  Pallas kernels  7.12 us (8%)
  local copies, waits for them, and re-layouts  5.57 us (7%)
  other arithmetic  4.64 us (6%)
    all_to_all x1, starting transfers between devices, local(): lax.all_to_all(jnp.broadcast_to(payload[None], (n_dom, WIDTH, LANES)), 'd...  16.6 us
    all_to_all x1, waiting for transfers between devices, local(): lax.all_to_all(jnp.broadcast_to(payload[None], (n_dom, WIDTH, LANES)), 'd...  16.4 us
    all_to_all x1, blocking collectives, local(): lax.all_to_all(columns.reshape(n_orb, WIDTH, LANES), 'orb', split_axis=0,...  10.1 us
    all_to_all x1, starting transfers between devices, local(): lax.all_to_all(projected.reshape(n_orb, WIDTH, LANES), 'orb', split_axis=...  8.14 us
    all_to_all x1, waiting for transfers between devices, local(): lax.all_to_all(projected.reshape(n_orb, WIDTH, LANES), 'orb', split_axis=...  4.4 us
    ppermute x1, starting transfers between devices, local(): lax.ppermute(packed(slice(CELLS - HALO, CELLS), CELLS - 1), 'dom', ahead)  4.38 us
    pallas_call x1, Pallas kernels, local(): pl.pallas_call(solve_kernel, out_shape=(jax.ShapeDtypeStruct((CELLS * WID...  4.32 us
    ppermute x1, waiting for transfers between devices, local(): lax.ppermute(packed(slice(0, HALO), 0), 'dom', [(b, a) for a, b in ahead])  3.95 us
  transfers between devices with their start and end apart: 4, of which 3 were waited for; matrix products, arithmetic and copies ran while one was open for 4% of the time, Pallas kernels for 0%

profile of v1, /device:TPU:1, one launch (start us, length us, event | category | flops | bytes accessed | tf_op | source)
XLA Modules:
  0.0 83.5 jit_solution(16210125545202034678)
XLA Ops:
  0.7 0.8 convert_element_type.58
  1.4 1.3 %select_reduce_fusion = s32[48,64]{1,0:T(8,128)S(1)} fusion(s32[48,64]{1,0:T(8,128)} %param.20), kind=kLoop, calls=%fused_computation | loop fusion | flops 586752 | bytes 24576 | tf_op jit(solution)/shard_map/reduce_sum | solution.py:212
  2.8 0.8 bitcast_convert_fusion.2
  3.5 0.9 %bitcast_convert_fusion = (f32[32,512]{1,0:T(8,128)S(1)}, f32[32,512]{1,0:T(8,128)S(1)}) fusion(bf16[48,8,512]{2,1,0:T(8,128)(2,1)} %param.15), kind=kLoop, calls=%fused_computation.5 | loop fusion | flops 32768 | bytes 196608 | tf_op jit(solution)/shard_map/convert_element_type | solution.py:227
  4.4 0.7 fusion.3
  5.2 0.7 broadcast_in_dim.47
  6.1 4.4 %collective-permute-start = (f32[48,512]{1,0:T(8,128)S(1)}, f32[48,512]{1,0:T(8,128)S(1)}, u32[]{:S(2)}, u32[]{:S(2)}) collective-permute-start(f32[48,512]{1,0:T(8,128)S(1)} %pad_maximum_fusion.1), channel_id=1, source_target_pairs={{0,8},{8,16},{16,24},{24,32},{32,40},{40,48},{48,56},{56,64},{64,7... | collective-permute-start | bytes 294920 | tf_op jit(solution)/shard_map/ppermute | solution.py:236
  10.5 1.3 %collective-permute-start.1 = (f32[48,512]{1,0:T(8,128)S(1)}, f32[48,512]{1,0:T(8,128)S(1)}, u32[]{:S(2)}, u32[]{:S(2)}) collective-permute-start(f32[48,512]{1,0:T(8,128)S(1)} %pad_maximum_fusion.2), channel_id=1, source_target_pairs={{8,0},{16,8},{24,16},{32,24},{40,32},{48,40},{56,48},{64,56},{72,6... | collective-permute-start | bytes 294920 | tf_op jit(solution)/shard_map/ppermute | solution.py:237
  12.1 3.9 %collective-permute-done.1.right = f32[48,512]{1,0:T(8,128)S(1)} collective-permute-done((f32[48,512]{1,0:T(8,128)S(1)}, f32[48,512]{1,0:T(8,128)S(1)}, u32[]{:S(2)}, u32[]{:S(2)}) %collective-permute-start.1) | collective-permute-done | bytes 98336 | tf_op jit(solution)/shard_map/ppermute | solution.py:237
  16.0 1.0 %copy-done.3 = bf16[48,8,512]{2,1,0:T(8,128)(2,1)S(1)} copy-done((bf16[48,8,512]{2,1,0:T(8,128)(2,1)S(1)}, bf16[48,8,512]{2,1,0:T(8,128)(2,1)}, u32[]{:S(2)}) %copy-start.3) | copy-done | bytes 393240
  17.0 4.3 %shard_map.157 = (bf16[384,512]{1,0:T(8,128)(2,1)}, f32[64,128]{1,0:T(8,128)}) custom-call(s32[2]{0:T(128)S(1)} %add_convert_fusion.1.edge, bf16[384,512]{1,0:T(8,128)(2,1)S(1)} %bitcast.35, bf16[384,512]{1,0:T(8,128)(2,1)S(1)} %bitcast.32, f32[48,512]{1,0:T(8,128)S(1)} %copy-done.4, f32[48,512]{1,0:T(8,128)S(1)} %pad_maximum_fusion.meta, ...), custom_call_target="tpu_custom_call" | custom-call | tf_op jit(solution)/shard_map/pallas_call | solution.py:254
  21.4 8.1 %all-to-all-start = ((f32[8,8,128]{2,1,0:T(8,128)}), f32[8,8,128]{2,1,0:T(8,128)S(1)}, u32[]{:S(2)}, u32[]{:S(2)}) async-start(f32[8,8,128]{2,1,0:T(8,128)} %bitcast.13), calls=%async_computation | async-start | bytes 65536 | tf_op jit(solution)/shard_map/all_to_all | solution.py:274
  29.7 0.1 concatenate.22
  29.8 4.4 %all-to-all-done = f32[8,8,128]{2,1,0:T(8,128)S(1)} async-done(((f32[8,8,128]{2,1,0:T(8,128)}), f32[8,8,128]{2,1,0:T(8,128)S(1)}, u32[]{:S(2)}, u32[]{:S(2)}) %all-to-all-start) | async-done | bytes 32800 | tf_op jit(solution)/shard_map/all_to_all | solution.py:274
  34.3 0.7 broadcast_in_dim.52
  35.0 16.6 %all-to-all-start.1 = ((f32[64,8,128]{2,1,0:T(8,128)}), f32[64,8,128]{2,1,0:T(8,128)S(1)}, u32[]{:S(2)}, u32[]{:S(2)}) async-start(f32[64,8,128]{2,1,0:T(8,128)} %broadcast_in_dim.52), calls=%async_computation.1 | async-start | bytes 524288 | tf_op jit(solution)/shard_map/all_to_all | solution.py:276
  51.6 0.5 slice.46
  52.1 0.5 slice.47
  52.7 1.4 %concatenate.23 = f32[128]{0:T(128)S(1)} concatenate(f32[64]{0:T(128)S(1)} %add_convert_fusion.2, f32[48]{0:T(128)S(1)} %get-tuple-element.20, f32[1]{0:T(128)} %bitcast.15, f32[1]{0:T(128)} %bitcast.16, f32[14]{0:T(128)S(1)} %broadcast.20), dimensions={0} | concatenate | bytes 1024 | tf_op jit(solution)/shard_map/concatenate | solution.py:280
  54.0 0.1 copy.27.wanted
  54.2 16.4 %all-to-all-done.1 = f32[64,8,128]{2,1,0:T(8,128)S(1)} async-done(((f32[64,8,128]{2,1,0:T(8,128)}), f32[64,8,128]{2,1,0:T(8,128)S(1)}, u32[]{:S(2)}, u32[]{:S(2)}) %all-to-all-start.1) | async-done | bytes 262176 | tf_op jit(solution)/shard_map/all_to_all | solution.py:276
  70.6 0.9 %shard_map.158 = f32[64,128]{1,0:T(8,128)S(1)} custom-call(f32[512,128]{1,0:T(8,128)S(1)} %bitcast.34, f32[128,1]{1,0:T(8,128)S(1)} %copy.27.wanted, bf16[128,128]{1,0:T(8,128)(2,1)S(1)} %copy-done.8), custom_call_target="tpu_custom_call" | custom-call | tf_op jit(solution)/shard_map/pallas_call | solution.py:288
  71.4 10.1 %all_to_all.15 = f32[8,8,128]{2,1,0:T(8,128)S(1)} all-to-all(f32[8,8,128]{2,1,0:T(8,128)S(1)} %bitcast.37), channel_id=1, replica_groups=mesh['dom'=64,'orb'=8] {'orb'}, dimensions={0} | all-to-all | bytes 65536 | tf_op jit(solution)/shard_map/all_to_all | solution.py:295
  81.6 1.9 %shard_map.159 = (f32[64,64]{1,0:T(8,128)}, bf16[384,512]{1,0:T(8,128)(2,1)}) custom-call(s32[2]{0:T(128)S(1)} %add_convert_fusion.1.edge, f32[64,128]{1,0:T(8,128)S(1)} %bitcast.36, bf16[384,512]{1,0:T(8,128)(2,1)S(1)} %bitcast.33, f32[48,512]{1,0:T(8,128)S(1)} %copy-done.4, f32[48,512]{1,0:T(8,128)S(1)} %pad_maximum_fusion.meta, ...), custom_call_target="tpu_custom_call" | custom-call | tf_op jit(solution)/shard_map/pallas_call | solution.py:296
  (41 shorter events, 0.8 us)
Async XLA Ops:
  0.6 11.2 %copy-start = (f32[64,64]{1,0:T(8,128)S(1)}, f32[64,64]{1,0:T(8,128)}, u32[]{:S(2)}) copy-start(f32[64,64]{1,0:T(8,128)} %param.25) | copy-start | bytes 49156
  0.6 5.4 %copy-start.4 = (f32[48,512]{1,0:T(8,128)S(1)}, f32[48,512]{1,0:T(8,128)}, u32[]{:S(2)}) copy-start(f32[48,512]{1,0:T(8,128)} %base.3) | copy-start | bytes 294916
  2.7 9.1 %copy-start.9 = (f32[8]{0:T(128)S(1)}, f32[8]{0:T(128)}, u32[]{:S(2)}) copy-start(f32[8]{0:T(128)} %param.16) | copy-start | bytes 100
  2.7 13.3 %copy-start.6 = (bf16[512,64]{0,1:T(8,128)(2,1)S(1)}, bf16[512,64]{0,1:T(8,128)(2,1)}, u32[]{:S(2)}) copy-start(bf16[512,64]{0,1:T(8,128)(2,1)} %param.21) | copy-start | bytes 196612
  3.5 12.5 %copy-start.1 = (bf16[512,512]{1,0:T(8,128)(2,1)S(1)}, bf16[512,512]{1,0:T(8,128)(2,1)}, u32[]{:S(2)}) copy-start(bf16[512,512]{1,0:T(8,128)(2,1)} %stiff.3) | copy-start | bytes 1572868
  3.5 12.5 %copy-start.2 = (bf16[48,8,512]{2,1,0:T(8,128)(2,1)S(1)}, bf16[48,8,512]{2,1,0:T(8,128)(2,1)}, u32[]{:S(2)}) copy-start(bf16[48,8,512]{2,1,0:T(8,128)(2,1)} %param.14) | copy-start | bytes 1179652
  3.5 12.5 %copy-start.5 = (bf16[128,384]{1,0:T(8,128)(2,1)S(1)}, bf16[128,384]{1,0:T(8,128)(2,1)}, u32[]{:S(2)}) copy-start(bf16[128,384]{1,0:T(8,128)(2,1)} %constant.11.clone.group) | copy-start | bytes 294916
  6.1 6.0 %collective-permute-start = (f32[48,512]{1,0:T(8,128)S(1)}, f32[48,512]{1,0:T(8,128)S(1)}, u32[]{:S(2)}, u32[]{:S(2)}) collective-permute-start(f32[48,512]{1,0:T(8,128)S(1)} %pad_maximum_fusion.1), channel_id=1, source_target_pairs={{0,8},{8,16},{16,24},{24,32},{32,40},{40,48},{48,56},{56,64},{64,7... | collective-permute-start | bytes 294920 | tf_op jit(solution)/shard_map/ppermute | solution.py:236
  10.5 5.5 %collective-permute-start.1 = (f32[48,512]{1,0:T(8,128)S(1)}, f32[48,512]{1,0:T(8,128)S(1)}, u32[]{:S(2)}, u32[]{:S(2)}) collective-permute-start(f32[48,512]{1,0:T(8,128)S(1)} %pad_maximum_fusion.2), channel_id=1, source_target_pairs={{8,0},{16,8},{24,16},{32,24},{40,32},{48,40},{56,48},{64,56},{72,6... | collective-permute-start | bytes 294920 | tf_op jit(solution)/shard_map/ppermute | solution.py:237
  16.0 1.0 %copy-start.3 = (bf16[48,8,512]{2,1,0:T(8,128)(2,1)S(1)}, bf16[48,8,512]{2,1,0:T(8,128)(2,1)}, u32[]{:S(2)}) copy-start(bf16[48,8,512]{2,1,0:T(8,128)(2,1)} %param.15) | copy-start | bytes 1179652
  17.0 12.5 %copy-start.10 = (s32[48,1]{0,1:T(1,128)S(1)}, s32[48,1]{0,1:T(1,128)}, u32[]{:S(2)}) copy-start(s32[48,1]{0,1:T(1,128)} %param.23) | copy-start | bytes 580
  21.4 49.2 %copy-start.8 = (bf16[128,128]{1,0:T(8,128)(2,1)S(1)}, bf16[128,128]{1,0:T(8,128)(2,1)}, u32[]{:S(2)}) copy-start(bf16[128,128]{1,0:T(8,128)(2,1)} %constant.32.clone.unpack) | copy-start | bytes 98308
  21.4 12.9 %all-to-all-start = ((f32[8,8,128]{2,1,0:T(8,128)}), f32[8,8,128]{2,1,0:T(8,128)S(1)}, u32[]{:S(2)}, u32[]{:S(2)}) async-start(f32[8,8,128]{2,1,0:T(8,128)} %bitcast.13), calls=%async_computation | async-start | bytes 65536 | tf_op jit(solution)/shard_map/all_to_all | solution.py:274
  35.0 46.6 %copy-start.7 = (bf16[64,512]{1,0:T(8,128)(2,1)S(1)}, bf16[64,512]{1,0:T(8,128)(2,1)}, u32[]{:S(2)}) copy-start(bf16[64,512]{1,0:T(8,128)(2,1)} %prolong.1) | copy-start | bytes 196612
  35.0 35.6 %all-to-all-start.1 = ((f32[64,8,128]{2,1,0:T(8,128)}), f32[64,8,128]{2,1,0:T(8,128)S(1)}, u32[]{:S(2)}, u32[]{:S(2)}) async-start(f32[64,8,128]{2,1,0:T(8,128)} %broadcast_in_dim.52), calls=%async_computation.1 | async-start | bytes 524288 | tf_op jit(solution)/shard_map/all_to_all | solution.py:276

commit v2 on v1

v2 whole, which is shorter than its diff:
```python
import jax
import jax.numpy as jnp
import numpy as np
from jax import lax
from jax.experimental import pallas as pl
from jax.experimental.pallas import tpu as pltpu
from jax.sharding import PartitionSpec as P

ITERS = 4
relax = 0.25
step_rate = 0.1

LANES = 128
HALF = 64
NODES = 512
WIDTH = 8
CELLS = 48
HALO = 4
EXT = CELLS + 2 * HALO
F32, BF16 = jnp.float32, jnp.bfloat16


def dot(a, b, contract=((1,), (0,))):
    return lax.dot_general(a, b, (contract, ((), ())), preferred_element_type=F32)


def split(a):
    high = a.astype(BF16)
    return high, (a - high.astype(F32)).astype(BF16)


def lane_below(bound):
    return lax.broadcasted_iota(jnp.int32, (WIDTH, LANES), 1) < bound


SRC_ROWS, ORB_AT, BASE_AT, META_AT, HALO_ROWS = 32, 32, 40, 44, 48
IDX, SCALE, TARGET = slice(0, 128), slice(128, 256), slice(256, 512)
STRIP = 3 * HALO
NT = ((1,), (1,))


def tile(e):
    return slice(e * WIDTH, (e + 1) * WIDTH)


def cols(t):
    return slice(t * LANES, (t + 1) * LANES)


def face_rows(perm, wanted_cells):
    twice = jnp.concatenate([perm, perm], 1).astype(F32)
    columns = jnp.transpose(twice)[0:HALF]
    node = lax.broadcasted_iota(jnp.int32, (HALF, LANES), 0).astype(F32)
    lane = lax.broadcasted_iota(jnp.int32, (HALF, LANES), 1).astype(F32)
    low = lax.broadcasted_iota(jnp.int32, (1, LANES), 1) < HALF
    rows = []
    for c in wanted_cells:
        inverse = jnp.sum(jnp.where(columns[:, c : c + 1] == lane, node, 0.0), axis=0, keepdims=True)
        rows.append(jnp.where(low, inverse + HALF, twice[c : c + 1]))
    return rows


def pack_kernel(scale, owner, slot, src_low, src_high, orb_low, orb_high, base_low, base_high, perm_low, perm_high,
                to_left, to_right):
    def put(out, src, orb, base, perm, first, orb_at, edge_cell):
        inner = 0 if first == 0 else WIDTH - HALO
        out[0:SRC_ROWS] = src[...].astype(F32)
        out[ORB_AT : ORB_AT + WIDTH] = orb[...].astype(F32)[tile(orb_at)]
        out[BASE_AT : BASE_AT + HALO] = base[inner : inner + HALO]
        faces = face_rows(perm[...], range(inner, inner + HALO))
        target = (owner[edge_cell] * HALF + slot[edge_cell]).astype(F32)
        for i in range(HALO):
            at = slice(META_AT + i, META_AT + i + 1)
            out[at, IDX] = faces[i]
            out[at, SCALE] = jnp.full((1, LANES), scale[first + i], F32)
            out[at, TARGET] = jnp.full((1, 2 * LANES), target, F32)

    put(to_left, src_low, orb_low, base_low, perm_low, 0, 0, 0)
    put(to_right, src_high, orb_high, base_high, perm_high, CELLS - HALO, 1, CELLS - 1)


def relaxed(strips, x, quarter, shifted, xb, kin, stiff, factor, index, gates):
    low = lane_below(HALF)
    cells = strips[-1][-1] + 1

    def step(_, carry):
        xb[...] = x[...].astype(BF16)
        kin[...] = dot(xb[...], stiff[...])
        for strip in strips:
            part_before = new_before = None
            for e in strip:
                rows = tile(e)
                scale = factor(e)
                parts, news = [], []
                for t in range(4):
                    here = x[rows, cols(t)]
                    part = scale * kin[rows, cols(t)] + shifted[rows, cols(t)] * here
                    parts.append(part)
                    news.append(here + quarter[rows, cols(t)] - relax * part)
                if e > strip[0]:
                    crossing = jnp.where(low, parts[0], part_before)
                    moved = relax * jnp.take_along_axis(crossing, index[tile(e - 1)], axis=1, mode="promise_in_bounds")
                    if e in gates:
                        moved = moved * gates[e]
                    news[0] = jnp.where(low, news[0] - moved, news[0])
                    x[tile(e - 1), cols(3)] = jnp.where(low, new_before, new_before - moved)
                for t in range(3):
                    x[rows, cols(t)] = news[t]
                part_before, new_before = parts[3], news[3]
            x[tile(strip[-1]), cols(3)] = new_before
        return carry

    lax.fori_loop(0, ITERS, step, 0)


def projection(orb_values, x_values, group, restrict_t):
    high, rest = split(orb_values.astype(F32) * x_values)
    density = dot(group, high) + dot(group, rest)
    high, rest = split(density)
    return dot(restrict_t, high, NT) + dot(restrict_t, rest, NT)


def interior_kernel(place, scale, owner, slot, src, orb, base, perm, eig, stiff, restrict_t, group, potential,
                    adjoint_out, projected_out, linear_out, index_out, static_out,
                    x, quarter, xb, kin, shifted, turned):
    quarter[...] = relax * src[...].astype(F32)
    x[...] = quarter[...]
    eig_column = eig[...]
    faces = face_rows(perm[...], range(CELLS))
    for c in range(CELLS):
        shifted[tile(c)] = base[c : c + 1] - eig_column
        index_out[tile(c)] = jnp.broadcast_to(faces[c].astype(jnp.int32), (WIDTH, LANES))
    relaxed([range(CELLS)], x, quarter, shifted, xb, kin, stiff, lambda c: scale[c], index_out, {})
    inner = slice(HALO * WIDTH, (CELLS - HALO) * WIDTH)
    adjoint_out[...] = x[inner].astype(BF16)
    projected_out[...] = projection(orb[inner], x[inner], group[...], restrict_t[...])
    kin[...] = dot(orb[...], stiff[...])
    for pair in range(CELLS // 2):
        values = orb[pair * 16 : pair * 16 + 16].astype(F32)
        for c in (2 * pair, 2 * pair + 1):
            linear_out[tile(c)] = scale[c] * kin[tile(c)] + base[c : c + 1] * values[tile(c % 2)]
    turned[...] = jnp.transpose(potential[...])
    columns = turned[pl.ds(pl.multiple_of(place[1] * WIDTH, WIDTH), WIDTH)]
    row = lax.broadcasted_iota(jnp.int32, (WIDTH, LANES), 0)
    lane = lax.broadcasted_iota(jnp.int32, (WIDTH, LANES), 1)
    at = jnp.where(lane >= CELLS + HALF, row * 12 + lane - CELLS - HALF, -1)
    at = jnp.where(lane < CELLS + HALF + 12, at, -1)
    static = jnp.concatenate([jnp.zeros((WIDTH, CELLS), F32), columns, jnp.zeros((WIDTH, 16), F32)], 1)
    for c in range(CELLS):
        static = jnp.where(at == c // 6 * 12 + c % 6, owner[c].astype(F32), static)
        static = jnp.where(at == c // 6 * 12 + 6 + c % 6, slot[c].astype(F32), static)
    static_out[...] = static


def boundary_kernel(place, scale, src, orb, base, index_own, left, right, eig, stiff, restrict_t, group, adjoint_mid,
                    projected_mid, adjoint_out, projected_out, ghost_out,
                    x, quarter, xb, kin, shifted, factor, index, ob):
    near, edge = 2 * HALO * WIDTH, HALO * WIDTH
    last = CELLS * WIDTH
    quarter[0:edge] = relax * left[0:SRC_ROWS]
    quarter[edge : edge + near] = relax * src[0:near].astype(F32)
    quarter[edge + near : edge + 2 * near] = relax * src[last - near :].astype(F32)
    quarter[edge + 2 * near :] = relax * right[0:SRC_ROWS]
    x[...] = quarter[...]
    eig_column = eig[...]
    for e in range(2 * STRIP):
        ghost = left if e < HALO else right if e >= 2 * STRIP - HALO else None
        if ghost is None:
            c = e - HALO if e < STRIP else CELLS - 2 * HALO + e - STRIP
            base_row = base[c : c + 1]
            factor[tile(e)] = jnp.full((WIDTH, LANES), scale[c], F32)
            index[tile(e)] = index_own[tile(c)]
        else:
            i = e if e < HALO else e - 2 * STRIP + HALO
            base_row = ghost[BASE_AT + i : BASE_AT + i + 1]
            meta_row = ghost[META_AT + i : META_AT + i + 1]
            factor[tile(e)] = jnp.broadcast_to(meta_row[:, SCALE], (WIDTH, LANES))
            index[tile(e)] = jnp.broadcast_to(meta_row[:, IDX].astype(jnp.int32), (WIDTH, LANES))
        shifted[tile(e)] = base_row - eig_column
    gates = {
        HALO: jnp.where(place[0] > 0, 1.0, 0.0),
        2 * STRIP - HALO: jnp.where(place[0] < place[2] - 1, 1.0, 0.0),
    }
    relaxed([range(STRIP), range(STRIP, 2 * STRIP)], x, quarter, shifted, xb, kin, stiff,
            lambda e: factor[tile(e)], index, gates)
    low_cells, high_cells = x[edge : 2 * edge], x[4 * edge : 5 * edge]
    adjoint_out[0:edge] = low_cells.astype(BF16)
    adjoint_out[edge : last - edge] = adjoint_mid[...]
    adjoint_out[last - edge :] = high_cells.astype(BF16)
    own_orb = jnp.concatenate([orb[0:edge], orb[last - edge :]], 0)
    own_x = jnp.concatenate([low_cells, high_cells], 0)
    projected_out[...] = projected_mid[...] + projection(own_orb, own_x, group[...], restrict_t[...])
    ghosts = jnp.concatenate([left[ORB_AT : ORB_AT + WIDTH], right[ORB_AT : ORB_AT + WIDTH]], 0)
    ob[...] = ghosts.astype(BF16)
    ghost_kin = dot(ob[...], stiff[...])
    for i, e, base_row in (
        (0, HALO - 1, left[BASE_AT + HALO - 1 : BASE_AT + HALO]),
        (1, 2 * STRIP - HALO, right[BASE_AT : BASE_AT + 1]),
    ):
        for t in range(4):
            ghost_out[tile(i), cols(t)] = (
                factor[tile(e)] * ghost_kin[tile(i), cols(t)] + base_row[:, cols(t)] * ghosts[tile(i), cols(t)]
            )


def sum_kernel(place, owner, slot, gathered, left, right, unpack, out, asked):
    sources = gathered.shape[0] // WIDTH
    own = lax.broadcasted_iota(jnp.int32, (HALF, LANES), 0) + place[0] * HALF
    asked[0:HALF] = own.astype(F32)
    for c in range(CELLS):
        asked[HALF + c : HALF + c + 1] = jnp.full((1, LANES), (owner[c] * HALF + slot[c]).astype(F32), F32)
    asked[HALF + CELLS : HALF + CELLS + 1] = left[META_AT + HALO - 1 : META_AT + HALO, 256:384]
    asked[HALF + CELLS + 1 : HALF + CELLS + 2] = right[META_AT : META_AT + 1, 256:384]
    asked[HALF + CELLS + 2 :] = jnp.full((LANES - HALF - CELLS - 2, LANES), -2.0, F32)
    values = gathered[...]
    high, rest = split(values)
    ids = dot(high, unpack[...])
    row = lax.broadcasted_iota(jnp.int32, ids.shape, 0) % WIDTH
    lane = lax.broadcasted_iota(jnp.int32, ids.shape, 1)
    ids = jnp.where(lane // 6 == row, ids, 0.0)
    ids = jnp.sum(ids.reshape(sources, WIDTH, LANES), axis=1)
    lane = lax.broadcasted_iota(jnp.int32, ids.shape, 1)
    source = lax.broadcasted_iota(jnp.int32, ids.shape, 0)
    known = (source * HALF + lane - CELLS).astype(F32)
    ids = jnp.where(lane < CELLS, ids, jnp.where(lane < CELLS + HALF, known, -1.0))
    wanted = asked[...]
    total = jnp.zeros((2 * WIDTH, LANES), F32)
    for s in range(0, sources, 2):
        hot = [jnp.where(wanted == ids[i : i + 1], 1.0, 0.0).astype(BF16) for i in (s, s + 1)]
        both = [jnp.concatenate([high[tile(i)], rest[tile(i)]], 0) for i in (s, s + 1)]
        total = total + dot(jnp.concatenate(both, 1), jnp.concatenate(hot, 1), NT)
    result = total[:WIDTH] + total[WIDTH:]
    for r in range(out.shape[0] // WIDTH):
        out[tile(r)] = result


def apply_kernel(place, columns, orb, linear, ghost, left, right, index, prolong, updated_out, applied_out):
    table = jnp.transpose(columns[...])
    updated_out[...] = table[0:HALF]
    high, rest = split(table[HALF:])
    node = dot(high, prolong[...]) + dot(rest, prolong[...])
    low = lane_below(HALF)
    part_before = new_before = index_before = None
    finished = []
    for e in range(CELLS + 2):
        c = e - 1
        if e == 0:
            values, start, node_at = left[ORB_AT : ORB_AT + WIDTH], ghost[tile(0)], CELLS
        elif e <= CELLS:
            values = orb[c // 2 * 16 : c // 2 * 16 + 16].astype(F32)[tile(c % 2)]
            start, node_at = linear[tile(c)], c
        else:
            values, start, node_at = right[ORB_AT : ORB_AT + WIDTH], ghost[tile(1)], CELLS + 1
        whole = start + node[node_at : node_at + 1] * values
        parts = [whole[:, cols(t)] for t in range(4)]
        if e > 0:
            crossing = jnp.where(low, parts[0], part_before)
            moved = jnp.take_along_axis(crossing, index_before, axis=1, mode="promise_in_bounds")
            if e == 1:
                moved = moved * jnp.where(place[0] > 0, 1.0, 0.0)
            if e == CELLS + 1:
                moved = moved * jnp.where(place[0] < place[2] - 1, 1.0, 0.0)
            done = jnp.where(low, new_before[3], new_before[3] + moved)
            if e > 1:
                finished.append(jnp.concatenate([*new_before[:3], done], 1))
            news = [jnp.where(low, parts[0] + moved, parts[0]), *parts[1:]]
        else:
            news = parts
        part_before, new_before = parts[3], news
        if e == 0:
            meta_row = left[META_AT + HALO - 1 : META_AT + HALO]
            index_before = jnp.broadcast_to(meta_row[:, IDX].astype(jnp.int32), (WIDTH, LANES))
        elif e <= CELLS:
            index_before = index[tile(c)]
        if len(finished) == 2:
            applied_out[(e - 3) * WIDTH : (e - 1) * WIDTH] = jnp.concatenate(finished, 0).astype(BF16)
            finished = []


def unpack_table():
    table = np.zeros((LANES, LANES), np.float32)
    for k in range(CELLS):
        table[112 + k % 6, k] = 64.0
        table[118 + k % 6, k] = 1.0
    return table


def group_table(cells):
    table = np.zeros((LANES, len(cells) * WIDTH), np.float32)
    for at, cell in enumerate(cells):
        table[cell, at * WIDTH : (at + 1) * WIDTH] = 1.0
    return table


def local(orbitals, adjoint_source, eigenvalues, cell_scale, base_potential, stiffness, face_perm, restrict,
          prolong, owner, pot_slot, potential):
    n_dom, n_orb = lax.axis_size("dom"), lax.axis_size("orb")
    dom, orb_at = lax.axis_index("dom"), lax.axis_index("orb")
    vmem = pl.BlockSpec(memory_space=pltpu.VMEM)
    smem = pl.BlockSpec(memory_space=pltpu.SMEM)
    params = pltpu.CompilerParams(vmem_limit_bytes=32 * 2**20)
    struct = jax.ShapeDtypeStruct

    orb2 = orbitals.reshape(CELLS * WIDTH, NODES)
    src2 = adjoint_source.reshape(CELLS * WIDTH, NODES)
    owner1 = owner.reshape(CELLS)
    place = jnp.stack([dom, orb_at, jnp.int32(n_dom)])

    def ends(shape, blocks):
        return [pl.BlockSpec(shape, lambda i: (0, 0)), pl.BlockSpec(shape, lambda i: (blocks - 1, 0))]

    whole = pl.BlockSpec((HALO_ROWS, NODES), lambda i: (0, 0))
    to_left, to_right = pl.pallas_call(
        pack_kernel,
        grid=(1,),
        out_shape=(struct((HALO_ROWS, NODES), F32),) * 2,
        in_specs=[smem] * 3
        + ends((SRC_ROWS, NODES), CELLS // HALO)
        + ends((16, NODES), CELLS // 2)
        + ends((WIDTH, NODES), CELLS // WIDTH)
        + ends((WIDTH, HALF), CELLS // WIDTH),
        out_specs=(whole, whole),
        compiler_params=params,
    )(cell_scale, owner1, pot_slot, src2, src2, orb2, orb2, base_potential, base_potential, face_perm, face_perm)

    ahead = [(i, i + 1) for i in range(n_dom - 1)]
    left = lax.ppermute(to_right, "dom", ahead)
    right = lax.ppermute(to_left, "dom", [(b, a) for a, b in ahead])

    eig = eigenvalues[:, None]
    restrict_t = restrict.T
    rows = CELLS * WIDTH
    inner = rows - 2 * HALO * WIDTH

    def scratch(n):
        return [
            pltpu.VMEM((n, NODES), F32),
            pltpu.VMEM((n, NODES), F32),
            pltpu.VMEM((n, NODES), BF16),
            pltpu.VMEM((n, NODES), F32),
            pltpu.VMEM((n, NODES), F32),
        ]

    adjoint_mid, projected_mid, linear, index, static = pl.pallas_call(
        interior_kernel,
        out_shape=(
            struct((inner, NODES), BF16),
            struct((HALF, LANES), F32),
            struct((rows, NODES), F32),
            struct((rows, LANES), jnp.int32),
            struct((WIDTH, LANES), F32),
        ),
        in_specs=[smem] * 4 + [vmem] * 9,
        out_specs=(vmem,) * 5,
        scratch_shapes=scratch(rows) + [pltpu.VMEM((HALF, HALF), F32)],
        compiler_params=params,
        cost_estimate=pl.CostEstimate(flops=5 * 2 * rows * NODES * NODES, bytes_accessed=4 * 2**20, transcendentals=0),
    )(place, cell_scale, owner1, pot_slot, src2, orb2, base_potential, face_perm, eig, stiffness, restrict_t,
      jnp.asarray(group_table(range(HALO, CELLS - HALO)), BF16), potential)

    edge_cells = [*range(HALO), *range(CELLS - HALO, CELLS)]
    strip_rows = 2 * STRIP * WIDTH
    adjoint2, projected, ghost = pl.pallas_call(
        boundary_kernel,
        out_shape=(
            struct((rows, NODES), BF16),
            struct((HALF, LANES), F32),
            struct((2 * WIDTH, NODES), F32),
        ),
        in_specs=[smem] * 2 + [vmem] * 12,
        out_specs=(vmem,) * 3,
        scratch_shapes=scratch(strip_rows)
        + [
            pltpu.VMEM((strip_rows, LANES), F32),
            pltpu.VMEM((strip_rows, LANES), jnp.int32),
            pltpu.VMEM((2 * WIDTH, NODES), BF16),
        ],
        compiler_params=params,
    )(place, cell_scale, src2, orb2, base_potential, index, left, right, eig, stiffness, restrict_t,
      jnp.asarray(group_table(edge_cells), BF16), adjoint_mid, projected_mid)

    mine = lax.all_to_all(projected.reshape(n_orb, WIDTH, LANES), "orb", split_axis=0, concat_axis=0, tiled=True)
    payload = static - step_rate * jnp.sum(mine, axis=0)
    gathered = lax.all_to_all(
        jnp.broadcast_to(payload[None], (n_dom, WIDTH, LANES)), "dom", split_axis=0, concat_axis=0, tiled=True
    )
    columns = pl.pallas_call(
        sum_kernel,
        out_shape=struct((n_orb * WIDTH, LANES), F32),
        in_specs=[smem] * 3 + [vmem] * 4,
        out_specs=vmem,
        scratch_shapes=[pltpu.VMEM((LANES, LANES), F32)],
        compiler_params=params,
    )(place, owner1, pot_slot, gathered.reshape(n_dom * WIDTH, LANES), left, right, jnp.asarray(unpack_table(), BF16))
    columns = lax.all_to_all(columns.reshape(n_orb, WIDTH, LANES), "orb", split_axis=0, concat_axis=0, tiled=True)
    updated, applied2 = pl.pallas_call(
        apply_kernel,
        out_shape=(struct((HALF, HALF), F32), struct((rows, NODES), BF16)),
        in_specs=[smem] + [vmem] * 8,
        out_specs=(vmem, vmem),
        compiler_params=params,
    )(place, columns.reshape(n_orb * WIDTH, LANES), orb2, linear, ghost, left, right, index, prolong)
    return adjoint2.reshape(orbitals.shape), updated, applied2.reshape(orbitals.shape)


def solution(mesh):
    in_specs = (
        P("dom", "orb", None),
        P("dom", "orb", None),
        P("orb"),
        P("dom"),
        P("dom", None),
        P(),
        P("dom", None),
        P(),
        P(),
        P("dom", None),
        P("dom"),
        P("dom", None),
    )
    out_specs = (P("dom", "orb", None), P("dom", None), P("dom", "orb", None))
    return jax.shard_map(local, mesh=mesh, in_specs=in_specs, out_specs=out_specs, check_vma=False)
```

time: 84.1 us -> 82.3 us (0.979)
  blocking collectives: 10.1 us -> 59.1 us
  waiting for transfers between devices: 24.8 us -> 0.01 us
  starting transfers between devices: 30.4 us -> 5.67 us
  other arithmetic: 4.64 us -> 0.09 us
  Pallas kernels: 7.12 us -> 11.6 us
  local copies, waits for them, and re-layouts: 5.57 us -> 4.44 us
    all_to_all x0 -> x2, blocking collectives: none -> 48.9 us  [the longest x1 37.4 us: local(): lax.all_to_all(jnp.broadcast_to(payload[None], (n_dom, WIDTH, LANES)), 'd...]
    all_to_all x2 -> x0, starting transfers between devices: 24.8 us -> none  [the longest x1 16.6 us: local(): lax.all_to_all(jnp.broadcast_to(payload[None], (n_dom, WIDTH, LANES)), 'd...]
    all_to_all x2 -> x0, waiting for transfers between devices: 20.8 us -> none  [the longest x1 16.4 us: local(): lax.all_to_all(jnp.broadcast_to(payload[None], (n_dom, WIDTH, LANES)), 'd...]
    pallas_call x3 -> x5, Pallas kernels: 7.12 us -> 11.6 us  [the longest x1 4.33 us: local(): pl.pallas_call(interior_kernel, out_shape=(struct((inner, NODES), BF16),...]
    ppermute x2, waiting for transfers between devices: 3.99 us -> 0.01 us  [the longest x1 0.01 us: local(): left = lax.ppermute(to_right, 'dom', ahead)]
    convert_element_type x8 -> x0, other arithmetic: 3.24 us -> none  [the longest x1 0.87 us: packed(): src2[rows].astype(F32)]
    unnamed x23 -> x38, local copies, waits for them, and re-layouts: 1.1 us -> 4.34 us
    concatenate x2 -> x0, local copies, waits for them, and re-layouts: 1.45 us -> none  [the longest x1 1.35 us: local(): jnp.concatenate([(dom * HALF + faces).astype(F32), target.astype(F32), ha...]
  transfers between devices with their start and end apart: 4 -> 2, of which waited for: 3 -> 0; matrix products, arithmetic and copies ran while one was open for 4% -> 0% of each run, Pallas kernels for 0% -> 5%
where the time goes in v2:
time: 82.3 us; the launch traced here: 81.8 us
  blocking collectives  59.1 us (72%)
  Pallas kernels  11.6 us (14%)
  starting transfers between devices  5.67 us (7%)
  local copies, waits for them, and re-layouts  4.44 us (5%)
  between operations  0.83 us (1%)
    all_to_all x1, blocking collectives, local(): lax.all_to_all(jnp.broadcast_to(payload[None], (n_dom, WIDTH, LANES)), 'd...  37.4 us
    all_to_all x1, blocking collectives, local(): lax.all_to_all(projected.reshape(n_orb, WIDTH, LANES), 'orb', split_axis=...  11.5 us
    all_to_all x1, blocking collectives, local(): lax.all_to_all(columns.reshape(n_orb, WIDTH, LANES), 'orb', split_axis=0,...  10.3 us
    ppermute x1, starting transfers between devices, local(): left = lax.ppermute(to_right, 'dom', ahead)  4.38 us
    unnamed x38, local copies, waits for them, and re-layouts  4.34 us
    pallas_call x1, Pallas kernels, local(): pl.pallas_call(interior_kernel, out_shape=(struct((inner, NODES), BF16),...  4.33 us
    pallas_call x1, Pallas kernels, local(): pl.pallas_call(boundary_kernel, out_shape=(struct((rows, NODES), BF16), s...  3.21 us
    pallas_call x1, Pallas kernels, local(): pl.pallas_call(apply_kernel, out_shape=(struct((HALF, HALF), F32), struct...  1.77 us
  transfers between devices with their start and end apart: 2, of which 0 were waited for; matrix products, arithmetic and copies ran while one was open for 0% of the time, Pallas kernels for 5%

profile of v2, /device:TPU:1, one launch (start us, length us, event | category | flops | bytes accessed | tf_op | source)
XLA Modules:
  0.0 81.8 jit_solution(5787420696797899107)
XLA Ops:
  0.7 0.6 copy-done.13
  1.3 0.0 copy-done.14
  1.3 0.0 copy-done.15
  1.3 1.0 %copy-done = bf16[48,8,512]{2,1,0:T(8,128)(2,1)S(1)} copy-done((bf16[48,8,512]{2,1,0:T(8,128)(2,1)S(1)}, bf16[48,8,512]{2,1,0:T(8,128)(2,1)}, u32[]{:S(2)}) %copy-start) | copy-done | bytes 393240
  2.3 1.0 %copy-done.2 = bf16[48,8,512]{2,1,0:T(8,128)(2,1)S(1)} copy-done((bf16[48,8,512]{2,1,0:T(8,128)(2,1)S(1)}, bf16[48,8,512]{2,1,0:T(8,128)(2,1)}, u32[]{:S(2)}) %copy-start.2) | copy-done | bytes 393240
  3.3 0.9 %copy-done.4 = f32[48,512]{1,0:T(8,128)S(1)} copy-done((f32[48,512]{1,0:T(8,128)S(1)}, f32[48,512]{1,0:T(8,128)}, u32[]{:S(2)}) %copy-start.4) | copy-done | bytes 98328
  4.2 0.7 copy-done.7
  5.0 0.0 copy-start.17
  5.0 0.9 %shard_map.167 = (f32[48,512]{1,0:T(8,128)S(1)}, f32[48,512]{1,0:T(8,128)S(1)}) custom-call(f32[48]{0:T(128)S(1)} %copy-done.15, s32[48]{0:T(128)S(1)} %bitcast.28, s32[48]{0:T(128)S(1)} %copy-done.14, bf16[384,512]{1,0:T(8,128)(2,1)S(1)} %bitcast.18, bf16[384,512]{1,0:T(8,128)(2,1)S(1)} %bitcast.19, bf16[384,512]{1,0:T(8,128)(2,1)S(1)} %bitcast.13, ...), custom_call_target="tpu_custom_call" | custom-call | tf_op jit(solution)/shard_map/pallas_call | solution.py:313
  5.9 0.0 copy-start.8
  5.9 4.4 %collective-permute-start = (f32[48,512]{1,0:T(8,128)S(1)}, f32[48,512]{1,0:T(8,128)S(1)}, u32[]{:S(2)}, u32[]{:S(2)}) collective-permute-start(f32[48,512]{1,0:T(8,128)S(1)} %get-tuple-element.16), channel_id=1, source_target_pairs={{0,8},{8,16},{16,24},{24,32},{32,40},{40,48},{48,56},{56,64},{64,7... | collective-permute-start | bytes 294920 | tf_op jit(solution)/shard_map/ppermute | solution.py:327
  10.3 1.3 %collective-permute-start.1 = (f32[48,512]{1,0:T(8,128)S(1)}, f32[48,512]{1,0:T(8,128)S(1)}, u32[]{:S(2)}, u32[]{:S(2)}) collective-permute-start(f32[48,512]{1,0:T(8,128)S(1)} %get-tuple-element.17), channel_id=1, source_target_pairs={{8,0},{16,8},{24,16},{32,24},{40,32},{48,40},{56,48},{64,56},{72,6... | collective-permute-start | bytes 294920 | tf_op jit(solution)/shard_map/ppermute | solution.py:328
  11.6 0.1 pad_add_fusion.place
  11.7 0.1 copy.18.eig
  11.8 0.0 copy-start.11
  11.8 4.3 %shard_map.166 = (bf16[320,512]{1,0:T(8,128)(2,1)S(1)}, f32[64,128]{1,0:T(8,128)S(1)}, f32[384,512]{1,0:T(8,128)S(1)}, s32[384,128]{1,0:T(8,128)S(1)}, f32[8,128]{1,0:T(8,128)S(1)}) custom-call(s32[3]{0:T(128)S(1)} %pad_add_fusion.place, f32[48]{0:T(128)S(1)} %copy-done.15, s32[48]{0:T(128)S(1)} %bitcast.29, s32[48]{0:T(128)S(1)} %copy-done.14, ...), custom_call_target="tpu_custom_call" | custom-call | flops 1006632960 | bytes 4194304 | tf_op jit(solution)/shard_map/pallas_call | solution.py:344
  16.1 0.0 collective-permute-done.left
  16.2 3.2 %shard_map.168 = (bf16[384,512]{1,0:T(8,128)(2,1)}, f32[64,128]{1,0:T(8,128)S(1)}, f32[16,512]{1,0:T(8,128)S(1)}) custom-call(s32[3]{0:T(128)S(1)} %pad_add_fusion.place, f32[48]{0:T(128)S(1)} %copy-done.15, bf16[384,512]{1,0:T(8,128)(2,1)S(1)} %bitcast.21, bf16[384,512]{1,0:T(8,128)(2,1)S(1)} %bitcast.16, f32[48,512]{1,0:T(8,128)S(1)} %copy-done.5, ...), custom_call_target="tpu_custom_call" | custom-call | tf_op jit(solution)/shard_map/pallas_call | solution.py:363
  19.4 11.5 %all_to_all.15 = f32[8,8,128]{2,1,0:T(8,128)S(1)} all-to-all(f32[8,8,128]{2,1,0:T(8,128)S(1)} %bitcast.27), channel_id=1, replica_groups=mesh['dom'=64,'orb'=8] {'orb'}, dimensions={0} | all-to-all | bytes 65536 | tf_op jit(solution)/shard_map/all_to_all | solution.py:382
  30.9 0.0 copy-start.12
  30.9 37.4 %all_to_all.16 = f32[64,8,128]{2,1,0:T(8,128)S(1)} all-to-all(f32[64,8,128]{2,1,0:T(8,128)S(1)} %broadcast_in_dim.10), channel_id=1, replica_groups=mesh['dom'=64,'orb'=8] {'dom'}, dimensions={0} | all-to-all | bytes 524288 | tf_op jit(solution)/shard_map/all_to_all | solution.py:384
  68.3 1.4 %shard_map.169 = f32[64,128]{1,0:T(8,128)S(1)} custom-call(s32[3]{0:T(128)S(1)} %pad_add_fusion.place, s32[48]{0:T(128)S(1)} %bitcast.30, s32[48]{0:T(128)S(1)} %copy-done.14, f32[512,128]{1,0:T(8,128)S(1)} %bitcast.22, f32[48,512]{1,0:T(8,128)S(1)} %collective-permute-done.left, f32[48,512]{1,0:T(8,128)S(1)} %collective-permute-done.1.right, ...), custom_call_target="tpu_custom_call" | custom-call | tf_op jit(solution)/shard_map/pallas_call | solution.py:387
  69.7 10.3 %all_to_all.17 = f32[8,8,128]{2,1,0:T(8,128)S(1)} all-to-all(f32[8,8,128]{2,1,0:T(8,128)S(1)} %bitcast.24), channel_id=1, replica_groups=mesh['dom'=64,'orb'=8] {'orb'}, dimensions={0} | all-to-all | bytes 65536 | tf_op jit(solution)/shard_map/all_to_all | solution.py:395
  80.0 1.8 %shard_map.170 = (f32[64,64]{1,0:T(8,128)}, bf16[384,512]{1,0:T(8,128)(2,1)}) custom-call(s32[3]{0:T(128)S(1)} %pad_add_fusion.place, f32[64,128]{1,0:T(8,128)S(1)} %bitcast.23, bf16[384,512]{1,0:T(8,128)(2,1)S(1)} %bitcast.17, f32[384,512]{1,0:T(8,128)S(1)} %get-tuple-element.23.linear, f32[16,512]{1,0:T(8,128)S(1)} %get-tuple-element.24.ghost, ...), custom_call_target="tpu_custom_call" | custom-call | tf_op jit(solution)/shard_map/pallas_call | solution.py:396
  (31 shorter events, 0.1 us)
Async XLA Ops:
  0.6 0.7 copy-start.13
  0.6 0.7 copy-start.14
  0.7 0.7 copy-start.15
  1.3 1.0 %copy-start = (bf16[48,8,512]{2,1,0:T(8,128)(2,1)S(1)}, bf16[48,8,512]{2,1,0:T(8,128)(2,1)}, u32[]{:S(2)}) copy-start(bf16[48,8,512]{2,1,0:T(8,128)(2,1)} %param.15) | copy-start | bytes 1179652
  2.3 1.0 %copy-start.2 = (bf16[48,8,512]{2,1,0:T(8,128)(2,1)S(1)}, bf16[48,8,512]{2,1,0:T(8,128)(2,1)}, u32[]{:S(2)}) copy-start(bf16[48,8,512]{2,1,0:T(8,128)(2,1)} %param.16) | copy-start | bytes 1179652
  3.3 0.9 %copy-start.4 = (f32[48,512]{1,0:T(8,128)S(1)}, f32[48,512]{1,0:T(8,128)}, u32[]{:S(2)}) copy-start(f32[48,512]{1,0:T(8,128)} %base.3) | copy-start | bytes 294916
  4.2 0.7 copy-start.7
  4.9 6.7 %copy-start.18 = (f32[8]{0:T(128)S(1)}, f32[8]{0:T(128)}, u32[]{:S(2)}) copy-start(f32[8]{0:T(128)} %param.17) | copy-start | bytes 100
  4.9 6.8 %copy-start.1 = (bf16[48,8,512]{2,1,0:T(8,128)(2,1)S(1)}, bf16[48,8,512]{2,1,0:T(8,128)(2,1)}, u32[]{:S(2)}) copy-start(bf16[48,8,512]{2,1,0:T(8,128)(2,1)} %param.15) | copy-start | bytes 1179652
  5.0 6.8 %copy-start.3 = (bf16[48,8,512]{2,1,0:T(8,128)(2,1)S(1)}, bf16[48,8,512]{2,1,0:T(8,128)(2,1)}, u32[]{:S(2)}) copy-start(bf16[48,8,512]{2,1,0:T(8,128)(2,1)} %param.16) | copy-start | bytes 1179652
  5.0 6.8 %copy-start.5 = (f32[48,512]{1,0:T(8,128)S(1)}, f32[48,512]{1,0:T(8,128)}, u32[]{:S(2)}) copy-start(f32[48,512]{1,0:T(8,128)} %base.3) | copy-start | bytes 294916
  5.0 6.8 %copy-start.6 = (bf16[512,512]{1,0:T(8,128)(2,1)S(1)}, bf16[512,512]{1,0:T(8,128)(2,1)}, u32[]{:S(2)}) copy-start(bf16[512,512]{1,0:T(8,128)(2,1)} %stiff.3) | copy-start | bytes 1572868
  5.0 6.8 %copy-start.9 = (bf16[512,64]{0,1:T(8,128)(2,1)S(1)}, bf16[512,64]{0,1:T(8,128)(2,1)}, u32[]{:S(2)}) copy-start(bf16[512,64]{0,1:T(8,128)(2,1)} %param.22) | copy-start | bytes 196612
  5.0 6.8 %copy-start.16 = (f32[64,64]{1,0:T(8,128)S(1)}, f32[64,64]{1,0:T(8,128)}, u32[]{:S(2)}) copy-start(f32[64,64]{1,0:T(8,128)} %potential.1) | copy-start | bytes 49156
  5.0 6.8 %copy-start.17 = (bf16[128,320]{1,0:T(8,128)(2,1)S(1)}, bf16[128,320]{1,0:T(8,128)(2,1)}, u32[]{:S(2)}) copy-start(bf16[128,320]{1,0:T(8,128)(2,1)} %constant.21.clone.group) | copy-start | bytes 245764
  5.9 5.9 %copy-start.8 = (s32[48,64]{1,0:T(8,128)S(1)}, s32[48,64]{1,0:T(8,128)}, u32[]{:S(2)}) copy-start(s32[48,64]{1,0:T(8,128)} %perm_high.1) | copy-start | bytes 36868
  5.9 10.3 %collective-permute-start = (f32[48,512]{1,0:T(8,128)S(1)}, f32[48,512]{1,0:T(8,128)S(1)}, u32[]{:S(2)}, u32[]{:S(2)}) collective-permute-start(f32[48,512]{1,0:T(8,128)S(1)} %get-tuple-element.16), channel_id=1, source_target_pairs={{0,8},{8,16},{16,24},{24,32},{32,40},{40,48},{48,56},{56,64},{64,7... | collective-permute-start | bytes 294920 | tf_op jit(solution)/shard_map/ppermute | solution.py:327
  10.3 5.9 %collective-permute-start.1 = (f32[48,512]{1,0:T(8,128)S(1)}, f32[48,512]{1,0:T(8,128)S(1)}, u32[]{:S(2)}, u32[]{:S(2)}) collective-permute-start(f32[48,512]{1,0:T(8,128)S(1)} %get-tuple-element.17), channel_id=1, source_target_pairs={{8,0},{16,8},{24,16},{32,24},{40,32},{48,40},{56,48},{64,56},{72,6... | collective-permute-start | bytes 294920 | tf_op jit(solution)/shard_map/ppermute | solution.py:328
  11.8 4.4 %copy-start.11 = (bf16[128,64]{1,0:T(8,128)(2,1)S(1)}, bf16[128,64]{1,0:T(8,128)(2,1)}, u32[]{:S(2)}) copy-start(bf16[128,64]{1,0:T(8,128)(2,1)} %constant.22.clone.group) | copy-start | bytes 49156
  30.9 37.4 %copy-start.12 = (bf16[128,128]{1,0:T(8,128)(2,1)S(1)}, bf16[128,128]{1,0:T(8,128)(2,1)}, u32[]{:S(2)}) copy-start(bf16[128,128]{1,0:T(8,128)(2,1)} %constant.23.clone.unpack) | copy-start | bytes 98308
  69.7 10.3 %copy-start.10 = (bf16[64,512]{1,0:T(8,128)(2,1)S(1)}, bf16[64,512]{1,0:T(8,128)(2,1)}, u32[]{:S(2)}) copy-start(bf16[64,512]{1,0:T(8,128)(2,1)} %prolong.1) | copy-start | bytes 196612

commit v3 on v2

--- a/solution.py
+++ b/solution.py
@@ -60,23 +60,37 @@
     return rows
 
 
-def pack_kernel(scale, owner, slot, src_low, src_high, orb_low, orb_high, base_low, base_high, perm_low, perm_high,
-                to_left, to_right):
-    def put(out, src, orb, base, perm, first, orb_at, edge_cell):
-        inner = 0 if first == 0 else WIDTH - HALO
-        out[0:SRC_ROWS] = src[...].astype(F32)
-        out[ORB_AT : ORB_AT + WIDTH] = orb[...].astype(F32)[tile(orb_at)]
-        out[BASE_AT : BASE_AT + HALO] = base[inner : inner + HALO]
-        faces = face_rows(perm[...], range(inner, inner + HALO))
+def in_hbm(array):
+    return pltpu.with_memory_space_constraint(array, pltpu.HBM)
+
+
+def pack_kernel(scale_hbm, owner_hbm, slot_hbm, src_hbm, orb_hbm, base_hbm, perm_hbm, to_left, to_right,
+                scale, owner, slot, src, orb, base, perm, sems):
+    top, rows = CELLS - WIDTH, CELLS * WIDTH
+    copies = [(scale_hbm, scale), (owner_hbm, owner), (slot_hbm, slot)]
+    for hbm, here, size, end in (
+        (src_hbm, src, SRC_ROWS, rows), (orb_hbm, orb, 16, rows), (base_hbm, base, WIDTH, CELLS), (perm_hbm, perm, WIDTH, CELLS)
+    ):
+        copies.append((hbm.at[0:size], here.at[0]))
+        copies.append((hbm.at[end - size : end], here.at[1]))
+    copies = [pltpu.make_async_copy(one, two, sems.at[i]) for i, (one, two) in enumerate(copies)]
+    for copy in copies:
+        copy.start()
+    for copy in copies:
+        copy.wait()
+    for end, out in enumerate((to_left, to_right)):
+        inner, first = (0, 0) if end == 0 else (HALO, CELLS - HALO)
+        edge_cell = end * (CELLS - 1)
+        out[0:SRC_ROWS] = src[end].astype(F32)
+        out[ORB_AT : ORB_AT + WIDTH] = orb[end].astype(F32)[tile(end)]
+        out[BASE_AT : BASE_AT + HALO] = base[end, inner : inner + HALO]
+        faces = face_rows(perm[end], range(inner, inner + HALO))
         target = (owner[edge_cell] * HALF + slot[edge_cell]).astype(F32)
         for i in range(HALO):
             at = slice(META_AT + i, META_AT + i + 1)
             out[at, IDX] = faces[i]
             out[at, SCALE] = jnp.full((1, LANES), scale[first + i], F32)
             out[at, TARGET] = jnp.full((1, 2 * LANES), target, F32)
-
-    put(to_left, src_low, orb_low, base_low, perm_low, 0, 0, 0)
-    put(to_right, src_high, orb_high, base_high, perm_high, CELLS - HALO, 1, CELLS - 1)
 
 
 def relaxed(strips, x, quarter, shifted, xb, kin, stiff, factor, index, gates):
@@ -120,9 +134,13 @@
     return dot(restrict_t, high, NT) + dot(restrict_t, rest, NT)
 
 
-def interior_kernel(place, scale, owner, slot, src, orb, base, perm, eig, stiff, restrict_t, group, potential,
-                    adjoint_out, projected_out, linear_out, index_out, static_out,
-                    x, quarter, xb, kin, shifted, turned):
+def interior_kernel(place, scale, owner, slot, src, orb, base, perm, eig, stiff_hbm, restrict_hbm, group_hbm,
+                    potential_hbm, adjoint_out, projected_out, linear_out, index_out, static_out,
+                    x, quarter, xb, kin, shifted, turned, stiff, restrict_t, group, potential, sems):
+    pairs = ((stiff_hbm, stiff), (restrict_hbm, restrict_t), (group_hbm, group), (potential_hbm, potential))
+    copies = [pltpu.make_async_copy(one, two, sems.at[i]) for i, (one, two) in enumerate(pairs)]
+    for copy in copies:
+        copy.start()
     quarter[...] = relax * src[...].astype(F32)
     x[...] = quarter[...]
     eig_column = eig[...]
@@ -130,6 +148,8 @@
     for c in range(CELLS):
         shifted[tile(c)] = base[c : c + 1] - eig_column
         index_out[tile(c)] = jnp.broadcast_to(faces[c].astype(jnp.int32), (WIDTH, LANES))
+    for copy in copies:
+        copy.wait()
     relaxed([range(CELLS)], x, quarter, shifted, xb, kin, stiff, lambda c: scale[c], index_out, {})
     inner = slice(HALO * WIDTH, (CELLS - HALO) * WIDTH)
     adjoint_out[...] = x[inner].astype(BF16)
@@ -154,9 +174,15 @@
 
 def boundary_kernel(place, scale, src, orb, base, index_own, left, right, eig, stiff, restrict_t, group, adjoint_mid,
                     projected_mid, adjoint_out, projected_out, ghost_out,
-                    x, quarter, xb, kin, shifted, factor, index, ob):
+                    x, quarter, xb, kin, shifted, factor, index, ob, adjoint_ends, sems):
     near, edge = 2 * HALO * WIDTH, HALO * WIDTH
     last = CELLS * WIDTH
+    copies = [
+        pltpu.make_async_copy(adjoint_mid, adjoint_out.at[edge : last - edge], sems.at[0]),
+        pltpu.make_async_copy(adjoint_ends.at[0], adjoint_out.at[0:edge], sems.at[1]),
+        pltpu.make_async_copy(adjoint_ends.at[1], adjoint_out.at[last - edge : last], sems.at[2]),
+    ]
+    copies[0].start()
     quarter[0:edge] = relax * left[0:SRC_ROWS]
     quarter[edge : edge + near] = relax * src[0:near].astype(F32)
     quarter[edge + near : edge + 2 * near] = relax * src[last - near :].astype(F32)
@@ -184,9 +210,10 @@
     relaxed([range(STRIP), range(STRIP, 2 * STRIP)], x, quarter, shifted, xb, kin, stiff,
             lambda e: factor[tile(e)], index, gates)
     low_cells, high_cells = x[edge : 2 * edge], x[4 * edge : 5 * edge]
-    adjoint_out[0:edge] = low_cells.astype(BF16)
-    adjoint_out[edge : last - edge] = adjoint_mid[...]
-    adjoint_out[last - edge :] = high_cells.astype(BF16)
+    adjoint_ends[0] = low_cells.astype(BF16)
+    adjoint_ends[1] = high_cells.astype(BF16)
+    copies[1].start()
+    copies[2].start()
     own_orb = jnp.concatenate([orb[0:edge], orb[last - edge :]], 0)
     own_x = jnp.concatenate([low_cells, high_cells], 0)
     projected_out[...] = projected_mid[...] + projection(own_orb, own_x, group[...], restrict_t[...])
@@ -201,6 +228,8 @@
             ghost_out[tile(i), cols(t)] = (
                 factor[tile(e)] * ghost_kin[tile(i), cols(t)] + base_row[:, cols(t)] * ghosts[tile(i), cols(t)]
             )
+    for copy in copies:
+        copy.wait()
 
 
 def sum_kernel(place, owner, slot, gathered, left, right, unpack, out, asked):
@@ -306,22 +335,24 @@
     owner1 = owner.reshape(CELLS)
     place = jnp.stack([dom, orb_at, jnp.int32(n_dom)])
 
-    def ends(shape, blocks):
-        return [pl.BlockSpec(shape, lambda i: (0, 0)), pl.BlockSpec(shape, lambda i: (blocks - 1, 0))]
-
-    whole = pl.BlockSpec((HALO_ROWS, NODES), lambda i: (0, 0))
+    hbm = pl.BlockSpec(memory_space=pltpu.HBM)
     to_left, to_right = pl.pallas_call(
         pack_kernel,
-        grid=(1,),
         out_shape=(struct((HALO_ROWS, NODES), F32),) * 2,
-        in_specs=[smem] * 3
-        + ends((SRC_ROWS, NODES), CELLS // HALO)
-        + ends((16, NODES), CELLS // 2)
-        + ends((WIDTH, NODES), CELLS // WIDTH)
-        + ends((WIDTH, HALF), CELLS // WIDTH),
-        out_specs=(whole, whole),
+        in_specs=[hbm] * 7,
+        out_specs=(vmem, vmem),
+        scratch_shapes=[
+            pltpu.SMEM((CELLS,), F32),
+            pltpu.SMEM((CELLS,), jnp.int32),
+            pltpu.SMEM((CELLS,), jnp.int32),
+            pltpu.VMEM((2, SRC_ROWS, NODES), BF16),
+            pltpu.VMEM((2, 16, NODES), BF16),
+            pltpu.VMEM((2, WIDTH, NODES), F32),
+            pltpu.VMEM((2, WIDTH, HALF), jnp.int32),
+            pltpu.SemaphoreType.DMA((11,)),
+        ],
         compiler_params=params,
-    )(cell_scale, owner1, pot_slot, src2, src2, orb2, orb2, base_potential, base_potential, face_perm, face_perm)
+    )(*map(in_hbm, (cell_scale, owner1, pot_slot, src2, orb2, base_potential, face_perm)))
 
     ahead = [(i, i + 1) for i in range(n_dom - 1)]
     left = lax.ppermute(to_right, "dom", ahead)
@@ -350,13 +381,22 @@
             struct((rows, LANES), jnp.int32),
             struct((WIDTH, LANES), F32),
         ),
-        in_specs=[smem] * 4 + [vmem] * 9,
+        in_specs=[smem] * 4 + [vmem] * 5 + [hbm] * 4,
         out_specs=(vmem,) * 5,
-        scratch_shapes=scratch(rows) + [pltpu.VMEM((HALF, HALF), F32)],
+        scratch_shapes=scratch(rows)
+        + [
+            pltpu.VMEM((HALF, HALF), F32),
+            pltpu.VMEM((NODES, NODES), BF16),
+            pltpu.VMEM((HALF, NODES), BF16),
+            pltpu.VMEM((LANES, inner), BF16),
+            pltpu.VMEM((HALF, HALF), F32),
+            pltpu.SemaphoreType.DMA((4,)),
+        ],
         compiler_params=params,
         cost_estimate=pl.CostEstimate(flops=5 * 2 * rows * NODES * NODES, bytes_accessed=4 * 2**20, transcendentals=0),
-    )(place, cell_scale, owner1, pot_slot, src2, orb2, base_potential, face_perm, eig, stiffness, restrict_t,
-      jnp.asarray(group_table(range(HALO, CELLS - HALO)), BF16), potential)
+    )(place, cell_scale, owner1, pot_slot, src2, orb2, base_potential, face_perm, eig, *map(
+          in_hbm, (stiffness, restrict_t, jnp.asarray(group_table(range(HALO, CELLS - HALO)), BF16), potential)
+      ))
 
     edge_cells = [*range(HALO), *range(CELLS - HALO, CELLS)]
     strip_rows = 2 * STRIP * WIDTH
@@ -368,12 +408,14 @@
             struct((2 * WIDTH, NODES), F32),
         ),
         in_specs=[smem] * 2 + [vmem] * 12,
-        out_specs=(vmem,) * 3,
+        out_specs=(hbm, vmem, vmem),
         scratch_shapes=scratch(strip_rows)
         + [
             pltpu.VMEM((strip_rows, LANES), F32),
             pltpu.VMEM((strip_rows, LANES), jnp.int32),
             pltpu.VMEM((2 * WIDTH, NODES), BF16),
+            pltpu.VMEM((2, HALO * WIDTH, NODES), BF16),
+            pltpu.SemaphoreType.DMA((3,)),
         ],
         compiler_params=params,
     )(place, cell_scale, src2, orb2, base_potential, index, left, right, eig, stiffness, restrict_t,

time: 82.3 us -> 78.7 us (0.956)
  local copies, waits for them, and re-layouts: 4.44 us -> 0.8 us
    unnamed x38 -> x26, local copies, waits for them, and re-layouts: 4.34 us -> 0.69 us
  transfers between devices with their start and end apart: 2 -> 2, of which waited for: 0 -> 0; matrix products, arithmetic and copies ran while one was open for 0% -> 0% of each run, Pallas kernels for 5% -> 6%
where the time goes in v3:
time: 78.7 us; the launch traced here: 78.3 us
  blocking collectives  59.2 us (75%)
  Pallas kernels  11.8 us (15%)
  starting transfers between devices  5.67 us (7%)
  between operations  0.81 us (1%)
  local copies, waits for them, and re-layouts  0.8 us (1%)
    all_to_all x1, blocking collectives, local(): lax.all_to_all(jnp.broadcast_to(payload[None], (n_dom, WIDTH, LANES)), 'd...  38 us
    all_to_all x1, blocking collectives, local(): lax.all_to_all(projected.reshape(n_orb, WIDTH, LANES), 'orb', split_axis=...  10.9 us
    all_to_all x1, blocking collectives, local(): lax.all_to_all(columns.reshape(n_orb, WIDTH, LANES), 'orb', split_axis=0,...  10.3 us
    pallas_call x1, Pallas kernels, local(): pl.pallas_call(interior_kernel, out_shape=(struct((inner, NODES), BF16),...  4.58 us
    ppermute x1, starting transfers between devices, local(): left = lax.ppermute(to_right, 'dom', ahead)  4.38 us
    pallas_call x1, Pallas kernels, local(): pl.pallas_call(boundary_kernel, out_shape=(struct((rows, NODES), BF16), s...  2.74 us
    pallas_call x1, Pallas kernels, local(): pl.pallas_call(apply_kernel, out_shape=(struct((HALF, HALF), F32), struct...  1.77 us
  transfers between devices with their start and end apart: 2, of which 0 were waited for; matrix products, arithmetic and copies ran while one was open for 0% of the time, Pallas kernels for 6%

profile of v3, /device:TPU:1, one launch (start us, length us, event | category | flops | bytes accessed | tf_op | source)
XLA Modules:
  0.0 78.3 jit_solution(4005896554071519251)
XLA Ops:
  0.6 0.0 copy-start.12
  0.6 0.0 copy-start
  0.7 1.3 %shard_map.167 = (f32[48,512]{1,0:T(8,128)S(1)}, f32[48,512]{1,0:T(8,128)S(1)}) custom-call(f32[48]{0:T(128)} %scale.3, s32[48]{0:T(128)} %bitcast.26, s32[48]{0:T(128)} %slot.3, bf16[384,512]{1,0:T(8,128)(2,1)} %bitcast.17, bf16[384,512]{1,0:T(8,128)(2,1)} %bitcast.13, f32[48,512]{1,0:T(8,128)} %base.3, s32[48,64]{1,0:T(8,128)} %perm_hbm.1), custom_call_target="tpu_custom_call" | custom-call | tf_op jit(solution)/shard_map/pallas_call | solution.py:339
  2.0 0.0 copy-start.8
  2.0 4.4 %collective-permute-start = (f32[48,512]{1,0:T(8,128)S(1)}, f32[48,512]{1,0:T(8,128)S(1)}, u32[]{:S(2)}, u32[]{:S(2)}) collective-permute-start(f32[48,512]{1,0:T(8,128)S(1)} %get-tuple-element.16), channel_id=1, source_target_pairs={{0,8},{8,16},{16,24},{24,32},{32,40},{40,48},{48,56},{56,64},{64,7... | collective-permute-start | bytes 294920 | tf_op jit(solution)/shard_map/ppermute | solution.py:358
  6.4 1.3 %collective-permute-start.1 = (f32[48,512]{1,0:T(8,128)S(1)}, f32[48,512]{1,0:T(8,128)S(1)}, u32[]{:S(2)}, u32[]{:S(2)}) collective-permute-start(f32[48,512]{1,0:T(8,128)S(1)} %get-tuple-element.17), channel_id=1, source_target_pairs={{8,0},{16,8},{24,16},{32,24},{40,32},{48,40},{56,48},{64,56},{72,6... | collective-permute-start | bytes 294920 | tf_op jit(solution)/shard_map/ppermute | solution.py:359
  7.7 0.1 pad_add_fusion.place
  7.8 0.1 copy.18.eig
  7.9 0.0 copy-done.1
  7.9 0.0 copy-done.3
  7.9 0.0 copy-done.8
  7.9 0.6 copy-done.9
  8.5 0.0 copy-done.10
  8.5 0.0 copy-done.11
  8.5 4.6 %shard_map.166 = (bf16[320,512]{1,0:T(8,128)(2,1)S(1)}, f32[64,128]{1,0:T(8,128)S(1)}, f32[384,512]{1,0:T(8,128)S(1)}, s32[384,128]{1,0:T(8,128)S(1)}, f32[8,128]{1,0:T(8,128)S(1)}) custom-call(s32[3]{0:T(128)S(1)} %pad_add_fusion.place, f32[48]{0:T(128)S(1)} %copy-done.11, s32[48]{0:T(128)S(1)} %bitcast.27, s32[48]{0:T(128)S(1)} %copy-done.10, ...), custom_call_target="tpu_custom_call" | custom-call | flops 1006632960 | bytes 4194304 | tf_op jit(solution)/shard_map/pallas_call | solution.py:375
  13.1 0.0 collective-permute-done.left
  13.1 0.0 collective-permute-done.1.right
  13.2 2.7 %shard_map.168 = (bf16[384,512]{1,0:T(8,128)(2,1)}, f32[64,128]{1,0:T(8,128)S(1)}, f32[16,512]{1,0:T(8,128)S(1)}) custom-call(s32[3]{0:T(128)S(1)} %pad_add_fusion.place, f32[48]{0:T(128)S(1)} %copy-done.11, bf16[384,512]{1,0:T(8,128)(2,1)S(1)} %bitcast.19, bf16[384,512]{1,0:T(8,128)(2,1)S(1)} %bitcast.15, f32[48,512]{1,0:T(8,128)S(1)} %copy-done.3, ...), custom_call_target="tpu_custom_call" | custom-call | tf_op jit(solution)/shard_map/pallas_call | solution.py:403
  15.9 10.9 %all_to_all.15 = f32[8,8,128]{2,1,0:T(8,128)S(1)} all-to-all(f32[8,8,128]{2,1,0:T(8,128)S(1)} %bitcast.25), channel_id=1, replica_groups=mesh['dom'=64,'orb'=8] {'orb'}, dimensions={0} | all-to-all | bytes 65536 | tf_op jit(solution)/shard_map/all_to_all | solution.py:424
  26.8 0.0 copy-start.7
  26.8 38.0 %all_to_all.16 = f32[64,8,128]{2,1,0:T(8,128)S(1)} all-to-all(f32[64,8,128]{2,1,0:T(8,128)S(1)} %broadcast_in_dim.10), channel_id=1, replica_groups=mesh['dom'=64,'orb'=8] {'dom'}, dimensions={0} | all-to-all | bytes 524288 | tf_op jit(solution)/shard_map/all_to_all | solution.py:426
  64.9 1.4 %shard_map.169 = f32[64,128]{1,0:T(8,128)S(1)} custom-call(s32[3]{0:T(128)S(1)} %pad_add_fusion.place, s32[48]{0:T(128)S(1)} %bitcast.28, s32[48]{0:T(128)S(1)} %copy-done.10, f32[512,128]{1,0:T(8,128)S(1)} %bitcast.20, f32[48,512]{1,0:T(8,128)S(1)} %collective-permute-done.left, f32[48,512]{1,0:T(8,128)S(1)} %collective-permute-done.1.right, ...), custom_call_target="tpu_custom_call" | custom-call | tf_op jit(solution)/shard_map/pallas_call | solution.py:429
  66.3 10.3 %all_to_all.17 = f32[8,8,128]{2,1,0:T(8,128)S(1)} all-to-all(f32[8,8,128]{2,1,0:T(8,128)S(1)} %bitcast.22), channel_id=1, replica_groups=mesh['dom'=64,'orb'=8] {'orb'}, dimensions={0} | all-to-all | bytes 65536 | tf_op jit(solution)/shard_map/all_to_all | solution.py:437
  76.5 1.8 %shard_map.170 = (f32[64,64]{1,0:T(8,128)}, bf16[384,512]{1,0:T(8,128)(2,1)}) custom-call(s32[3]{0:T(128)S(1)} %pad_add_fusion.place, f32[64,128]{1,0:T(8,128)S(1)} %bitcast.21, bf16[384,512]{1,0:T(8,128)(2,1)S(1)} %bitcast.16, f32[384,512]{1,0:T(8,128)S(1)} %get-tuple-element.23.linear, f32[16,512]{1,0:T(8,128)S(1)} %get-tuple-element.24.ghost, ...), custom_call_target="tpu_custom_call" | custom-call | tf_op jit(solution)/shard_map/pallas_call | solution.py:438
  (19 shorter events, 0.1 us)
Async XLA Ops:
  0.6 7.1 %copy-start.12 = (f32[8]{0:T(128)S(1)}, f32[8]{0:T(128)}, u32[]{:S(2)}) copy-start(f32[8]{0:T(128)} %param.17) | copy-start | bytes 100
  0.6 7.2 %copy-start = (bf16[48,8,512]{2,1,0:T(8,128)(2,1)S(1)}, bf16[48,8,512]{2,1,0:T(8,128)(2,1)}, u32[]{:S(2)}) copy-start(bf16[48,8,512]{2,1,0:T(8,128)(2,1)} %param.15) | copy-start | bytes 1179652
  0.7 7.2 %copy-start.1 = (bf16[48,8,512]{2,1,0:T(8,128)(2,1)S(1)}, bf16[48,8,512]{2,1,0:T(8,128)(2,1)}, u32[]{:S(2)}) copy-start(bf16[48,8,512]{2,1,0:T(8,128)(2,1)} %param.16) | copy-start | bytes 1179652
  0.7 7.2 %copy-start.3 = (f32[48,512]{1,0:T(8,128)S(1)}, f32[48,512]{1,0:T(8,128)}, u32[]{:S(2)}) copy-start(f32[48,512]{1,0:T(8,128)} %base.3) | copy-start | bytes 294916
  2.0 5.9 %copy-start.8 = (s32[48,64]{1,0:T(8,128)S(1)}, s32[48,64]{1,0:T(8,128)}, u32[]{:S(2)}) copy-start(s32[48,64]{1,0:T(8,128)} %perm_hbm.1) | copy-start | bytes 36868
  2.0 11.1 %collective-permute-start = (f32[48,512]{1,0:T(8,128)S(1)}, f32[48,512]{1,0:T(8,128)S(1)}, u32[]{:S(2)}, u32[]{:S(2)}) collective-permute-start(f32[48,512]{1,0:T(8,128)S(1)} %get-tuple-element.16), channel_id=1, source_target_pairs={{0,8},{8,16},{16,24},{24,32},{32,40},{40,48},{48,56},{56,64},{64,7... | collective-permute-start | bytes 294920 | tf_op jit(solution)/shard_map/ppermute | solution.py:358
  6.4 6.8 %collective-permute-start.1 = (f32[48,512]{1,0:T(8,128)S(1)}, f32[48,512]{1,0:T(8,128)S(1)}, u32[]{:S(2)}, u32[]{:S(2)}) collective-permute-start(f32[48,512]{1,0:T(8,128)S(1)} %get-tuple-element.17), channel_id=1, source_target_pairs={{8,0},{16,8},{24,16},{32,24},{40,32},{48,40},{56,48},{64,56},{72,6... | collective-permute-start | bytes 294920 | tf_op jit(solution)/shard_map/ppermute | solution.py:359
  7.8 0.7 copy-start.9
  7.8 0.7 copy-start.10
  7.8 0.7 copy-start.11
  8.5 4.6 %copy-start.2 = (bf16[512,512]{1,0:T(8,128)(2,1)S(1)}, bf16[512,512]{1,0:T(8,128)(2,1)}, u32[]{:S(2)}) copy-start(bf16[512,512]{1,0:T(8,128)(2,1)} %stiff.1) | copy-start | bytes 1572868
  8.5 4.6 %copy-start.4 = (bf16[512,64]{0,1:T(8,128)(2,1)S(1)}, bf16[512,64]{0,1:T(8,128)(2,1)}, u32[]{:S(2)}) copy-start(bf16[512,64]{0,1:T(8,128)(2,1)} %param.22) | copy-start | bytes 196612
  8.5 4.6 %copy-start.6 = (bf16[128,64]{1,0:T(8,128)(2,1)S(1)}, bf16[128,64]{1,0:T(8,128)(2,1)}, u32[]{:S(2)}) copy-start(bf16[128,64]{1,0:T(8,128)(2,1)} %constant.22.clone.group) | copy-start | bytes 49156
  26.8 38.0 %copy-start.7 = (bf16[128,128]{1,0:T(8,128)(2,1)S(1)}, bf16[128,128]{1,0:T(8,128)(2,1)}, u32[]{:S(2)}) copy-start(bf16[128,128]{1,0:T(8,128)(2,1)} %constant.23.clone.unpack) | copy-start | bytes 98308
  66.3 10.3 %copy-start.5 = (bf16[64,512]{1,0:T(8,128)(2,1)S(1)}, bf16[64,512]{1,0:T(8,128)(2,1)}, u32[]{:S(2)}) copy-start(bf16[64,512]{1,0:T(8,128)(2,1)} %prolong.1) | copy-start | bytes 196612

commit v4 on v3

--- a/solution.py
+++ b/solution.py
@@ -34,7 +34,11 @@
 
 
 SRC_ROWS, ORB_AT, BASE_AT, META_AT, HALO_ROWS = 32, 32, 40, 44, 48
-IDX, SCALE, TARGET = slice(0, 128), slice(128, 256), slice(256, 512)
+IDX, SCALE, OWNER, SLOT = slice(0, 128), slice(128, 256), slice(256, 384), slice(384, 512)
+POT, IDS, GHOST_IDS = CELLS, CELLS + HALF, CELLS + HALF + 12
+X, Z, Y, CORES = 4, 16, 4, 2
+DOM, ORB, OUTER = ("x", "z"), ("y", "core"), ("x", "y", "core")
+COPIES = Y * CORES
 STRIP = 3 * HALO
 NT = ((1,), (1,))
 
@@ -85,12 +89,12 @@
         out[ORB_AT : ORB_AT + WIDTH] = orb[end].astype(F32)[tile(end)]
         out[BASE_AT : BASE_AT + HALO] = base[end, inner : inner + HALO]
         faces = face_rows(perm[end], range(inner, inner + HALO))
-        target = (owner[edge_cell] * HALF + slot[edge_cell]).astype(F32)
         for i in range(HALO):
             at = slice(META_AT + i, META_AT + i + 1)
             out[at, IDX] = faces[i]
             out[at, SCALE] = jnp.full((1, LANES), scale[first + i], F32)
-            out[at, TARGET] = jnp.full((1, 2 * LANES), target, F32)
+            out[at, OWNER] = jnp.full((1, LANES), owner[edge_cell].astype(F32), F32)
+            out[at, SLOT] = jnp.full((1, LANES), slot[edge_cell].astype(F32), F32)
 
 
 def relaxed(strips, x, quarter, shifted, xb, kin, stiff, factor, index, gates):
@@ -135,8 +139,8 @@
 
 
 def interior_kernel(place, scale, owner, slot, src, orb, base, perm, eig, stiff_hbm, restrict_hbm, group_hbm,
-                    potential_hbm, adjoint_out, projected_out, linear_out, index_out, static_out,
-                    x, quarter, xb, kin, shifted, turned, stiff, restrict_t, group, potential, sems):
+                    potential_hbm, adjoint_out, projected_out, linear_out, index_out,
+                    x, quarter, xb, kin, shifted, stiff, restrict_t, group, potential, sems):
     pairs = ((stiff_hbm, stiff), (restrict_hbm, restrict_t), (group_hbm, group), (potential_hbm, potential))
     copies = [pltpu.make_async_copy(one, two, sems.at[i]) for i, (one, two) in enumerate(pairs)]
     for copy in copies:
@@ -153,23 +157,22 @@
     relaxed([range(CELLS)], x, quarter, shifted, xb, kin, stiff, lambda c: scale[c], index_out, {})
     inner = slice(HALO * WIDTH, (CELLS - HALO) * WIDTH)
     adjoint_out[...] = x[inner].astype(BF16)
-    projected_out[...] = projection(orb[inner], x[inner], group[...], restrict_t[...])
     kin[...] = dot(orb[...], stiff[...])
     for pair in range(CELLS // 2):
         values = orb[pair * 16 : pair * 16 + 16].astype(F32)
         for c in (2 * pair, 2 * pair + 1):
             linear_out[tile(c)] = scale[c] * kin[tile(c)] + base[c : c + 1] * values[tile(c % 2)]
-    turned[...] = jnp.transpose(potential[...])
-    columns = turned[pl.ds(pl.multiple_of(place[1] * WIDTH, WIDTH), WIDTH)]
     row = lax.broadcasted_iota(jnp.int32, (WIDTH, LANES), 0)
     lane = lax.broadcasted_iota(jnp.int32, (WIDTH, LANES), 1)
-    at = jnp.where(lane >= CELLS + HALF, row * 12 + lane - CELLS - HALF, -1)
-    at = jnp.where(lane < CELLS + HALF + 12, at, -1)
-    static = jnp.concatenate([jnp.zeros((WIDTH, CELLS), F32), columns, jnp.zeros((WIDTH, 16), F32)], 1)
+    at = jnp.where((lane >= IDS) & (lane < GHOST_IDS), row * 12 + lane - IDS, -1)
+    ids = jnp.zeros((WIDTH, LANES), F32)
     for c in range(CELLS):
-        static = jnp.where(at == c // 6 * 12 + c % 6, owner[c].astype(F32), static)
-        static = jnp.where(at == c // 6 * 12 + 6 + c % 6, slot[c].astype(F32), static)
-    static_out[...] = static
+        ids = jnp.where(at == c // 6 * 12 + c % 6, owner[c].astype(F32), ids)
+        ids = jnp.where(at == c // 6 * 12 + 6 + c % 6, slot[c].astype(F32), ids)
+    turned = jnp.transpose(potential[...])
+    static = jnp.concatenate([jnp.zeros((HALF, CELLS), F32), turned, jnp.zeros((HALF, 16), F32)], 1)
+    static = (static + jnp.concatenate([ids] * (HALF // WIDTH), 0)) * (1.0 / COPIES)
+    projected_out[...] = static - step_rate * projection(orb[inner], x[inner], group[...], restrict_t[...])
 
 
 def boundary_kernel(place, scale, src, orb, base, index_own, left, right, eig, stiff, restrict_t, group, adjoint_mid,
@@ -205,7 +208,7 @@
         shifted[tile(e)] = base_row - eig_column
     gates = {
         HALO: jnp.where(place[0] > 0, 1.0, 0.0),
-        2 * STRIP - HALO: jnp.where(place[0] < place[2] - 1, 1.0, 0.0),
+        2 * STRIP - HALO: jnp.where(place[0] < X * Z - 1, 1.0, 0.0),
     }
     relaxed([range(STRIP), range(STRIP, 2 * STRIP)], x, quarter, shifted, xb, kin, stiff,
             lambda e: factor[tile(e)], index, gates)
@@ -216,7 +219,15 @@
     copies[2].start()
     own_orb = jnp.concatenate([orb[0:edge], orb[last - edge :]], 0)
     own_x = jnp.concatenate([low_cells, high_cells], 0)
-    projected_out[...] = projected_mid[...] + projection(own_orb, own_x, group[...], restrict_t[...])
+    lane = lax.broadcasted_iota(jnp.int32, (1, LANES), 1)
+    ghost_ids = jnp.zeros((1, LANES), F32)
+    for i, row in enumerate((left[META_AT + HALO - 1 : META_AT + HALO], right[META_AT : META_AT + 1])):
+        ghost_ids = jnp.where(lane == GHOST_IDS + 2 * i, row[:, OWNER], ghost_ids)
+        ghost_ids = jnp.where(lane == GHOST_IDS + 2 * i + 1, row[:, SLOT], ghost_ids)
+    added = projection(own_orb, own_x, group[...], restrict_t[...])
+    whole = projected_mid[...] + ghost_ids * (1.0 / COPIES) - step_rate * added
+    for i in range(X):
+        projected_out[i * HALF : (i + 1) * HALF] = whole
     ghosts = jnp.concatenate([left[ORB_AT : ORB_AT + WIDTH], right[ORB_AT : ORB_AT + WIDTH]], 0)
     ob[...] = ghosts.astype(BF16)
     ghost_kin = dot(ob[...], stiff[...])
@@ -232,41 +243,44 @@
         copy.wait()
 
 
-def sum_kernel(place, owner, slot, gathered, left, right, unpack, out, asked):
-    sources = gathered.shape[0] // WIDTH
-    own = lax.broadcasted_iota(jnp.int32, (HALF, LANES), 0) + place[0] * HALF
-    asked[0:HALF] = own.astype(F32)
-    for c in range(CELLS):
-        asked[HALF + c : HALF + c + 1] = jnp.full((1, LANES), (owner[c] * HALF + slot[c]).astype(F32), F32)
-    asked[HALF + CELLS : HALF + CELLS + 1] = left[META_AT + HALO - 1 : META_AT + HALO, 256:384]
-    asked[HALF + CELLS + 1 : HALF + CELLS + 2] = right[META_AT : META_AT + 1, 256:384]
-    asked[HALF + CELLS + 2 :] = jnp.full((LANES - HALF - CELLS - 2, LANES), -2.0, F32)
-    values = gathered[...]
-    high, rest = split(values)
-    ids = dot(high, unpack[...])
+def sum_kernel(place, gathered, asking, unpack, out):
+    high, rest = split(gathered[...])
+    ids = dot(jnp.concatenate([high, asking[...].astype(BF16)], 0), unpack[...])
     row = lax.broadcasted_iota(jnp.int32, ids.shape, 0) % WIDTH
     lane = lax.broadcasted_iota(jnp.int32, ids.shape, 1)
-    ids = jnp.where(lane // 6 == row, ids, 0.0)
-    ids = jnp.sum(ids.reshape(sources, WIDTH, LANES), axis=1)
+    ids = jnp.where(jnp.where(lane < CELLS, lane // 6, 0) == row, ids, 0.0)
+    ids = jnp.sum(ids.reshape(Z + X, WIDTH, LANES), axis=1)
     lane = lax.broadcasted_iota(jnp.int32, ids.shape, 1)
-    source = lax.broadcasted_iota(jnp.int32, ids.shape, 0)
-    known = (source * HALF + lane - CELLS).astype(F32)
-    ids = jnp.where(lane < CELLS, ids, jnp.where(lane < CELLS + HALF, known, -1.0))
-    wanted = asked[...]
-    total = jnp.zeros((2 * WIDTH, LANES), F32)
-    for s in range(0, sources, 2):
-        hot = [jnp.where(wanted == ids[i : i + 1], 1.0, 0.0).astype(BF16) for i in (s, s + 1)]
+    row = lax.broadcasted_iota(jnp.int32, ids.shape, 0)
+    dom = jnp.where(row < Z, place[1] * Z + row, (row - Z) * Z + place[2])
+    slots = (dom * HALF + lane - POT).astype(F32)
+    ids = jnp.where((lane >= POT) & (lane < IDS), slots, ids)
+    known = jnp.where(lane[:Z] < IDS, ids[:Z], -1.0)
+    wanted = jnp.where(lane[Z:] < IDS + 2, ids[Z:], -2.0)
+    known = jnp.transpose(jnp.concatenate([known, jnp.zeros((LANES - Z, LANES), F32)], 0))
+    total = jnp.zeros((2 * WIDTH, X * LANES), F32)
+    for s in range(0, Z, 2):
+        hot = [
+            jnp.concatenate(
+                [jnp.where(known[:, i : i + 1] == wanted[m : m + 1], 1.0, 0.0).astype(BF16) for m in range(X)], 1
+            )
+            for i in (s, s + 1)
+        ]
         both = [jnp.concatenate([high[tile(i)], rest[tile(i)]], 0) for i in (s, s + 1)]
-        total = total + dot(jnp.concatenate(both, 1), jnp.concatenate(hot, 1), NT)
+        total = total + dot(jnp.concatenate(both, 1), jnp.concatenate(hot, 0))
     result = total[:WIDTH] + total[WIDTH:]
-    for r in range(out.shape[0] // WIDTH):
-        out[tile(r)] = result
+    for m in range(X):
+        for i in range(COPIES):
+            out[tile(m * COPIES + i)] = result[:, cols(m)]
 
 
 def apply_kernel(place, columns, orb, linear, ghost, left, right, index, prolong, updated_out, applied_out):
-    table = jnp.transpose(columns[...])
-    updated_out[...] = table[0:HALF]
-    high, rest = split(table[HALF:])
+    summed = columns[0:HALF]
+    for i in range(1, X):
+        summed = summed + columns[i * HALF : (i + 1) * HALF]
+    table = jnp.transpose(summed)
+    updated_out[...] = table[POT:IDS]
+    high, rest = split(table)
     node = dot(high, prolong[...]) + dot(rest, prolong[...])
     low = lane_below(HALF)
     part_before = new_before = index_before = None
@@ -274,12 +288,12 @@
     for e in range(CELLS + 2):
         c = e - 1
         if e == 0:
-            values, start, node_at = left[ORB_AT : ORB_AT + WIDTH], ghost[tile(0)], CELLS
+            values, start, node_at = left[ORB_AT : ORB_AT + WIDTH], ghost[tile(0)], IDS
         elif e <= CELLS:
             values = orb[c // 2 * 16 : c // 2 * 16 + 16].astype(F32)[tile(c % 2)]
             start, node_at = linear[tile(c)], c
         else:
-            values, start, node_at = right[ORB_AT : ORB_AT + WIDTH], ghost[tile(1)], CELLS + 1
+            values, start, node_at = right[ORB_AT : ORB_AT + WIDTH], ghost[tile(1)], IDS + 1
         whole = start + node[node_at : node_at + 1] * values
         parts = [whole[:, cols(t)] for t in range(4)]
         if e > 0:
@@ -288,7 +302,7 @@
             if e == 1:
                 moved = moved * jnp.where(place[0] > 0, 1.0, 0.0)
             if e == CELLS + 1:
-                moved = moved * jnp.where(place[0] < place[2] - 1, 1.0, 0.0)
+                moved = moved * jnp.where(place[0] < X * Z - 1, 1.0, 0.0)
             done = jnp.where(low, new_before[3], new_before[3] + moved)
             if e > 1:
                 finished.append(jnp.concatenate([*new_before[:3], done], 1))
@@ -311,6 +325,9 @@
     for k in range(CELLS):
         table[112 + k % 6, k] = 64.0
         table[118 + k % 6, k] = 1.0
+    for i in range(2):
+        table[GHOST_IDS + 2 * i, IDS + i] = 64.0
+        table[GHOST_IDS + 2 * i + 1, IDS + i] = 1.0
     return table
 
 
@@ -323,8 +340,7 @@
 
 def local(orbitals, adjoint_source, eigenvalues, cell_scale, base_potential, stiffness, face_perm, restrict,
           prolong, owner, pot_slot, potential):
-    n_dom, n_orb = lax.axis_size("dom"), lax.axis_size("orb")
-    dom, orb_at = lax.axis_index("dom"), lax.axis_index("orb")
+    x_at, z_at = lax.axis_index("x"), lax.axis_index("z")
     vmem = pl.BlockSpec(memory_space=pltpu.VMEM)
     smem = pl.BlockSpec(memory_space=pltpu.SMEM)
     params = pltpu.CompilerParams(vmem_limit_bytes=32 * 2**20)
@@ -333,7 +349,7 @@
     orb2 = orbitals.reshape(CELLS * WIDTH, NODES)
     src2 = adjoint_source.reshape(CELLS * WIDTH, NODES)
     owner1 = owner.reshape(CELLS)
-    place = jnp.stack([dom, orb_at, jnp.int32(n_dom)])
+    place = jnp.stack([x_at * Z + z_at, x_at, z_at])
 
     hbm = pl.BlockSpec(memory_space=pltpu.HBM)
     to_left, to_right = pl.pallas_call(
@@ -354,9 +370,9 @@
         compiler_params=params,
     )(*map(in_hbm, (cell_scale, owner1, pot_slot, src2, orb2, base_potential, face_perm)))
 
-    ahead = [(i, i + 1) for i in range(n_dom - 1)]
-    left = lax.ppermute(to_right, "dom", ahead)
-    right = lax.ppermute(to_left, "dom", [(b, a) for a, b in ahead])
+    ahead = [(i, i + 1) for i in range(X * Z - 1)]
+    left = lax.ppermute(to_right, DOM, ahead)
+    right = lax.ppermute(to_left, DOM, [(b, a) for a, b in ahead])
 
     eig = eigenvalues[:, None]
     restrict_t = restrict.T
@@ -372,20 +388,18 @@
             pltpu.VMEM((n, NODES), F32),
         ]
 
-    adjoint_mid, projected_mid, linear, index, static = pl.pallas_call(
+    adjoint_mid, projected_mid, linear, index = pl.pallas_call(
         interior_kernel,
         out_shape=(
             struct((inner, NODES), BF16),
             struct((HALF, LANES), F32),
             struct((rows, NODES), F32),
             struct((rows, LANES), jnp.int32),
-            struct((WIDTH, LANES), F32),
         ),
         in_specs=[smem] * 4 + [vmem] * 5 + [hbm] * 4,
-        out_specs=(vmem,) * 5,
+        out_specs=(vmem,) * 4,
         scratch_shapes=scratch(rows)
         + [
-            pltpu.VMEM((HALF, HALF), F32),
             pltpu.VMEM((NODES, NODES), BF16),
             pltpu.VMEM((HALF, NODES), BF16),
             pltpu.VMEM((LANES, inner), BF16),
@@ -404,7 +418,7 @@
         boundary_kernel,
         out_shape=(
             struct((rows, NODES), BF16),
-            struct((HALF, LANES), F32),
+            struct((X * HALF, LANES), F32),
             struct((2 * WIDTH, NODES), F32),
         ),
         in_specs=[smem] * 2 + [vmem] * 12,
@@ -421,44 +435,46 @@
     )(place, cell_scale, src2, orb2, base_potential, index, left, right, eig, stiffness, restrict_t,
       jnp.asarray(group_table(edge_cells), BF16), adjoint_mid, projected_mid)
 
-    mine = lax.all_to_all(projected.reshape(n_orb, WIDTH, LANES), "orb", split_axis=0, concat_axis=0, tiled=True)
-    payload = static - step_rate * jnp.sum(mine, axis=0)
-    gathered = lax.all_to_all(
-        jnp.broadcast_to(payload[None], (n_dom, WIDTH, LANES)), "dom", split_axis=0, concat_axis=0, tiled=True
-    )
+    def exchanged(array, axes):
+        return lax.all_to_all(array, axes, split_axis=0, concat_axis=0, tiled=True)
+
+    tiles = exchanged(projected.reshape(X * COPIES, WIDTH, LANES), OUTER)
+    tiles = jnp.sum(tiles.reshape(X, COPIES, WIDTH, LANES), axis=1)
+    mine = lax.dynamic_slice(tiles, (x_at, 0, 0), (1, WIDTH, LANES), allow_negative_indices=False)
+    gathered = exchanged(jnp.broadcast_to(mine, (Z, WIDTH, LANES)), ("z",))
     columns = pl.pallas_call(
         sum_kernel,
-        out_shape=struct((n_orb * WIDTH, LANES), F32),
-        in_specs=[smem] * 3 + [vmem] * 4,
+        out_shape=struct((X * HALF, LANES), F32),
+        in_specs=[smem] + [vmem] * 3,
         out_specs=vmem,
-        scratch_shapes=[pltpu.VMEM((LANES, LANES), F32)],
         compiler_params=params,
-    )(place, owner1, pot_slot, gathered.reshape(n_dom * WIDTH, LANES), left, right, jnp.asarray(unpack_table(), BF16))
-    columns = lax.all_to_all(columns.reshape(n_orb, WIDTH, LANES), "orb", split_axis=0, concat_axis=0, tiled=True)
+    )(place, gathered.reshape(Z * WIDTH, LANES), tiles.reshape(X * WIDTH, LANES), jnp.asarray(unpack_table(), BF16))
+    columns = exchanged(columns.reshape(X * COPIES, WIDTH, LANES), OUTER)
     updated, applied2 = pl.pallas_call(
         apply_kernel,
         out_shape=(struct((HALF, HALF), F32), struct((rows, NODES), BF16)),
         in_specs=[smem] + [vmem] * 8,
         out_specs=(vmem, vmem),
         compiler_params=params,
-    )(place, columns.reshape(n_orb * WIDTH, LANES), orb2, linear, ghost, left, right, index, prolong)
+    )(place, columns.reshape(X * HALF, LANES), orb2, linear, ghost, left, right, index, prolong)
     return adjoint2.reshape(orbitals.shape), updated, applied2.reshape(orbitals.shape)
 
 
 def solution(mesh):
+    axes = jax.sharding.Mesh(mesh.devices.reshape(X, Z, Y, CORES), ("x", "z", "y", "core"))
     in_specs = (
-        P("dom", "orb", None),
-        P("dom", "orb", None),
-        P("orb"),
-        P("dom"),
-        P("dom", None),
+        P(DOM, ORB, None),
+        P(DOM, ORB, None),
+        P(ORB),
+        P(DOM),
+        P(DOM, None),
         P(),
-        P("dom", None),
+        P(DOM, None),
         P(),
         P(),
-        P("dom", None),
-        P("dom"),
-        P("dom", None),
+        P(DOM, None),
+        P(DOM),
+        P(DOM, None),
     )
-    out_specs = (P("dom", "orb", None), P("dom", None), P("dom", "orb", None))
-    return jax.shard_map(local, mesh=mesh, in_specs=in_specs, out_specs=out_specs, check_vma=False)
+    out_specs = (P(DOM, ORB, None), P(DOM, None), P(DOM, ORB, None))
+    return jax.shard_map(local, mesh=axes, in_specs=in_specs, out_specs=out_specs, check_vma=False)

time: 78.7 us -> 77.7 us (0.987)
  blocking collectives: 59.2 us -> 56.8 us
    all_to_all x3, blocking collectives: 59.2 us -> 56.8 us  [exchanged(): return lax.all_to_all(array, axes, split_axis=0, concat_axis=0, tiled=True)]
  transfers between devices with their start and end apart: 2 -> 2, of which waited for: 0 -> 0; matrix products, arithmetic and copies ran while one was open for 0% -> 0% of each run, Pallas kernels for 6% -> 7%
where the time goes in v4:
time: 77.7 us; the launch traced here: 77.3 us
  blocking collectives  56.8 us (73%)
  Pallas kernels  12.5 us (16%)
  starting transfers between devices  5.67 us (7%)
  local copies, waits for them, and re-layouts  1.45 us (2%)
  between operations  0.83 us (1%)
    all_to_all x3, blocking collectives, exchanged(): return lax.all_to_all(array, axes, split_axis=0, concat_axis=0, tiled=True)  56.8 us
    pallas_call x1, Pallas kernels, local(): pl.pallas_call(interior_kernel, out_shape=(struct((inner, NODES), BF16),...  5.08 us
    ppermute x1, starting transfers between devices, local(): left = lax.ppermute(to_right, DOM, ahead)  4.38 us
    pallas_call x1, Pallas kernels, local(): pl.pallas_call(boundary_kernel, out_shape=(struct((rows, NODES), BF16), s...  2.98 us
    pallas_call x1, Pallas kernels, local(): pl.pallas_call(apply_kernel, out_shape=(struct((HALF, HALF), F32), struct...  1.79 us
  transfers between devices with their start and end apart: 2, of which 0 were waited for; matrix products, arithmetic and copies ran while one was open for 0% of the time, Pallas kernels for 7%

profile of v4, /device:TPU:1, one launch (start us, length us, event | category | flops | bytes accessed | tf_op | source)
XLA Modules:
  0.0 77.3 jit_solution(5103412913703140648)
XLA Ops:
  0.6 0.0 copy-start
  0.7 1.3 %shard_map.167 = (f32[48,512]{1,0:T(8,128)S(1)}, f32[48,512]{1,0:T(8,128)S(1)}) custom-call(f32[48]{0:T(128)} %scale.3, s32[48]{0:T(128)} %bitcast.33, s32[48]{0:T(128)} %slot_hbm.1, bf16[384,512]{1,0:T(8,128)(2,1)} %bitcast.23, bf16[384,512]{1,0:T(8,128)(2,1)} %bitcast.19, f32[48,512]{1,0:T(8,128)} %base.3, s32[48,64]{1,0:T(8,128)} %perm_hbm.1), custom_call_target="tpu_custom_call" | custom-call | tf_op jit(solution)/shard_map/pallas_call | solution.py:355
  2.0 0.0 copy-start.8
  2.0 4.4 %collective-permute-start = (f32[48,512]{1,0:T(8,128)S(1)}, f32[48,512]{1,0:T(8,128)S(1)}, u32[]{:S(2)}, u32[]{:S(2)}) collective-permute-start(f32[48,512]{1,0:T(8,128)S(1)} %get-tuple-element.15), channel_id=1, source_target_pairs={{0,8},{8,16},{16,24},{24,32},{32,40},{40,48},{48,56},{56,64},{64,7... | collective-permute-start | bytes 294920 | tf_op jit(solution)/shard_map/ppermute | solution.py:374
  6.4 1.3 %collective-permute-start.1 = (f32[48,512]{1,0:T(8,128)S(1)}, f32[48,512]{1,0:T(8,128)S(1)}, u32[]{:S(2)}, u32[]{:S(2)}) collective-permute-start(f32[48,512]{1,0:T(8,128)S(1)} %get-tuple-element.16), channel_id=1, source_target_pairs={{8,0},{16,8},{24,16},{32,24},{40,32},{48,40},{56,48},{64,56},{72,6... | collective-permute-start | bytes 294920 | tf_op jit(solution)/shard_map/ppermute | solution.py:375
  7.7 0.1 pad_add_fusion.place
  7.7 0.7 copy-done.12
  8.4 0.1 copy.18.eig
  8.5 0.0 copy-done
  8.5 0.6 copy-done.9
  9.1 0.0 copy-done.10
  9.2 0.0 copy-done.11
  9.2 5.1 %shard_map.166 = (bf16[320,512]{1,0:T(8,128)(2,1)S(1)}, f32[64,128]{1,0:T(8,128)S(1)}, f32[384,512]{1,0:T(8,128)S(1)}, s32[384,128]{1,0:T(8,128)S(1)}) custom-call(s32[3]{0:T(128)S(1)} %pad_add_fusion.place, f32[48]{0:T(128)S(1)} %copy-done.9, s32[48]{0:T(128)S(1)} %bitcast.34, s32[48]{0:T(128)S(1)} %copy-done.11, bf16[384,512]{1,0:T(8,128)(2,1)S(1)} %bitcast.24, ...), custom_call_target="tpu_custom_call" | custom-call | flops 1006632960 | bytes 4194304 | tf_op jit(solution)/shard_map/pallas_call | solution.py:391
  14.3 0.0 collective-permute-done.left
  14.3 0.0 collective-permute-done.1.right
  14.3 3.0 %shard_map.168 = (bf16[384,512]{1,0:T(8,128)(2,1)}, f32[256,128]{1,0:T(8,128)S(1)}, f32[16,512]{1,0:T(8,128)S(1)}) custom-call(s32[3]{0:T(128)S(1)} %pad_add_fusion.place, f32[48]{0:T(128)S(1)} %copy-done.9, bf16[384,512]{1,0:T(8,128)(2,1)S(1)} %bitcast.25, bf16[384,512]{1,0:T(8,128)(2,1)S(1)} %bitcast.21, f32[48,512]{1,0:T(8,128)S(1)} %copy-done.3, ...), custom_call_target="tpu_custom_call" | custom-call | tf_op jit(solution)/shard_map/pallas_call | solution.py:417
  17.3 23.7 %all_to_all.15 = f32[32,8,128]{2,1,0:T(8,128)S(1)} all-to-all(f32[32,8,128]{2,1,0:T(8,128)S(1)} %bitcast.29), channel_id=1, replica_groups=mesh['x'=4,'z'=16,'y'=4,'core'=2] {'x','y','core'}, dimensions={0} | all-to-all | bytes 262144 | tf_op jit(solution)/shard_map/all_to_all | solution.py:439
  41.1 0.0 copy-start.7
  41.1 20.0 %all_to_all.16 = f32[16,8,128]{2,1,0:T(8,128)S(1)} all-to-all(f32[16,8,128]{2,1,0:T(8,128)S(1)} %broadcast_in_dim.12), channel_id=1, replica_groups=mesh['x'=4,'z'=16,'y'=4,'core'=2] {'z'}, dimensions={0} | all-to-all | bytes 131072 | tf_op jit(solution)/shard_map/all_to_all | solution.py:439
  61.2 1.3 %shard_map.169 = f32[256,128]{1,0:T(8,128)S(1)} custom-call(s32[3]{0:T(128)S(1)} %pad_add_fusion.place, f32[128,128]{1,0:T(8,128)S(1)} %bitcast.28, f32[32,128]{1,0:T(8,128)S(1)} %bitcast.30, bf16[128,128]{1,0:T(8,128)(2,1)S(1)} %copy-done.7), custom_call_target="tpu_custom_call" | custom-call | tf_op jit(solution)/shard_map/pallas_call | solution.py:445
  62.5 0.0 copy-start.5
  62.5 13.0 %all_to_all.17 = f32[32,8,128]{2,1,0:T(8,128)S(1)} all-to-all(f32[32,8,128]{2,1,0:T(8,128)S(1)} %bitcast.26), channel_id=1, replica_groups=mesh['x'=4,'z'=16,'y'=4,'core'=2] {'x','y','core'}, dimensions={0} | all-to-all | bytes 262144 | tf_op jit(solution)/shard_map/all_to_all | solution.py:439
  75.5 0.0 copy-done.5
  75.5 1.8 %shard_map.170 = (f32[64,64]{1,0:T(8,128)}, bf16[384,512]{1,0:T(8,128)(2,1)}) custom-call(s32[3]{0:T(128)S(1)} %pad_add_fusion.place, f32[256,128]{1,0:T(8,128)S(1)} %bitcast.27, bf16[384,512]{1,0:T(8,128)(2,1)S(1)} %bitcast.22, f32[384,512]{1,0:T(8,128)S(1)} %get-tuple-element.21.linear, f32[16,512]{1,0:T(8,128)S(1)} %get-tuple-element.22.ghost, ...), custom_call_target="tpu_custom_call" | custom-call | tf_op jit(solution)/shard_map/pallas_call | solution.py:453
  (19 shorter events, 0.1 us)
Async XLA Ops:
  0.6 7.9 %copy-start = (bf16[48,8,512]{2,1,0:T(8,128)(2,1)S(1)}, bf16[48,8,512]{2,1,0:T(8,128)(2,1)}, u32[]{:S(2)}) copy-start(bf16[48,8,512]{2,1,0:T(8,128)(2,1)} %param.15) | copy-start | bytes 1179652
  0.6 7.9 %copy-start.1 = (bf16[48,8,512]{2,1,0:T(8,128)(2,1)S(1)}, bf16[48,8,512]{2,1,0:T(8,128)(2,1)}, u32[]{:S(2)}) copy-start(bf16[48,8,512]{2,1,0:T(8,128)(2,1)} %param.16) | copy-start | bytes 1179652
  0.7 7.9 %copy-start.3 = (f32[48,512]{1,0:T(8,128)S(1)}, f32[48,512]{1,0:T(8,128)}, u32[]{:S(2)}) copy-start(f32[48,512]{1,0:T(8,128)} %base.3) | copy-start | bytes 294916
  2.0 6.6 %copy-start.8 = (s32[48,64]{1,0:T(8,128)S(1)}, s32[48,64]{1,0:T(8,128)}, u32[]{:S(2)}) copy-start(s32[48,64]{1,0:T(8,128)} %perm_hbm.1) | copy-start | bytes 36868
  2.0 12.3 %collective-permute-start = (f32[48,512]{1,0:T(8,128)S(1)}, f32[48,512]{1,0:T(8,128)S(1)}, u32[]{:S(2)}, u32[]{:S(2)}) collective-permute-start(f32[48,512]{1,0:T(8,128)S(1)} %get-tuple-element.15), channel_id=1, source_target_pairs={{0,8},{8,16},{16,24},{24,32},{32,40},{40,48},{48,56},{56,64},{64,7... | collective-permute-start | bytes 294920 | tf_op jit(solution)/shard_map/ppermute | solution.py:374
  6.4 7.9 %collective-permute-start.1 = (f32[48,512]{1,0:T(8,128)S(1)}, f32[48,512]{1,0:T(8,128)S(1)}, u32[]{:S(2)}, u32[]{:S(2)}) collective-permute-start(f32[48,512]{1,0:T(8,128)S(1)} %get-tuple-element.16), channel_id=1, source_target_pairs={{8,0},{16,8},{24,16},{32,24},{40,32},{48,40},{56,48},{64,56},{72,6... | collective-permute-start | bytes 294920 | tf_op jit(solution)/shard_map/ppermute | solution.py:375
  7.7 0.7 copy-start.12
  8.5 0.7 copy-start.9
  8.5 0.7 copy-start.10
  8.5 0.7 copy-start.11
  9.2 5.1 %copy-start.2 = (bf16[512,512]{1,0:T(8,128)(2,1)S(1)}, bf16[512,512]{1,0:T(8,128)(2,1)}, u32[]{:S(2)}) copy-start(bf16[512,512]{1,0:T(8,128)(2,1)} %stiff.1) | copy-start | bytes 1572868
  9.2 5.1 %copy-start.4 = (bf16[512,64]{0,1:T(8,128)(2,1)S(1)}, bf16[512,64]{0,1:T(8,128)(2,1)}, u32[]{:S(2)}) copy-start(bf16[512,64]{0,1:T(8,128)(2,1)} %param.22) | copy-start | bytes 196612
  9.2 5.1 %copy-start.6 = (bf16[128,64]{1,0:T(8,128)(2,1)S(1)}, bf16[128,64]{1,0:T(8,128)(2,1)}, u32[]{:S(2)}) copy-start(bf16[128,64]{1,0:T(8,128)(2,1)} %constant.24.clone.group) | copy-start | bytes 49156
  41.1 20.1 %copy-start.7 = (bf16[128,128]{1,0:T(8,128)(2,1)S(1)}, bf16[128,128]{1,0:T(8,128)(2,1)}, u32[]{:S(2)}) copy-start(bf16[128,128]{1,0:T(8,128)(2,1)} %constant.25.clone.unpack) | copy-start | bytes 98308
  62.5 13.0 %copy-start.5 = (bf16[64,512]{1,0:T(8,128)(2,1)S(1)}, bf16[64,512]{1,0:T(8,128)(2,1)}, u32[]{:S(2)}) copy-start(bf16[64,512]{1,0:T(8,128)(2,1)} %prolong.1) | copy-start | bytes 196612

commit v5 on v4

--- a/solution.py
+++ b/solution.py
@@ -64,12 +64,32 @@
     return rows
 
 
+def face_tiles(perm):
+    half = CELLS // 2
+    perm = perm.astype(F32)
+    pairs = jnp.concatenate([perm[:half], perm[half:]], 1)
+    twice = jnp.concatenate([perm, perm], 1)
+    node = lax.broadcasted_iota(jnp.int32, (HALF, LANES), 0).astype(F32)
+    row = lax.broadcasted_iota(jnp.int32, (WIDTH, LANES), 0)
+    lane = lax.broadcasted_iota(jnp.int32, (WIDTH, LANES), 1)
+    counts = jnp.where(lane // HALF == row, lane % HALF, 0).astype(F32).astype(BF16)
+    empty = jnp.zeros((HALF, LANES), BF16)
+    tiles = [None] * CELLS
+    for p in range(half):
+        hot = jnp.where(pairs[p : p + 1] == node, 1.0, 0.0).astype(BF16)
+        inverse = dot(counts, jnp.concatenate([hot, empty], 0), NT)
+        for i, c in enumerate((p, p + half)):
+            rows = jnp.where(lane[:1] < HALF, inverse[i : i + 1] + HALF, twice[c : c + 1])
+            tiles[c] = jnp.broadcast_to(rows.astype(jnp.int32), (WIDTH, LANES))
+    return tiles
+
+
 def in_hbm(array):
     return pltpu.with_memory_space_constraint(array, pltpu.HBM)
 
 
-def pack_kernel(scale_hbm, owner_hbm, slot_hbm, src_hbm, orb_hbm, base_hbm, perm_hbm, to_left, to_right,
-                scale, owner, slot, src, orb, base, perm, sems):
+def pack_kernel(scale_hbm, owner_hbm, slot_hbm, src_hbm, orb_hbm, base_hbm, perm_hbm, stiff_hbm, eig_hbm,
+                to_left, to_right, factor_out, eig_out, stiff_out, scale, owner, slot, src, orb, base, perm, eig, sems):
     top, rows = CELLS - WIDTH, CELLS * WIDTH
     copies = [(scale_hbm, scale), (owner_hbm, owner), (slot_hbm, slot)]
     for hbm, here, size, end in (
@@ -77,11 +97,19 @@
     ):
         copies.append((hbm.at[0:size], here.at[0]))
         copies.append((hbm.at[end - size : end], here.at[1]))
+    copies += [(eig_hbm, eig), (stiff_hbm, stiff_out)]
     copies = [pltpu.make_async_copy(one, two, sems.at[i]) for i, (one, two) in enumerate(copies)]
     for copy in copies:
         copy.start()
-    for copy in copies:
+    for copy in copies[:-1]:
         copy.wait()
+    row = lax.broadcasted_iota(jnp.int32, (WIDTH, LANES), 0)
+    eig_tile = jnp.zeros((WIDTH, LANES), F32)
+    for i in range(WIDTH):
+        eig_tile = jnp.where(row == i, eig[i], eig_tile)
+    eig_out[...] = eig_tile
+    for c in range(CELLS):
+        factor_out[c : c + 1] = jnp.full((1, LANES), scale[c], F32)
     for end, out in enumerate((to_left, to_right)):
         inner, first = (0, 0) if end == 0 else (HALO, CELLS - HALO)
         edge_cell = end * (CELLS - 1)
@@ -94,41 +122,51 @@
             out[at, IDX] = faces[i]
             out[at, SCALE] = jnp.full((1, LANES), scale[first + i], F32)
             out[at, OWNER] = jnp.full((1, LANES), owner[edge_cell].astype(F32), F32)
-            out[at, SLOT] = jnp.full((1, LANES), slot[edge_cell].astype(F32), F32)
-
-
-def relaxed(strips, x, quarter, shifted, xb, kin, stiff, factor, index, gates):
+            mark = slot[edge_cell].astype(F32) if i == end * (HALO - 1) else 1.0
+            out[at, SLOT] = jnp.full((1, LANES), mark, F32)
+    copies[-1].wait()
+
+
+def relax_step(strips, x, quarter, shifted, kin, stiff, factor, index, gates):
     low = lane_below(HALF)
-    cells = strips[-1][-1] + 1
-
-    def step(_, carry):
-        xb[...] = x[...].astype(BF16)
-        kin[...] = dot(xb[...], stiff[...])
-        for strip in strips:
-            part_before = new_before = None
-            for e in strip:
-                rows = tile(e)
-                scale = factor(e)
-                parts, news = [], []
-                for t in range(4):
-                    here = x[rows, cols(t)]
-                    part = scale * kin[rows, cols(t)] + shifted[rows, cols(t)] * here
-                    parts.append(part)
-                    news.append(here + quarter[rows, cols(t)] - relax * part)
-                if e > strip[0]:
-                    crossing = jnp.where(low, parts[0], part_before)
-                    moved = relax * jnp.take_along_axis(crossing, index[tile(e - 1)], axis=1, mode="promise_in_bounds")
-                    if e in gates:
-                        moved = moved * gates[e]
-                    news[0] = jnp.where(low, news[0] - moved, news[0])
-                    x[tile(e - 1), cols(3)] = jnp.where(low, new_before, new_before - moved)
-                for t in range(3):
-                    x[rows, cols(t)] = news[t]
-                part_before, new_before = parts[3], news[3]
-            x[tile(strip[-1]), cols(3)] = new_before
-        return carry
-
-    lax.fori_loop(0, ITERS, step, 0)
+    held = [x[strip[0] * WIDTH : (strip[-1] + 1) * WIDTH].astype(BF16) for strip in strips]
+    held = held[0] if len(held) == 1 else jnp.concatenate(held, 0)
+    kin[0 : held.shape[0]] = dot(held, stiff[...])
+    at = 0
+    for strip in strips:
+        part_before = new_before = None
+        for e in strip:
+            rows = tile(e)
+            scale = factor(e)
+            parts, news = [], []
+            for t in range(4):
+                here = x[rows, cols(t)]
+                part = scale * kin[tile(at), cols(t)] + shifted[rows, cols(t)] * here
+                parts.append(part)
+                news.append(here + quarter[rows, cols(t)] - relax * part)
+            at += 1
+            if e > strip[0]:
+                crossing = jnp.where(low, parts[0], part_before)
+                moved = relax * jnp.take_along_axis(crossing, index[tile(e - 1)], axis=1, mode="promise_in_bounds")
+                if e in gates:
+                    moved = moved * gates[e]
+                news[0] = jnp.where(low, news[0] - moved, news[0])
+                x[tile(e - 1), cols(3)] = jnp.where(low, new_before, new_before - moved)
+            for t in range(3):
+                x[rows, cols(t)] = news[t]
+            part_before, new_before = parts[3], news[3]
+        x[tile(strip[-1]), cols(3)] = new_before
+
+
+def group_of(row_cells):
+    shape = (LANES, len(row_cells) * WIDTH)
+    cell = lax.broadcasted_iota(jnp.int32, shape, 0)
+    at = lax.broadcasted_iota(jnp.int32, shape, 1) // WIDTH
+    gap = [i for i in range(1, len(row_cells)) if row_cells[i] != row_cells[i - 1] + 1]
+    owner = at + row_cells[0]
+    for i in gap:
+        owner = owner + jnp.where(at >= i, row_cells[i] - row_cells[i - 1] - 1, 0)
+    return jnp.where(cell == owner, 1.0, 0.0).astype(BF16)
 
 
 def projection(orb_values, x_values, group, restrict_t):
@@ -138,30 +176,43 @@
     return dot(restrict_t, high, NT) + dot(restrict_t, rest, NT)
 
 
-def interior_kernel(place, scale, owner, slot, src, orb, base, perm, eig, stiff_hbm, restrict_hbm, group_hbm,
-                    potential_hbm, adjoint_out, projected_out, linear_out, index_out,
-                    x, quarter, xb, kin, shifted, stiff, restrict_t, group, potential, sems):
-    pairs = ((stiff_hbm, stiff), (restrict_hbm, restrict_t), (group_hbm, group), (potential_hbm, potential))
+def interior_kernel(owner_hbm, slot_hbm, restrict_hbm, potential_hbm, src, orb, base, perm, factor, eig, stiff,
+                    adjoint_out, projected_out, linear_out, index_out, restrict_t,
+                    x, quarter, kin, shifted, owner, slot, potential, sems):
+    pairs = ((restrict_hbm, restrict_t), (potential_hbm, potential), (owner_hbm, owner), (slot_hbm, slot))
     copies = [pltpu.make_async_copy(one, two, sems.at[i]) for i, (one, two) in enumerate(pairs)]
     for copy in copies:
         copy.start()
     quarter[...] = relax * src[...].astype(F32)
     x[...] = quarter[...]
-    eig_column = eig[...]
-    faces = face_rows(perm[...], range(CELLS))
+    faces = face_tiles(perm[...])
+    eig_tile = eig[...]
+
+    def scale(c):
+        return jnp.broadcast_to(factor[c : c + 1], (WIDTH, LANES))
+
     for c in range(CELLS):
-        shifted[tile(c)] = base[c : c + 1] - eig_column
-        index_out[tile(c)] = jnp.broadcast_to(faces[c].astype(jnp.int32), (WIDTH, LANES))
+        for t in range(4):
+            shifted[tile(c), cols(t)] = base[c : c + 1, cols(t)] - eig_tile
+        index_out[tile(c)] = faces[c]
+
+    def step(_, carry):
+        relax_step([range(CELLS)], x, quarter, shifted, kin, stiff, scale, index_out, {})
+        return carry
+
+    lax.fori_loop(0, ITERS, step, 0)
     for copy in copies:
         copy.wait()
-    relaxed([range(CELLS)], x, quarter, shifted, xb, kin, stiff, lambda c: scale[c], index_out, {})
     inner = slice(HALO * WIDTH, (CELLS - HALO) * WIDTH)
     adjoint_out[...] = x[inner].astype(BF16)
     kin[...] = dot(orb[...], stiff[...])
     for pair in range(CELLS // 2):
         values = orb[pair * 16 : pair * 16 + 16].astype(F32)
         for c in (2 * pair, 2 * pair + 1):
-            linear_out[tile(c)] = scale[c] * kin[tile(c)] + base[c : c + 1] * values[tile(c % 2)]
+            for t in range(4):
+                linear_out[tile(c), cols(t)] = (
+                    scale(c) * kin[tile(c), cols(t)] + base[c : c + 1, cols(t)] * values[tile(c % 2), cols(t)]
+                )
     row = lax.broadcasted_iota(jnp.int32, (WIDTH, LANES), 0)
     lane = lax.broadcasted_iota(jnp.int32, (WIDTH, LANES), 1)
     at = jnp.where((lane >= IDS) & (lane < GHOST_IDS), row * 12 + lane - IDS, -1)
@@ -172,12 +223,14 @@
     turned = jnp.transpose(potential[...])
     static = jnp.concatenate([jnp.zeros((HALF, CELLS), F32), turned, jnp.zeros((HALF, 16), F32)], 1)
     static = (static + jnp.concatenate([ids] * (HALF // WIDTH), 0)) * (1.0 / COPIES)
-    projected_out[...] = static - step_rate * projection(orb[inner], x[inner], group[...], restrict_t[...])
-
-
-def boundary_kernel(place, scale, src, orb, base, index_own, left, right, eig, stiff, restrict_t, group, adjoint_mid,
-                    projected_mid, adjoint_out, projected_out, ghost_out,
-                    x, quarter, xb, kin, shifted, factor, index, ob, adjoint_ends, sems):
+    projected_out[...] = static - step_rate * projection(
+        orb[inner], x[inner], group_of(range(HALO, CELLS - HALO)), restrict_t[...]
+    )
+
+
+def boundary_kernel(src, orb, base, index_own, factor_own, eig, left, right, stiff, restrict_t, adjoint_mid, projected_mid,
+                    adjoint_out, projected_out, ghost_out,
+                    x, quarter, kin, shifted, factor, index, adjoint_ends, sems):
     near, edge = 2 * HALO * WIDTH, HALO * WIDTH
     last = CELLS * WIDTH
     copies = [
@@ -191,13 +244,13 @@
     quarter[edge + near : edge + 2 * near] = relax * src[last - near :].astype(F32)
     quarter[edge + 2 * near :] = relax * right[0:SRC_ROWS]
     x[...] = quarter[...]
-    eig_column = eig[...]
+    eig_tile = eig[...]
     for e in range(2 * STRIP):
         ghost = left if e < HALO else right if e >= 2 * STRIP - HALO else None
         if ghost is None:
             c = e - HALO if e < STRIP else CELLS - 2 * HALO + e - STRIP
             base_row = base[c : c + 1]
-            factor[tile(e)] = jnp.full((WIDTH, LANES), scale[c], F32)
+            factor[tile(e)] = jnp.broadcast_to(factor_own[c : c + 1], (WIDTH, LANES))
             index[tile(e)] = index_own[tile(c)]
         else:
             i = e if e < HALO else e - 2 * STRIP + HALO
@@ -205,13 +258,12 @@
             meta_row = ghost[META_AT + i : META_AT + i + 1]
             factor[tile(e)] = jnp.broadcast_to(meta_row[:, SCALE], (WIDTH, LANES))
             index[tile(e)] = jnp.broadcast_to(meta_row[:, IDX].astype(jnp.int32), (WIDTH, LANES))
-        shifted[tile(e)] = base_row - eig_column
-    gates = {
-        HALO: jnp.where(place[0] > 0, 1.0, 0.0),
-        2 * STRIP - HALO: jnp.where(place[0] < X * Z - 1, 1.0, 0.0),
-    }
-    relaxed([range(STRIP), range(STRIP, 2 * STRIP)], x, quarter, shifted, xb, kin, stiff,
-            lambda e: factor[tile(e)], index, gates)
+        for t in range(4):
+            shifted[tile(e), cols(t)] = base_row[:, cols(t)] - eig_tile
+    gates = {HALO: left[META_AT : META_AT + 1, SLOT], 2 * STRIP - HALO: right[HALO_ROWS - 1 : HALO_ROWS, SLOT]}
+    for k in range(ITERS):
+        strips = [range(k, STRIP - k), range(STRIP + k, 2 * STRIP - k)]
+        relax_step(strips, x, quarter, shifted, kin, stiff, lambda e: factor[tile(e)], index, gates)
     low_cells, high_cells = x[edge : 2 * edge], x[4 * edge : 5 * edge]
     adjoint_ends[0] = low_cells.astype(BF16)
     adjoint_ends[1] = high_cells.astype(BF16)
@@ -224,13 +276,12 @@
     for i, row in enumerate((left[META_AT + HALO - 1 : META_AT + HALO], right[META_AT : META_AT + 1])):
         ghost_ids = jnp.where(lane == GHOST_IDS + 2 * i, row[:, OWNER], ghost_ids)
         ghost_ids = jnp.where(lane == GHOST_IDS + 2 * i + 1, row[:, SLOT], ghost_ids)
-    added = projection(own_orb, own_x, group[...], restrict_t[...])
+    added = projection(own_orb, own_x, group_of([*range(HALO), *range(CELLS - HALO, CELLS)]), restrict_t[...])
     whole = projected_mid[...] + ghost_ids * (1.0 / COPIES) - step_rate * added
     for i in range(X):
         projected_out[i * HALF : (i + 1) * HALF] = whole
     ghosts = jnp.concatenate([left[ORB_AT : ORB_AT + WIDTH], right[ORB_AT : ORB_AT + WIDTH]], 0)
-    ob[...] = ghosts.astype(BF16)
-    ghost_kin = dot(ob[...], stiff[...])
+    ghost_kin = dot(ghosts.astype(BF16), stiff[...])
     for i, e, base_row in (
         (0, HALO - 1, left[BASE_AT + HALO - 1 : BASE_AT + HALO]),
         (1, 2 * STRIP - HALO, right[BASE_AT : BASE_AT + 1]),
@@ -252,8 +303,8 @@
     ids = jnp.sum(ids.reshape(Z + X, WIDTH, LANES), axis=1)
     lane = lax.broadcasted_iota(jnp.int32, ids.shape, 1)
     row = lax.broadcasted_iota(jnp.int32, ids.shape, 0)
-    dom = jnp.where(row < Z, place[1] * Z + row, (row - Z) * Z + place[2])
-    slots = (dom * HALF + lane - POT).astype(F32)
+    mine = jnp.where(row < Z, place[0:1], place[1:2])
+    slots = mine + (jnp.where(row < Z, row, (row - Z) * Z) * HALF + lane - POT).astype(F32)
     ids = jnp.where((lane >= POT) & (lane < IDS), slots, ids)
     known = jnp.where(lane[:Z] < IDS, ids[:Z], -1.0)
     wanted = jnp.where(lane[Z:] < IDS + 2, ids[Z:], -2.0)
@@ -274,7 +325,7 @@
             out[tile(m * COPIES + i)] = result[:, cols(m)]
 
 
-def apply_kernel(place, columns, orb, linear, ghost, left, right, index, prolong, updated_out, applied_out):
+def apply_kernel(columns, orb, linear, ghost, left, right, index, prolong, updated_out, applied_out):
     summed = columns[0:HALF]
     for i in range(1, X):
         summed = summed + columns[i * HALF : (i + 1) * HALF]
@@ -300,9 +351,9 @@
             crossing = jnp.where(low, parts[0], part_before)
             moved = jnp.take_along_axis(crossing, index_before, axis=1, mode="promise_in_bounds")
             if e == 1:
-                moved = moved * jnp.where(place[0] > 0, 1.0, 0.0)
+                moved = moved * left[META_AT : META_AT + 1, SLOT]
             if e == CELLS + 1:
-                moved = moved * jnp.where(place[0] < X * Z - 1, 1.0, 0.0)
+                moved = moved * right[HALO_ROWS - 1 : HALO_ROWS, SLOT]
             done = jnp.where(low, new_before[3], new_before[3] + moved)
             if e > 1:
                 finished.append(jnp.concatenate([*new_before[:3], done], 1))
@@ -331,32 +382,31 @@
     return table
 
 
-def group_table(cells):
-    table = np.zeros((LANES, len(cells) * WIDTH), np.float32)
-    for at, cell in enumerate(cells):
-        table[cell, at * WIDTH : (at + 1) * WIDTH] = 1.0
-    return table
-
-
 def local(orbitals, adjoint_source, eigenvalues, cell_scale, base_potential, stiffness, face_perm, restrict,
           prolong, owner, pot_slot, potential):
     x_at, z_at = lax.axis_index("x"), lax.axis_index("z")
     vmem = pl.BlockSpec(memory_space=pltpu.VMEM)
-    smem = pl.BlockSpec(memory_space=pltpu.SMEM)
     params = pltpu.CompilerParams(vmem_limit_bytes=32 * 2**20)
     struct = jax.ShapeDtypeStruct
 
     orb2 = orbitals.reshape(CELLS * WIDTH, NODES)
     src2 = adjoint_source.reshape(CELLS * WIDTH, NODES)
     owner1 = owner.reshape(CELLS)
-    place = jnp.stack([x_at * Z + z_at, x_at, z_at])
+    first = jnp.stack([x_at * Z, z_at]) * HALF
+    place = jnp.broadcast_to(first.astype(F32)[:, None], (2, LANES))
 
     hbm = pl.BlockSpec(memory_space=pltpu.HBM)
-    to_left, to_right = pl.pallas_call(
+    to_left, to_right, factor, eig, stiff = pl.pallas_call(
         pack_kernel,
-        out_shape=(struct((HALO_ROWS, NODES), F32),) * 2,
-        in_specs=[hbm] * 7,
-        out_specs=(vmem, vmem),
+        out_shape=(
+            struct((HALO_ROWS, NODES), F32),
+            struct((HALO_ROWS, NODES), F32),
+            struct((CELLS, LANES), F32),
+            struct((WIDTH, LANES), F32),
+            struct((NODES, NODES), BF16),
+        ),
+        in_specs=[hbm] * 9,
+        out_specs=(vmem,) * 5,
         scratch_shapes=[
             pltpu.SMEM((CELLS,), F32),
             pltpu.SMEM((CELLS,), jnp.int32),
@@ -365,54 +415,40 @@
             pltpu.VMEM((2, 16, NODES), BF16),
             pltpu.VMEM((2, WIDTH, NODES), F32),
             pltpu.VMEM((2, WIDTH, HALF), jnp.int32),
-            pltpu.SemaphoreType.DMA((11,)),
+            pltpu.SMEM((WIDTH,), F32),
+            pltpu.SemaphoreType.DMA((13,)),
         ],
         compiler_params=params,
-    )(*map(in_hbm, (cell_scale, owner1, pot_slot, src2, orb2, base_potential, face_perm)))
+    )(*map(in_hbm, (cell_scale, owner1, pot_slot, src2, orb2, base_potential, face_perm, stiffness, eigenvalues)))
 
     ahead = [(i, i + 1) for i in range(X * Z - 1)]
     left = lax.ppermute(to_right, DOM, ahead)
     right = lax.ppermute(to_left, DOM, [(b, a) for a, b in ahead])
 
-    eig = eigenvalues[:, None]
-    restrict_t = restrict.T
     rows = CELLS * WIDTH
     inner = rows - 2 * HALO * WIDTH
-
-    def scratch(n):
-        return [
-            pltpu.VMEM((n, NODES), F32),
-            pltpu.VMEM((n, NODES), F32),
-            pltpu.VMEM((n, NODES), BF16),
-            pltpu.VMEM((n, NODES), F32),
-            pltpu.VMEM((n, NODES), F32),
-        ]
-
-    adjoint_mid, projected_mid, linear, index = pl.pallas_call(
+    adjoint_mid, projected_mid, linear, index, restrict_t = pl.pallas_call(
         interior_kernel,
         out_shape=(
             struct((inner, NODES), BF16),
             struct((HALF, LANES), F32),
             struct((rows, NODES), F32),
             struct((rows, LANES), jnp.int32),
+            struct((HALF, NODES), BF16),
         ),
-        in_specs=[smem] * 4 + [vmem] * 5 + [hbm] * 4,
-        out_specs=(vmem,) * 4,
-        scratch_shapes=scratch(rows)
+        in_specs=[hbm] * 4 + [vmem] * 7,
+        out_specs=(vmem,) * 5,
+        scratch_shapes=[pltpu.VMEM((rows, NODES), F32)] * 4
         + [
-            pltpu.VMEM((NODES, NODES), BF16),
-            pltpu.VMEM((HALF, NODES), BF16),
-            pltpu.VMEM((LANES, inner), BF16),
+            pltpu.SMEM((CELLS,), jnp.int32),
+            pltpu.SMEM((CELLS,), jnp.int32),
             pltpu.VMEM((HALF, HALF), F32),
             pltpu.SemaphoreType.DMA((4,)),
         ],
         compiler_params=params,
         cost_estimate=pl.CostEstimate(flops=5 * 2 * rows * NODES * NODES, bytes_accessed=4 * 2**20, transcendentals=0),
-    )(place, cell_scale, owner1, pot_slot, src2, orb2, base_potential, face_perm, eig, *map(
-          in_hbm, (stiffness, restrict_t, jnp.asarray(group_table(range(HALO, CELLS - HALO)), BF16), potential)
-      ))
-
-    edge_cells = [*range(HALO), *range(CELLS - HALO, CELLS)]
+    )(*map(in_hbm, (owner1, pot_slot, restrict.T, potential)), src2, orb2, base_potential, face_perm, factor, eig, stiff)
+
     strip_rows = 2 * STRIP * WIDTH
     adjoint2, projected, ghost = pl.pallas_call(
         boundary_kernel,
@@ -421,23 +457,22 @@
             struct((X * HALF, LANES), F32),
             struct((2 * WIDTH, NODES), F32),
         ),
-        in_specs=[smem] * 2 + [vmem] * 12,
+        in_specs=[vmem] * 12,
         out_specs=(hbm, vmem, vmem),
-        scratch_shapes=scratch(strip_rows)
+        scratch_shapes=[pltpu.VMEM((strip_rows, NODES), F32)] * 4
         + [
             pltpu.VMEM((strip_rows, LANES), F32),
             pltpu.VMEM((strip_rows, LANES), jnp.int32),
-            pltpu.VMEM((2 * WIDTH, NODES), BF16),
             pltpu.VMEM((2, HALO * WIDTH, NODES), BF16),
             pltpu.SemaphoreType.DMA((3,)),
         ],
         compiler_params=params,
-    )(place, cell_scale, src2, orb2, base_potential, index, left, right, eig, stiffness, restrict_t,
-      jnp.asarray(group_table(edge_cells), BF16), adjoint_mid, projected_mid)
+    )(src2, orb2, base_potential, index, factor, eig, left, right, stiff, restrict_t, adjoint_mid, projected_mid)
 
     def exchanged(array, axes):
         return lax.all_to_all(array, axes, split_axis=0, concat_axis=0, tiled=True)
 
+    projected, place, x_at = lax.optimization_barrier((projected, place, x_at))
     tiles = exchanged(projected.reshape(X * COPIES, WIDTH, LANES), OUTER)
     tiles = jnp.sum(tiles.reshape(X, COPIES, WIDTH, LANES), axis=1)
     mine = lax.dynamic_slice(tiles, (x_at, 0, 0), (1, WIDTH, LANES), allow_negative_indices=False)
@@ -445,7 +480,7 @@
     columns = pl.pallas_call(
         sum_kernel,
         out_shape=struct((X * HALF, LANES), F32),
-        in_specs=[smem] + [vmem] * 3,
+        in_specs=[vmem] * 4,
         out_specs=vmem,
         compiler_params=params,
     )(place, gathered.reshape(Z * WIDTH, LANES), tiles.reshape(X * WIDTH, LANES), jnp.asarray(unpack_table(), BF16))
@@ -453,10 +488,10 @@
     updated, applied2 = pl.pallas_call(
         apply_kernel,
         out_shape=(struct((HALF, HALF), F32), struct((rows, NODES), BF16)),
-        in_specs=[smem] + [vmem] * 8,
+        in_specs=[vmem] * 8,
         out_specs=(vmem, vmem),
         compiler_params=params,
-    )(place, columns.reshape(X * HALF, LANES), orb2, linear, ghost, left, right, index, prolong)
+    )(columns.reshape(X * HALF, LANES), orb2, linear, ghost, left, right, index, prolong)
     return adjoint2.reshape(orbitals.shape), updated, applied2.reshape(orbitals.shape)
 
 

time: 77.7 us -> 72.5 us (0.933)
  Pallas kernels: 12.5 us -> 8.65 us
  local copies, waits for them, and re-layouts: 1.45 us -> 0.12 us
    pallas_call x1, Pallas kernels: 5.08 us -> 3.52 us  [local(): pl.pallas_call(interior_kernel, out_shape=(struct((inner, NODES), BF16),...]
    unnamed x26 -> x12, local copies, waits for them, and re-layouts: 1.35 us -> 0.03 us
    pallas_call x1, Pallas kernels: 2.98 us -> 1.77 us  [local(): pl.pallas_call(boundary_kernel, out_shape=(struct((rows, NODES), BF16), s...]
  transfers between devices with their start and end apart: 2 -> 2, of which waited for: 0 -> 1; matrix products, arithmetic and copies ran while one was open for 0% -> 0% of each run, Pallas kernels for 7% -> 5%
where the time goes in v5:
time: 72.5 us; the launch traced here: 72.1 us
  blocking collectives  56.2 us (78%)
  Pallas kernels  8.65 us (12%)
  starting transfers between devices  5.67 us (8%)
  between operations  0.78 us (1%)
    all_to_all x3, blocking collectives, exchanged(): return lax.all_to_all(array, axes, split_axis=0, concat_axis=0, tiled=True)  56.2 us
    ppermute x1, starting transfers between devices, local(): left = lax.ppermute(to_right, DOM, ahead)  4.38 us
    pallas_call x1, Pallas kernels, local(): pl.pallas_call(interior_kernel, out_shape=(struct((inner, NODES), BF16),...  3.52 us
    pallas_call x1, Pallas kernels, local(): pl.pallas_call(boundary_kernel, out_shape=(struct((rows, NODES), BF16), s...  1.77 us
  transfers between devices with their start and end apart: 2, of which 1 were waited for; matrix products, arithmetic and copies ran while one was open for 0% of the time, Pallas kernels for 5%

profile of v5, /device:TPU:1, one launch (start us, length us, event | category | flops | bytes accessed | tf_op | source)
XLA Modules:
  0.0 72.1 jit_solution(9032968106385932592)
XLA Ops:
  0.6 0.0 copy-start
  0.6 0.0 copy-start.1
  0.7 0.0 copy-start.2
  0.7 1.3 %shard_map.148 = (f32[48,512]{1,0:T(8,128)S(1)}, f32[48,512]{1,0:T(8,128)S(1)}, f32[48,128]{1,0:T(8,128)S(1)}, f32[8,128]{1,0:T(8,128)S(1)}, bf16[512,512]{1,0:T(8,128)(2,1)S(1)}) custom-call(f32[48]{0:T(128)} %scale_hbm.1, s32[48]{0:T(128)} %bitcast.29, s32[48]{0:T(128)} %slot_hbm.3, bf16[384,512]{1,0:T(8,128)(2,1)} %bitcast.21, bf16[384,512]{1,0:T(8,128)(2,1)} %bitcast.17, ...), custom_call_target="tpu_custom_call" | custom-call | tf_op jit(solution)/shard_map/pallas_call | solution.py:399
  2.0 0.0 copy-start.5
  2.0 4.4 %collective-permute-start = (f32[48,512]{1,0:T(8,128)S(1)}, f32[48,512]{1,0:T(8,128)S(1)}, u32[]{:S(2)}, u32[]{:S(2)}) collective-permute-start(f32[48,512]{1,0:T(8,128)S(1)} %get-tuple-element.25), channel_id=1, source_target_pairs={{0,8},{8,16},{16,24},{24,32},{32,40},{40,48},{48,56},{56,64},{64,7... | collective-permute-start | bytes 294920 | tf_op jit(solution)/shard_map/ppermute | solution.py:425
  6.4 1.3 %collective-permute-start.1 = (f32[48,512]{1,0:T(8,128)S(1)}, f32[48,512]{1,0:T(8,128)S(1)}, u32[]{:S(2)}, u32[]{:S(2)}) collective-permute-start(f32[48,512]{1,0:T(8,128)S(1)} %get-tuple-element.26), channel_id=1, source_target_pairs={{8,0},{16,8},{24,16},{32,24},{40,32},{48,40},{56,48},{64,56},{72,6... | collective-permute-start | bytes 294920 | tf_op jit(solution)/shard_map/ppermute | solution.py:426
  7.7 0.1 fusion
  7.8 0.0 copy-done
  7.8 0.0 copy-done.1
  7.8 0.0 copy-done.2
  7.8 3.5 %shard_map.149 = (bf16[320,512]{1,0:T(8,128)(2,1)S(1)}, f32[64,128]{1,0:T(8,128)S(1)}, f32[384,512]{1,0:T(8,128)S(1)}, s32[384,128]{1,0:T(8,128)S(1)}, bf16[64,512]{1,0:T(8,128)(2,1)S(1)}) custom-call(s32[48]{0:T(128)} %bitcast.30, s32[48]{0:T(128)} %slot_hbm.3, bf16[64,512]{1,0:T(8,128)(2,1)} %bitcast.33, f32[64,64]{1,0:T(8,128)} %potential_hbm.1, ...), custom_call_target="tpu_custom_call" | custom-call | flops 1006632960 | bytes 4194304 | tf_op jit(solution)/shard_map/pallas_call | solution.py:430
  11.3 0.0 collective-permute-done.left
  11.3 0.6 collective-permute-done.1.right
  12.0 1.8 %shard_map.150 = (bf16[384,512]{1,0:T(8,128)(2,1)}, f32[256,128]{1,0:T(8,128)S(1)}, f32[16,512]{1,0:T(8,128)S(1)}) custom-call(bf16[384,512]{1,0:T(8,128)(2,1)S(1)} %bitcast.23, bf16[384,512]{1,0:T(8,128)(2,1)S(1)} %bitcast.19, f32[48,512]{1,0:T(8,128)S(1)} %copy-done.2, s32[384,128]{1,0:T(8,128)S(1)} %get-tuple-element.24.index_own.index, ...), custom_call_target="tpu_custom_call" | custom-call | tf_op jit(solution)/shard_map/pallas_call | solution.py:453
  13.7 0.1 broadcast_in_dim.6.place
  13.8 23.1 %all_to_all.15 = f32[32,8,128]{2,1,0:T(8,128)S(1)} all-to-all(f32[32,8,128]{2,1,0:T(8,128)S(1)} %bitcast.27), channel_id=1, replica_groups=mesh['x'=4,'z'=16,'y'=4,'core'=2] {'x','y','core'}, dimensions={0} | all-to-all | bytes 262144 | tf_op jit(solution)/shard_map/all_to_all | solution.py:473
  37.0 0.0 copy-start.4
  37.0 20.0 %all_to_all.16 = f32[16,8,128]{2,1,0:T(8,128)S(1)} all-to-all(f32[16,8,128]{2,1,0:T(8,128)S(1)} %broadcast_in_dim.15), channel_id=1, replica_groups=mesh['x'=4,'z'=16,'y'=4,'core'=2] {'z'}, dimensions={0} | all-to-all | bytes 131072 | tf_op jit(solution)/shard_map/all_to_all | solution.py:473
  57.0 0.0 copy-done.4
  57.0 0.8 %shard_map.151 = f32[256,128]{1,0:T(8,128)S(1)} custom-call(f32[2,128]{1,0:T(2,128)S(1)} %broadcast_in_dim.6.place, f32[128,128]{1,0:T(8,128)S(1)} %bitcast.26, f32[32,128]{1,0:T(8,128)S(1)} %bitcast.28, bf16[128,128]{1,0:T(8,128)(2,1)S(1)} %copy-done.4), custom_call_target="tpu_custom_call" | custom-call | tf_op jit(solution)/shard_map/pallas_call | solution.py:480
  57.8 0.0 copy-start.3
  57.8 13.0 %all_to_all.17 = f32[32,8,128]{2,1,0:T(8,128)S(1)} all-to-all(f32[32,8,128]{2,1,0:T(8,128)S(1)} %bitcast.25), channel_id=1, replica_groups=mesh['x'=4,'z'=16,'y'=4,'core'=2] {'x','y','core'}, dimensions={0} | all-to-all | bytes 262144 | tf_op jit(solution)/shard_map/all_to_all | solution.py:473
  70.8 1.3 %shard_map.152 = (f32[64,64]{1,0:T(8,128)}, bf16[384,512]{1,0:T(8,128)(2,1)}) custom-call(f32[256,128]{1,0:T(8,128)S(1)} %bitcast.24, bf16[384,512]{1,0:T(8,128)(2,1)S(1)} %bitcast.20, f32[384,512]{1,0:T(8,128)S(1)} %get-tuple-element.35.linear, f32[16,512]{1,0:T(8,128)S(1)} %get-tuple-element.36.ghost, f32[48,512]{1,0:T(8,128)S(1)} %collective-permute-done.left, ...), custom_call_target="tpu_custom_call" | custom-call | tf_op jit(solution)/shard_map/pallas_call | solution.py:488
  (5 shorter events, 0.0 us)
Async XLA Ops:
  0.6 7.2 %copy-start = (bf16[48,8,512]{2,1,0:T(8,128)(2,1)S(1)}, bf16[48,8,512]{2,1,0:T(8,128)(2,1)}, u32[]{:S(2)}) copy-start(bf16[48,8,512]{2,1,0:T(8,128)(2,1)} %param.13) | copy-start | bytes 1179652
  0.6 7.2 %copy-start.1 = (bf16[48,8,512]{2,1,0:T(8,128)(2,1)S(1)}, bf16[48,8,512]{2,1,0:T(8,128)(2,1)}, u32[]{:S(2)}) copy-start(bf16[48,8,512]{2,1,0:T(8,128)(2,1)} %param.14) | copy-start | bytes 1179652
  0.7 7.1 %copy-start.2 = (f32[48,512]{1,0:T(8,128)S(1)}, f32[48,512]{1,0:T(8,128)}, u32[]{:S(2)}) copy-start(f32[48,512]{1,0:T(8,128)} %base.3) | copy-start | bytes 294916
  2.0 5.8 %copy-start.5 = (s32[48,64]{1,0:T(8,128)S(1)}, s32[48,64]{1,0:T(8,128)}, u32[]{:S(2)}) copy-start(s32[48,64]{1,0:T(8,128)} %perm.1) | copy-start | bytes 36868
  2.0 9.3 %collective-permute-start = (f32[48,512]{1,0:T(8,128)S(1)}, f32[48,512]{1,0:T(8,128)S(1)}, u32[]{:S(2)}, u32[]{:S(2)}) collective-permute-start(f32[48,512]{1,0:T(8,128)S(1)} %get-tuple-element.25), channel_id=1, source_target_pairs={{0,8},{8,16},{16,24},{24,32},{32,40},{40,48},{48,56},{56,64},{64,7... | collective-permute-start | bytes 294920 | tf_op jit(solution)/shard_map/ppermute | solution.py:425
  6.4 5.5 %collective-permute-start.1 = (f32[48,512]{1,0:T(8,128)S(1)}, f32[48,512]{1,0:T(8,128)S(1)}, u32[]{:S(2)}, u32[]{:S(2)}) collective-permute-start(f32[48,512]{1,0:T(8,128)S(1)} %get-tuple-element.26), channel_id=1, source_target_pairs={{8,0},{16,8},{24,16},{32,24},{40,32},{48,40},{56,48},{64,56},{72,6... | collective-permute-start | bytes 294920 | tf_op jit(solution)/shard_map/ppermute | solution.py:426
  37.0 20.1 %copy-start.4 = (bf16[128,128]{1,0:T(8,128)(2,1)S(1)}, bf16[128,128]{1,0:T(8,128)(2,1)}, u32[]{:S(2)}) copy-start(bf16[128,128]{1,0:T(8,128)(2,1)} %constant.21.clone.unpack) | copy-start | bytes 98308
  57.8 13.0 %copy-start.3 = (bf16[64,512]{1,0:T(8,128)(2,1)S(1)}, bf16[64,512]{1,0:T(8,128)(2,1)}, u32[]{:S(2)}) copy-start(bf16[64,512]{1,0:T(8,128)(2,1)} %prolong.1) | copy-start | bytes 196612

commit v6 on v5

--- a/solution.py
+++ b/solution.py
@@ -300,36 +300,28 @@
     row = lax.broadcasted_iota(jnp.int32, ids.shape, 0) % WIDTH
     lane = lax.broadcasted_iota(jnp.int32, ids.shape, 1)
     ids = jnp.where(jnp.where(lane < CELLS, lane // 6, 0) == row, ids, 0.0)
-    ids = jnp.sum(ids.reshape(Z + X, WIDTH, LANES), axis=1)
-    lane = lax.broadcasted_iota(jnp.int32, ids.shape, 1)
-    row = lax.broadcasted_iota(jnp.int32, ids.shape, 0)
-    mine = jnp.where(row < Z, place[0:1], place[1:2])
-    slots = mine + (jnp.where(row < Z, row, (row - Z) * Z) * HALF + lane - POT).astype(F32)
-    ids = jnp.where((lane >= POT) & (lane < IDS), slots, ids)
-    known = jnp.where(lane[:Z] < IDS, ids[:Z], -1.0)
-    wanted = jnp.where(lane[Z:] < IDS + 2, ids[Z:], -2.0)
-    known = jnp.transpose(jnp.concatenate([known, jnp.zeros((LANES - Z, LANES), F32)], 0))
-    total = jnp.zeros((2 * WIDTH, X * LANES), F32)
-    for s in range(0, Z, 2):
-        hot = [
-            jnp.concatenate(
-                [jnp.where(known[:, i : i + 1] == wanted[m : m + 1], 1.0, 0.0).astype(BF16) for m in range(X)], 1
-            )
-            for i in (s, s + 1)
-        ]
+    ids = jnp.sum(ids.reshape(X * Z + 1, WIDTH, LANES), axis=1)
+    known, wanted = ids[: X * Z], ids[X * Z :]
+    lane = lax.broadcasted_iota(jnp.int32, known.shape, 1)
+    row = lax.broadcasted_iota(jnp.int32, known.shape, 0)
+    slots = ((row % X * Z + row // X) * HALF + lane - POT).astype(F32)
+    known = jnp.where(lane < POT, known, jnp.where(lane < IDS, slots, -1.0))
+    lane = lane[:1]
+    wanted = jnp.where((lane >= POT) & (lane < IDS), place[...] + (lane - POT).astype(F32), wanted)
+    wanted = jnp.where(lane < IDS + 2, wanted, -2.0)
+    wanted = jnp.transpose(jnp.broadcast_to(wanted, (LANES, LANES)))
+    total = jnp.zeros((2 * WIDTH, LANES), F32)
+    for s in range(0, X * Z, 2):
+        hot = [jnp.where(wanted == known[i : i + 1], 1.0, 0.0).astype(BF16) for i in (s, s + 1)]
         both = [jnp.concatenate([high[tile(i)], rest[tile(i)]], 0) for i in (s, s + 1)]
-        total = total + dot(jnp.concatenate(both, 1), jnp.concatenate(hot, 0))
+        total = total + dot(jnp.concatenate(both, 1), jnp.concatenate(hot, 1), NT)
     result = total[:WIDTH] + total[WIDTH:]
-    for m in range(X):
-        for i in range(COPIES):
-            out[tile(m * COPIES + i)] = result[:, cols(m)]
+    for i in range(COPIES):
+        out[tile(i)] = result
 
 
 def apply_kernel(columns, orb, linear, ghost, left, right, index, prolong, updated_out, applied_out):
-    summed = columns[0:HALF]
-    for i in range(1, X):
-        summed = summed + columns[i * HALF : (i + 1) * HALF]
-    table = jnp.transpose(summed)
+    table = jnp.transpose(columns[...])
     updated_out[...] = table[POT:IDS]
     high, rest = split(table)
     node = dot(high, prolong[...]) + dot(rest, prolong[...])
@@ -392,8 +384,7 @@
     orb2 = orbitals.reshape(CELLS * WIDTH, NODES)
     src2 = adjoint_source.reshape(CELLS * WIDTH, NODES)
     owner1 = owner.reshape(CELLS)
-    first = jnp.stack([x_at * Z, z_at]) * HALF
-    place = jnp.broadcast_to(first.astype(F32)[:, None], (2, LANES))
+    place = jnp.full((1, LANES), ((x_at * Z + z_at) * HALF).astype(F32))
 
     hbm = pl.BlockSpec(memory_space=pltpu.HBM)
     to_left, to_right, factor, eig, stiff = pl.pallas_call(
@@ -476,22 +467,23 @@
     tiles = exchanged(projected.reshape(X * COPIES, WIDTH, LANES), OUTER)
     tiles = jnp.sum(tiles.reshape(X, COPIES, WIDTH, LANES), axis=1)
     mine = lax.dynamic_slice(tiles, (x_at, 0, 0), (1, WIDTH, LANES), allow_negative_indices=False)
-    gathered = exchanged(jnp.broadcast_to(mine, (Z, WIDTH, LANES)), ("z",))
+    tiles, mine = lax.optimization_barrier((tiles, mine))
+    gathered = exchanged(jnp.broadcast_to(tiles.reshape(1, X * WIDTH, LANES), (Z, X * WIDTH, LANES)), ("z",))
     columns = pl.pallas_call(
         sum_kernel,
-        out_shape=struct((X * HALF, LANES), F32),
+        out_shape=struct((HALF, LANES), F32),
         in_specs=[vmem] * 4,
         out_specs=vmem,
         compiler_params=params,
-    )(place, gathered.reshape(Z * WIDTH, LANES), tiles.reshape(X * WIDTH, LANES), jnp.asarray(unpack_table(), BF16))
-    columns = exchanged(columns.reshape(X * COPIES, WIDTH, LANES), OUTER)
+    )(place, gathered.reshape(X * Z * WIDTH, LANES), mine.reshape(WIDTH, LANES), jnp.asarray(unpack_table(), BF16))
+    columns = exchanged(columns.reshape(COPIES, WIDTH, LANES), ORB)
     updated, applied2 = pl.pallas_call(
         apply_kernel,
         out_shape=(struct((HALF, HALF), F32), struct((rows, NODES), BF16)),
         in_specs=[vmem] * 8,
         out_specs=(vmem, vmem),
         compiler_params=params,
-    )(columns.reshape(X * HALF, LANES), orb2, linear, ghost, left, right, index, prolong)
+    )(columns.reshape(HALF, LANES), orb2, linear, ghost, left, right, index, prolong)
     return adjoint2.reshape(orbitals.shape), updated, applied2.reshape(orbitals.shape)
 
 

time: 72.5 us -> 74.5 us (1.028)
  blocking collectives: 56.2 us -> 57.9 us
    all_to_all x3, blocking collectives: 56.2 us -> 57.9 us  [exchanged(): return lax.all_to_all(array, axes, split_axis=0, concat_axis=0, tiled=True)]
where the time goes in v6:
time: 74.5 us; the launch traced here: 74.1 us
  blocking collectives  57.9 us (78%)
  Pallas kernels  8.93 us (12%)
  starting transfers between devices  5.67 us (8%)
  between operations  0.79 us (1%)
    all_to_all x3, blocking collectives, exchanged(): return lax.all_to_all(array, axes, split_axis=0, concat_axis=0, tiled=True)  57.9 us
    ppermute x1, starting transfers between devices, local(): left = lax.ppermute(to_right, DOM, ahead)  4.38 us
    pallas_call x1, Pallas kernels, local(): pl.pallas_call(interior_kernel, out_shape=(struct((inner, NODES), BF16),...  3.51 us
    pallas_call x1, Pallas kernels, local(): pl.pallas_call(boundary_kernel, out_shape=(struct((rows, NODES), BF16), s...  1.77 us
  transfers between devices with their start and end apart: 2, of which 1 were waited for; matrix products, arithmetic and copies ran while one was open for 0% of the time, Pallas kernels for 5%

profile of v6, /device:TPU:1, one launch (start us, length us, event | category | flops | bytes accessed | tf_op | source)
XLA Modules:
  0.0 74.1 jit_solution(14042437114523801826)
XLA Ops:
  0.6 0.0 copy-start
  0.6 0.0 copy-start.1
  0.7 0.0 copy-start.2
  0.7 1.3 %shard_map.148 = (f32[48,512]{1,0:T(8,128)S(1)}, f32[48,512]{1,0:T(8,128)S(1)}, f32[48,128]{1,0:T(8,128)S(1)}, f32[8,128]{1,0:T(8,128)S(1)}, bf16[512,512]{1,0:T(8,128)(2,1)S(1)}) custom-call(f32[48]{0:T(128)} %scale_hbm.1, s32[48]{0:T(128)} %bitcast.27, s32[48]{0:T(128)} %slot_hbm.3, bf16[384,512]{1,0:T(8,128)(2,1)} %bitcast.18, bf16[384,512]{1,0:T(8,128)(2,1)} %bitcast.14, ...), custom_call_target="tpu_custom_call" | custom-call | tf_op jit(solution)/shard_map/pallas_call | solution.py:390
  2.0 0.0 copy-start.5
  2.0 4.4 %collective-permute-start = (f32[48,512]{1,0:T(8,128)S(1)}, f32[48,512]{1,0:T(8,128)S(1)}, u32[]{:S(2)}, u32[]{:S(2)}) collective-permute-start(f32[48,512]{1,0:T(8,128)S(1)} %get-tuple-element.27), channel_id=1, source_target_pairs={{0,8},{8,16},{16,24},{24,32},{32,40},{40,48},{48,56},{56,64},{64,7... | collective-permute-start | bytes 294920 | tf_op jit(solution)/shard_map/ppermute | solution.py:416
  6.4 1.3 %collective-permute-start.1 = (f32[48,512]{1,0:T(8,128)S(1)}, f32[48,512]{1,0:T(8,128)S(1)}, u32[]{:S(2)}, u32[]{:S(2)}) collective-permute-start(f32[48,512]{1,0:T(8,128)S(1)} %get-tuple-element.28), channel_id=1, source_target_pairs={{8,0},{16,8},{24,16},{32,24},{40,32},{48,40},{56,48},{64,56},{72,6... | collective-permute-start | bytes 294920 | tf_op jit(solution)/shard_map/ppermute | solution.py:417
  7.7 0.0 copy-done
  7.7 0.0 copy-done.1
  7.7 0.0 copy-done.2
  7.7 0.0 copy-done.5
  7.8 3.5 %shard_map.149 = (bf16[320,512]{1,0:T(8,128)(2,1)S(1)}, f32[64,128]{1,0:T(8,128)S(1)}, f32[384,512]{1,0:T(8,128)S(1)}, s32[384,128]{1,0:T(8,128)S(1)}, bf16[64,512]{1,0:T(8,128)(2,1)S(1)}) custom-call(s32[48]{0:T(128)} %bitcast.28, s32[48]{0:T(128)} %slot_hbm.3, bf16[64,512]{1,0:T(8,128)(2,1)} %bitcast.31, f32[64,64]{1,0:T(8,128)} %potential_hbm.1, ...), custom_call_target="tpu_custom_call" | custom-call | flops 1006632960 | bytes 4194304 | tf_op jit(solution)/shard_map/pallas_call | solution.py:421
  11.3 0.0 collective-permute-done.left
  11.3 0.7 collective-permute-done.1.right
  12.0 1.8 %shard_map.150 = (bf16[384,512]{1,0:T(8,128)(2,1)}, f32[256,128]{1,0:T(8,128)S(1)}, f32[16,512]{1,0:T(8,128)S(1)}) custom-call(bf16[384,512]{1,0:T(8,128)(2,1)S(1)} %bitcast.20, bf16[384,512]{1,0:T(8,128)(2,1)S(1)} %bitcast.16, f32[48,512]{1,0:T(8,128)S(1)} %copy-done.2, s32[384,128]{1,0:T(8,128)S(1)} %get-tuple-element.26.index_own.index, ...), custom_call_target="tpu_custom_call" | custom-call | tf_op jit(solution)/shard_map/pallas_call | solution.py:444
  13.7 23.1 %all_to_all.15 = f32[32,8,128]{2,1,0:T(8,128)S(1)} all-to-all(f32[32,8,128]{2,1,0:T(8,128)S(1)} %bitcast.22), channel_id=1, replica_groups=mesh['x'=4,'z'=16,'y'=4,'core'=2] {'x','y','core'}, dimensions={0} | all-to-all | bytes 262144 | tf_op jit(solution)/shard_map/all_to_all | solution.py:464
  36.9 0.0 copy-start.4
  36.9 22.4 %all_to_all.16 = f32[16,32,128]{2,1,0:T(8,128)S(1)} all-to-all(f32[16,32,128]{2,1,0:T(8,128)S(1)} %broadcast_in_dim.12), channel_id=1, replica_groups=mesh['x'=4,'z'=16,'y'=4,'core'=2] {'z'}, dimensions={0} | all-to-all | bytes 524288 | tf_op jit(solution)/shard_map/all_to_all | solution.py:464
  59.3 0.0 copy-done.4
  59.3 1.1 %shard_map.151 = f32[64,128]{1,0:T(8,128)S(1)} custom-call(f32[1,128]{1,0:T(1,128)S(1)} %broadcast_in_dim.10.place, f32[512,128]{1,0:T(8,128)S(1)} %bitcast.21, f32[8,128]{1,0:T(8,128)S(1)} %bitcast.25, bf16[128,128]{1,0:T(8,128)(2,1)S(1)} %copy-done.4), custom_call_target="tpu_custom_call" | custom-call | tf_op jit(solution)/shard_map/pallas_call | solution.py:472
  60.4 0.0 copy-start.3
  60.4 12.4 %all_to_all.17 = f32[8,8,128]{2,1,0:T(8,128)S(1)} all-to-all(f32[8,8,128]{2,1,0:T(8,128)S(1)} %bitcast.23), channel_id=1, replica_groups=mesh['x'=4,'z'=16,'y'=4,'core'=2] {'y','core'}, dimensions={0} | all-to-all | bytes 65536 | tf_op jit(solution)/shard_map/all_to_all | solution.py:464
  72.8 0.0 copy-done.3
  72.8 1.3 %shard_map.152 = (f32[64,64]{1,0:T(8,128)}, bf16[384,512]{1,0:T(8,128)(2,1)}) custom-call(f32[64,128]{1,0:T(8,128)S(1)} %bitcast.24, bf16[384,512]{1,0:T(8,128)(2,1)S(1)} %bitcast.17, f32[384,512]{1,0:T(8,128)S(1)} %get-tuple-element.39.linear, f32[16,512]{1,0:T(8,128)S(1)} %get-tuple-element.40.ghost, f32[48,512]{1,0:T(8,128)S(1)} %collective-permute-done.left, ...), custom_call_target="tpu_custom_call" | custom-call | tf_op jit(solution)/shard_map/pallas_call | solution.py:480
  (4 shorter events, 0.0 us)
Async XLA Ops:
  0.6 7.1 %copy-start = (bf16[48,8,512]{2,1,0:T(8,128)(2,1)S(1)}, bf16[48,8,512]{2,1,0:T(8,128)(2,1)}, u32[]{:S(2)}) copy-start(bf16[48,8,512]{2,1,0:T(8,128)(2,1)} %param.13) | copy-start | bytes 1179652
  0.6 7.1 %copy-start.1 = (bf16[48,8,512]{2,1,0:T(8,128)(2,1)S(1)}, bf16[48,8,512]{2,1,0:T(8,128)(2,1)}, u32[]{:S(2)}) copy-start(bf16[48,8,512]{2,1,0:T(8,128)(2,1)} %param.14) | copy-start | bytes 1179652
  0.7 7.1 %copy-start.2 = (f32[48,512]{1,0:T(8,128)S(1)}, f32[48,512]{1,0:T(8,128)}, u32[]{:S(2)}) copy-start(f32[48,512]{1,0:T(8,128)} %base.3) | copy-start | bytes 294916
  2.0 5.7 %copy-start.5 = (s32[48,64]{1,0:T(8,128)S(1)}, s32[48,64]{1,0:T(8,128)}, u32[]{:S(2)}) copy-start(s32[48,64]{1,0:T(8,128)} %perm.1) | copy-start | bytes 36868
  2.0 9.3 %collective-permute-start = (f32[48,512]{1,0:T(8,128)S(1)}, f32[48,512]{1,0:T(8,128)S(1)}, u32[]{:S(2)}, u32[]{:S(2)}) collective-permute-start(f32[48,512]{1,0:T(8,128)S(1)} %get-tuple-element.27), channel_id=1, source_target_pairs={{0,8},{8,16},{16,24},{24,32},{32,40},{40,48},{48,56},{56,64},{64,7... | collective-permute-start | bytes 294920 | tf_op jit(solution)/shard_map/ppermute | solution.py:416
  6.4 5.5 %collective-permute-start.1 = (f32[48,512]{1,0:T(8,128)S(1)}, f32[48,512]{1,0:T(8,128)S(1)}, u32[]{:S(2)}, u32[]{:S(2)}) collective-permute-start(f32[48,512]{1,0:T(8,128)S(1)} %get-tuple-element.28), channel_id=1, source_target_pairs={{8,0},{16,8},{24,16},{32,24},{40,32},{48,40},{56,48},{64,56},{72,6... | collective-permute-start | bytes 294920 | tf_op jit(solution)/shard_map/ppermute | solution.py:417
  36.9 22.4 %copy-start.4 = (bf16[128,128]{1,0:T(8,128)(2,1)S(1)}, bf16[128,128]{1,0:T(8,128)(2,1)}, u32[]{:S(2)}) copy-start(bf16[128,128]{1,0:T(8,128)(2,1)} %constant.21.clone.unpack) | copy-start | bytes 98308
  60.4 12.4 %copy-start.3 = (bf16[64,512]{1,0:T(8,128)(2,1)S(1)}, bf16[64,512]{1,0:T(8,128)(2,1)}, u32[]{:S(2)}) copy-start(bf16[64,512]{1,0:T(8,128)(2,1)} %prolong.1) | copy-start | bytes 196612

commit v7 on v5

--- a/solution.py
+++ b/solution.py
@@ -89,7 +89,8 @@
 
 
 def pack_kernel(scale_hbm, owner_hbm, slot_hbm, src_hbm, orb_hbm, base_hbm, perm_hbm, stiff_hbm, eig_hbm,
-                to_left, to_right, factor_out, eig_out, stiff_out, scale, owner, slot, src, orb, base, perm, eig, sems):
+                to_mate, to_other, factor_out, eig_out, stiff_out,
+                scale, owner, slot, src, orb, base, perm, eig, to_left, to_right, sems):
     top, rows = CELLS - WIDTH, CELLS * WIDTH
     copies = [(scale_hbm, scale), (owner_hbm, owner), (slot_hbm, slot)]
     for hbm, here, size, end in (
@@ -124,6 +125,9 @@
             out[at, OWNER] = jnp.full((1, LANES), owner[edge_cell].astype(F32), F32)
             mark = slot[edge_cell].astype(F32) if i == end * (HALO - 1) else 1.0
             out[at, SLOT] = jnp.full((1, LANES), mark, F32)
+    even = lax.axis_index("z") % 2 == 0
+    to_mate[...] = jnp.where(even, to_right[...], to_left[...])
+    to_other[...] = jnp.where(even, to_left[...], to_right[...])
     copies[-1].wait()
 
 
@@ -228,8 +232,8 @@
     )
 
 
-def boundary_kernel(src, orb, base, index_own, factor_own, eig, left, right, stiff, restrict_t, adjoint_mid, projected_mid,
-                    adjoint_out, projected_out, ghost_out,
+def boundary_kernel(src, orb, base, index_own, factor_own, eig, of_mate, of_other, stiff, restrict_t, adjoint_mid,
+                    projected_mid, adjoint_out, projected_out, ghost_out, left, right,
                     x, quarter, kin, shifted, factor, index, adjoint_ends, sems):
     near, edge = 2 * HALO * WIDTH, HALO * WIDTH
     last = CELLS * WIDTH
@@ -239,6 +243,9 @@
         pltpu.make_async_copy(adjoint_ends.at[1], adjoint_out.at[last - edge : last], sems.at[2]),
     ]
     copies[0].start()
+    even = lax.axis_index("z") % 2 == 0
+    left[...] = jnp.where(even, of_other[...], of_mate[...])
+    right[...] = jnp.where(even, of_mate[...], of_other[...])
     quarter[0:edge] = relax * left[0:SRC_ROWS]
     quarter[edge : edge + near] = relax * src[0:near].astype(F32)
     quarter[edge + near : edge + 2 * near] = relax * src[last - near :].astype(F32)
@@ -396,7 +403,7 @@
     place = jnp.broadcast_to(first.astype(F32)[:, None], (2, LANES))
 
     hbm = pl.BlockSpec(memory_space=pltpu.HBM)
-    to_left, to_right, factor, eig, stiff = pl.pallas_call(
+    to_mate, to_other, factor, eig, stiff = pl.pallas_call(
         pack_kernel,
         out_shape=(
             struct((HALO_ROWS, NODES), F32),
@@ -416,14 +423,15 @@
             pltpu.VMEM((2, WIDTH, NODES), F32),
             pltpu.VMEM((2, WIDTH, HALF), jnp.int32),
             pltpu.SMEM((WIDTH,), F32),
+            pltpu.VMEM((HALO_ROWS, NODES), F32),
+            pltpu.VMEM((HALO_ROWS, NODES), F32),
             pltpu.SemaphoreType.DMA((13,)),
         ],
         compiler_params=params,
     )(*map(in_hbm, (cell_scale, owner1, pot_slot, src2, orb2, base_potential, face_perm, stiffness, eigenvalues)))
 
-    ahead = [(i, i + 1) for i in range(X * Z - 1)]
-    left = lax.ppermute(to_right, DOM, ahead)
-    right = lax.ppermute(to_left, DOM, [(b, a) for a, b in ahead])
+    of_mate = lax.ppermute(to_mate, DOM, [(i, i ^ 1) for i in range(X * Z)])
+    of_other = lax.ppermute(to_other, DOM, [(i, i + 1 if i % 2 else i - 1) for i in range(1, X * Z - 1)])
 
     rows = CELLS * WIDTH
     inner = rows - 2 * HALO * WIDTH
@@ -450,15 +458,17 @@
     )(*map(in_hbm, (owner1, pot_slot, restrict.T, potential)), src2, orb2, base_potential, face_perm, factor, eig, stiff)
 
     strip_rows = 2 * STRIP * WIDTH
-    adjoint2, projected, ghost = pl.pallas_call(
+    adjoint2, projected, ghost, left, right = pl.pallas_call(
         boundary_kernel,
         out_shape=(
             struct((rows, NODES), BF16),
             struct((X * HALF, LANES), F32),
             struct((2 * WIDTH, NODES), F32),
+            struct((HALO_ROWS, NODES), F32),
+            struct((HALO_ROWS, NODES), F32),
         ),
         in_specs=[vmem] * 12,
-        out_specs=(hbm, vmem, vmem),
+        out_specs=(hbm, vmem, vmem, vmem, vmem),
         scratch_shapes=[pltpu.VMEM((strip_rows, NODES), F32)] * 4
         + [
             pltpu.VMEM((strip_rows, LANES), F32),
@@ -467,7 +477,8 @@
             pltpu.SemaphoreType.DMA((3,)),
         ],
         compiler_params=params,
-    )(src2, orb2, base_potential, index, factor, eig, left, right, stiff, restrict_t, adjoint_mid, projected_mid)
+    )(src2, orb2, base_potential, index, factor, eig, of_mate, of_other, stiff, restrict_t, adjoint_mid,
+      projected_mid)
 
     def exchanged(array, axes):
         return lax.all_to_all(array, axes, split_axis=0, concat_axis=0, tiled=True)

time: 72.5 us -> 72.6 us (level)
  blocking collectives: 56.2 us -> 57.3 us
    all_to_all x3, blocking collectives: 56.2 us -> 57.3 us  [exchanged(): return lax.all_to_all(array, axes, split_axis=0, concat_axis=0, tiled=True)]
  transfers between devices with their start and end apart: 2 -> 2, of which waited for: 1 -> 0; matrix products, arithmetic and copies ran while one was open for 0% -> 0% of each run, Pallas kernels for 5% -> 5%
where the time goes in v7:
time: 72.6 us; the launch traced here: 72.2 us
  blocking collectives  57.3 us (79%)
  Pallas kernels  8.83 us (12%)
  starting transfers between devices  5.04 us (7%)
  between operations  0.78 us (1%)
    all_to_all x3, blocking collectives, exchanged(): return lax.all_to_all(array, axes, split_axis=0, concat_axis=0, tiled=True)  57.3 us
    ppermute x1, starting transfers between devices, local(): of_mate = lax.ppermute(to_mate, DOM, [(i, i ^ 1) for i in range(X * Z)])  4.38 us
    pallas_call x1, Pallas kernels, local(): pl.pallas_call(interior_kernel, out_shape=(struct((inner, NODES), BF16),...  3.51 us
    pallas_call x1, Pallas kernels, local(): pl.pallas_call(boundary_kernel, out_shape=(struct((rows, NODES), BF16), s...  1.96 us
  transfers between devices with their start and end apart: 2, of which 0 were waited for; matrix products, arithmetic and copies ran while one was open for 0% of the time, Pallas kernels for 5%

profile of v7, /device:TPU:1, one launch (start us, length us, event | category | flops | bytes accessed | tf_op | source)
XLA Modules:
  0.0 72.2 jit_solution(5955599972333304701)
XLA Ops:
  0.6 0.0 copy-start
  0.6 0.0 copy-start.1
  0.7 0.0 copy-start.2
  0.7 1.3 %shard_map.148 = (f32[48,512]{1,0:T(8,128)S(1)}, f32[48,512]{1,0:T(8,128)S(1)}, f32[48,128]{1,0:T(8,128)S(1)}, f32[8,128]{1,0:T(8,128)S(1)}, bf16[512,512]{1,0:T(8,128)(2,1)S(1)}) custom-call(f32[48]{0:T(128)} %scale_hbm.1, s32[48]{0:T(128)} %bitcast.29, s32[48]{0:T(128)} %slot_hbm.3, bf16[384,512]{1,0:T(8,128)(2,1)} %bitcast.21, bf16[384,512]{1,0:T(8,128)(2,1)} %bitcast.17, ...), custom_call_target="tpu_custom_call" | custom-call | tf_op jit(solution)/shard_map/pallas_call | solution.py:406
  2.0 0.0 copy-start.5
  2.0 4.4 %collective-permute-start = (f32[48,512]{1,0:T(8,128)S(1)}, f32[48,512]{1,0:T(8,128)S(1)}, u32[]{:S(2)}, u32[]{:S(2)}) collective-permute-start(f32[48,512]{1,0:T(8,128)S(1)} %get-tuple-element.27), channel_id=1, source_target_pairs={{0,8},{8,0},{16,24},{24,16},{32,40},{40,32},{48,56},{56,48},{64,72... | collective-permute-start | bytes 294920 | tf_op jit(solution)/shard_map/ppermute | solution.py:433
  6.4 0.7 collective-permute-start.1
  7.1 0.1 fusion
  7.2 0.0 copy-done
  7.2 0.0 copy-done.1
  7.2 0.0 copy-done.2
  7.2 0.0 copy-done.5
  7.2 3.5 %shard_map.149 = (bf16[320,512]{1,0:T(8,128)(2,1)S(1)}, f32[64,128]{1,0:T(8,128)S(1)}, f32[384,512]{1,0:T(8,128)S(1)}, s32[384,128]{1,0:T(8,128)S(1)}, bf16[64,512]{1,0:T(8,128)(2,1)S(1)}) custom-call(s32[48]{0:T(128)} %bitcast.30, s32[48]{0:T(128)} %slot_hbm.3, bf16[64,512]{1,0:T(8,128)(2,1)} %bitcast.33, f32[64,64]{1,0:T(8,128)} %potential_hbm.1, ...), custom_call_target="tpu_custom_call" | custom-call | flops 1006632960 | bytes 4194304 | tf_op jit(solution)/shard_map/pallas_call | solution.py:438
  10.7 0.0 collective-permute-done.of_mate
  10.7 0.0 collective-permute-done.1.of_other
  10.7 2.0 %shard_map.150 = (bf16[384,512]{1,0:T(8,128)(2,1)}, f32[256,128]{1,0:T(8,128)S(1)}, f32[16,512]{1,0:T(8,128)S(1)}, f32[48,512]{1,0:T(8,128)S(1)}, f32[48,512]{1,0:T(8,128)S(1)}) custom-call(bf16[384,512]{1,0:T(8,128)(2,1)S(1)} %bitcast.23, bf16[384,512]{1,0:T(8,128)(2,1)S(1)} %bitcast.19, f32[48,512]{1,0:T(8,128)S(1)} %copy-done.2, ...), custom_call_target="tpu_custom_call" | custom-call | tf_op jit(solution)/shard_map/pallas_call | solution.py:461
  12.7 0.1 broadcast_in_dim.6.place
  12.8 25.4 %all_to_all.15 = f32[32,8,128]{2,1,0:T(8,128)S(1)} all-to-all(f32[32,8,128]{2,1,0:T(8,128)S(1)} %bitcast.27), channel_id=1, replica_groups=mesh['x'=4,'z'=16,'y'=4,'core'=2] {'x','y','core'}, dimensions={0} | all-to-all | bytes 262144 | tf_op jit(solution)/shard_map/all_to_all | solution.py:484
  38.2 0.0 copy-start.4
  38.2 19.0 %all_to_all.16 = f32[16,8,128]{2,1,0:T(8,128)S(1)} all-to-all(f32[16,8,128]{2,1,0:T(8,128)S(1)} %broadcast_in_dim.15), channel_id=1, replica_groups=mesh['x'=4,'z'=16,'y'=4,'core'=2] {'z'}, dimensions={0} | all-to-all | bytes 131072 | tf_op jit(solution)/shard_map/all_to_all | solution.py:484
  57.2 0.8 %shard_map.151 = f32[256,128]{1,0:T(8,128)S(1)} custom-call(f32[2,128]{1,0:T(2,128)S(1)} %broadcast_in_dim.6.place, f32[128,128]{1,0:T(8,128)S(1)} %bitcast.26, f32[32,128]{1,0:T(8,128)S(1)} %bitcast.28, bf16[128,128]{1,0:T(8,128)(2,1)S(1)} %copy-done.4), custom_call_target="tpu_custom_call" | custom-call | tf_op jit(solution)/shard_map/pallas_call | solution.py:491
  57.9 0.0 copy-start.3
  57.9 13.0 %all_to_all.17 = f32[32,8,128]{2,1,0:T(8,128)S(1)} all-to-all(f32[32,8,128]{2,1,0:T(8,128)S(1)} %bitcast.25), channel_id=1, replica_groups=mesh['x'=4,'z'=16,'y'=4,'core'=2] {'x','y','core'}, dimensions={0} | all-to-all | bytes 262144 | tf_op jit(solution)/shard_map/all_to_all | solution.py:484
  70.9 1.3 %shard_map.152 = (f32[64,64]{1,0:T(8,128)}, bf16[384,512]{1,0:T(8,128)(2,1)}) custom-call(f32[256,128]{1,0:T(8,128)S(1)} %bitcast.24, bf16[384,512]{1,0:T(8,128)(2,1)S(1)} %bitcast.20, f32[384,512]{1,0:T(8,128)S(1)} %get-tuple-element.37.linear, f32[16,512]{1,0:T(8,128)S(1)} %get-tuple-element.38.ghost, f32[48,512]{1,0:T(8,128)S(1)} %get-tuple-element.39.left, ...), custom_call_target="tpu_custom_call" | custom-call | tf_op jit(solution)/shard_map/pallas_call | solution.py:499
  (5 shorter events, 0.0 us)
Async XLA Ops:
  0.6 6.5 %copy-start = (bf16[48,8,512]{2,1,0:T(8,128)(2,1)S(1)}, bf16[48,8,512]{2,1,0:T(8,128)(2,1)}, u32[]{:S(2)}) copy-start(bf16[48,8,512]{2,1,0:T(8,128)(2,1)} %param.13) | copy-start | bytes 1179652
  0.6 6.5 %copy-start.1 = (bf16[48,8,512]{2,1,0:T(8,128)(2,1)S(1)}, bf16[48,8,512]{2,1,0:T(8,128)(2,1)}, u32[]{:S(2)}) copy-start(bf16[48,8,512]{2,1,0:T(8,128)(2,1)} %param.14) | copy-start | bytes 1179652
  0.7 6.5 %copy-start.2 = (f32[48,512]{1,0:T(8,128)S(1)}, f32[48,512]{1,0:T(8,128)}, u32[]{:S(2)}) copy-start(f32[48,512]{1,0:T(8,128)} %base.3) | copy-start | bytes 294916
  2.0 5.2 %copy-start.5 = (s32[48,64]{1,0:T(8,128)S(1)}, s32[48,64]{1,0:T(8,128)}, u32[]{:S(2)}) copy-start(s32[48,64]{1,0:T(8,128)} %perm.1) | copy-start | bytes 36868
  2.0 8.7 %collective-permute-start = (f32[48,512]{1,0:T(8,128)S(1)}, f32[48,512]{1,0:T(8,128)S(1)}, u32[]{:S(2)}, u32[]{:S(2)}) collective-permute-start(f32[48,512]{1,0:T(8,128)S(1)} %get-tuple-element.27), channel_id=1, source_target_pairs={{0,8},{8,0},{16,24},{24,16},{32,40},{40,32},{48,56},{56,48},{64,72... | collective-permute-start | bytes 294920 | tf_op jit(solution)/shard_map/ppermute | solution.py:433
  6.4 4.3 %collective-permute-start.1 = (f32[48,512]{1,0:T(8,128)S(1)}, f32[48,512]{1,0:T(8,128)S(1)}, u32[]{:S(2)}, u32[]{:S(2)}) collective-permute-start(f32[48,512]{1,0:T(8,128)S(1)} %get-tuple-element.28), channel_id=1, source_target_pairs={{8,16},{16,8},{24,32},{32,24},{40,48},{48,40},{56,64},{64,56},{72,... | collective-permute-start | bytes 294920 | tf_op jit(solution)/shard_map/ppermute | solution.py:434
  38.2 19.0 %copy-start.4 = (bf16[128,128]{1,0:T(8,128)(2,1)S(1)}, bf16[128,128]{1,0:T(8,128)(2,1)}, u32[]{:S(2)}) copy-start(bf16[128,128]{1,0:T(8,128)(2,1)} %constant.21.clone.unpack) | copy-start | bytes 98308
  57.9 13.0 %copy-start.3 = (bf16[64,512]{1,0:T(8,128)(2,1)S(1)}, bf16[64,512]{1,0:T(8,128)(2,1)}, u32[]{:S(2)}) copy-start(bf16[64,512]{1,0:T(8,128)(2,1)} %prolong.1) | copy-start | bytes 196612

commit v8 on v7

--- a/solution.py
+++ b/solution.py
@@ -35,7 +35,7 @@
 
 SRC_ROWS, ORB_AT, BASE_AT, META_AT, HALO_ROWS = 32, 32, 40, 44, 48
 IDX, SCALE, OWNER, SLOT = slice(0, 128), slice(128, 256), slice(256, 384), slice(384, 512)
-POT, IDS, GHOST_IDS = CELLS, CELLS + HALF, CELLS + HALF + 12
+POT, IDS, EDGE_IDS = CELLS, CELLS + HALF, CELLS + HALF + 12
 X, Z, Y, CORES = 4, 16, 4, 2
 DOM, ORB, OUTER = ("x", "z"), ("y", "core"), ("x", "y", "core")
 COPIES = Y * CORES
@@ -89,7 +89,7 @@
 
 
 def pack_kernel(scale_hbm, owner_hbm, slot_hbm, src_hbm, orb_hbm, base_hbm, perm_hbm, stiff_hbm, eig_hbm,
-                to_mate, to_other, factor_out, eig_out, stiff_out,
+                to_mate, to_other, ids_out, factor_out, eig_out, stiff_out,
                 scale, owner, slot, src, orb, base, perm, eig, to_left, to_right, sems):
     top, rows = CELLS - WIDTH, CELLS * WIDTH
     copies = [(scale_hbm, scale), (owner_hbm, owner), (slot_hbm, slot)]
@@ -125,6 +125,13 @@
             out[at, OWNER] = jnp.full((1, LANES), owner[edge_cell].astype(F32), F32)
             mark = slot[edge_cell].astype(F32) if i == end * (HALO - 1) else 1.0
             out[at, SLOT] = jnp.full((1, LANES), mark, F32)
+    lane = lax.broadcasted_iota(jnp.int32, (WIDTH, LANES), 1)
+    ids = [jnp.zeros((WIDTH, LANES), F32)] * 4
+    for c in range(CELLS):
+        ids[c % 4] = jnp.where(lane == c, (owner[c] * HALF + slot[c]).astype(F32), ids[c % 4])
+    for i, value in enumerate((owner[0], slot[0], owner[CELLS - 1], slot[CELLS - 1])):
+        ids[i] = jnp.where(lane == EDGE_IDS + i, value.astype(F32), ids[i])
+    ids_out[...] = (ids[0] + ids[1]) + (ids[2] + ids[3])
     even = lax.axis_index("z") % 2 == 0
     to_mate[...] = jnp.where(even, to_right[...], to_left[...])
     to_other[...] = jnp.where(even, to_left[...], to_right[...])
@@ -219,7 +226,7 @@
                 )
     row = lax.broadcasted_iota(jnp.int32, (WIDTH, LANES), 0)
     lane = lax.broadcasted_iota(jnp.int32, (WIDTH, LANES), 1)
-    at = jnp.where((lane >= IDS) & (lane < GHOST_IDS), row * 12 + lane - IDS, -1)
+    at = jnp.where((lane >= IDS) & (lane < EDGE_IDS), row * 12 + lane - IDS, -1)
     ids = jnp.zeros((WIDTH, LANES), F32)
     for c in range(CELLS):
         ids = jnp.where(at == c // 6 * 12 + c % 6, owner[c].astype(F32), ids)
@@ -232,7 +239,7 @@
     )
 
 
-def boundary_kernel(src, orb, base, index_own, factor_own, eig, of_mate, of_other, stiff, restrict_t, adjoint_mid,
+def boundary_kernel(src, orb, base, index_own, factor_own, eig, of_mate, of_other, ids_of_x, stiff, restrict_t, adjoint_mid,
                     projected_mid, adjoint_out, projected_out, ghost_out, left, right,
                     x, quarter, kin, shifted, factor, index, adjoint_ends, sems):
     near, edge = 2 * HALO * WIDTH, HALO * WIDTH
@@ -278,15 +285,17 @@
     copies[2].start()
     own_orb = jnp.concatenate([orb[0:edge], orb[last - edge :]], 0)
     own_x = jnp.concatenate([low_cells, high_cells], 0)
-    lane = lax.broadcasted_iota(jnp.int32, (1, LANES), 1)
-    ghost_ids = jnp.zeros((1, LANES), F32)
-    for i, row in enumerate((left[META_AT + HALO - 1 : META_AT + HALO], right[META_AT : META_AT + 1])):
-        ghost_ids = jnp.where(lane == GHOST_IDS + 2 * i, row[:, OWNER], ghost_ids)
-        ghost_ids = jnp.where(lane == GHOST_IDS + 2 * i + 1, row[:, SLOT], ghost_ids)
     added = projection(own_orb, own_x, group_of([*range(HALO), *range(CELLS - HALO, CELLS)]), restrict_t[...])
-    whole = projected_mid[...] + ghost_ids * (1.0 / COPIES) - step_rate * added
-    for i in range(X):
-        projected_out[i * HALF : (i + 1) * HALF] = whole
+    whole = projected_mid[...] - step_rate * added
+    member = lax.axis_index("y") * CORES + lax.axis_index("core")
+    x_of_ids = (lax.axis_index("x") + member) % X
+    row = lax.broadcasted_iota(jnp.int32, (WIDTH, LANES), 0)
+    lane = lax.broadcasted_iota(jnp.int32, (WIDTH, LANES), 1)
+    ids = jnp.where(row == x_of_ids, ids_of_x[0:1] * (X / COPIES), 0.0)
+    edges = jnp.where(lane >= EDGE_IDS, ids, 0.0)
+    for i in range(COPIES):
+        projected_out[tile(2 * i)] = whole[tile(i)] + edges
+        projected_out[tile(2 * i + 1)] = ids
     ghosts = jnp.concatenate([left[ORB_AT : ORB_AT + WIDTH], right[ORB_AT : ORB_AT + WIDTH]], 0)
     ghost_kin = dot(ghosts.astype(BF16), stiff[...])
     for i, e, base_row in (
@@ -301,21 +310,29 @@
         copy.wait()
 
 
-def sum_kernel(place, gathered, asking, unpack, out):
+def sum_kernel(gathered, asking, unpack, out):
     high, rest = split(gathered[...])
-    ids = dot(jnp.concatenate([high, asking[...].astype(BF16)], 0), unpack[...])
+    ids = dot(high, unpack[...])
     row = lax.broadcasted_iota(jnp.int32, ids.shape, 0) % WIDTH
     lane = lax.broadcasted_iota(jnp.int32, ids.shape, 1)
-    ids = jnp.where(jnp.where(lane < CELLS, lane // 6, 0) == row, ids, 0.0)
-    ids = jnp.sum(ids.reshape(Z + X, WIDTH, LANES), axis=1)
+    ids = jnp.where(lane // 6 == row, ids, 0.0)
+    ids = jnp.sum(ids.reshape(Z, WIDTH, LANES), axis=1)
     lane = lax.broadcasted_iota(jnp.int32, ids.shape, 1)
     row = lax.broadcasted_iota(jnp.int32, ids.shape, 0)
-    mine = jnp.where(row < Z, place[0:1], place[1:2])
-    slots = mine + (jnp.where(row < Z, row, (row - Z) * Z) * HALF + lane - POT).astype(F32)
-    ids = jnp.where((lane >= POT) & (lane < IDS), slots, ids)
-    known = jnp.where(lane[:Z] < IDS, ids[:Z], -1.0)
-    wanted = jnp.where(lane[Z:] < IDS + 2, ids[Z:], -2.0)
+    slots = ((lax.axis_index("x") * Z + row) * HALF + lane - POT).astype(F32)
+    known = jnp.where(lane < POT, ids, jnp.where(lane < IDS, slots, -1.0))
     known = jnp.transpose(jnp.concatenate([known, jnp.zeros((LANES - Z, LANES), F32)], 0))
+    z_at = lax.axis_index("z")
+    before = gathered[pl.ds(pl.multiple_of((z_at + Z - 1) % Z * WIDTH, WIDTH), WIDTH)]
+    after = gathered[pl.ds(pl.multiple_of((z_at + 1) % Z * WIDTH, WIDTH), WIDTH)]
+    before = jnp.where(z_at == 0, pltpu.roll(before, 1, 0), before)
+    after = jnp.where(z_at == Z - 1, pltpu.roll(after, WIDTH - 1, 0), after)
+    low_id = before[:, EDGE_IDS + 2 : EDGE_IDS + 3] * HALF + before[:, EDGE_IDS + 3 : EDGE_IDS + 4]
+    high_id = after[:, EDGE_IDS : EDGE_IDS + 1] * HALF + after[:, EDGE_IDS + 1 : EDGE_IDS + 2]
+    lane, row = lane[:WIDTH], row[:WIDTH]
+    slots = ((row * Z + z_at) * HALF + lane - POT).astype(F32)
+    wanted = jnp.where(lane < POT, asking[...], jnp.where(lane < IDS, slots, -2.0))
+    wanted = jnp.where(lane == IDS, low_id, jnp.where(lane == IDS + 1, high_id, wanted))
     total = jnp.zeros((2 * WIDTH, X * LANES), F32)
     for s in range(0, Z, 2):
         hot = [
@@ -383,15 +400,11 @@
     for k in range(CELLS):
         table[112 + k % 6, k] = 64.0
         table[118 + k % 6, k] = 1.0
-    for i in range(2):
-        table[GHOST_IDS + 2 * i, IDS + i] = 64.0
-        table[GHOST_IDS + 2 * i + 1, IDS + i] = 1.0
     return table
 
 
 def local(orbitals, adjoint_source, eigenvalues, cell_scale, base_potential, stiffness, face_perm, restrict,
           prolong, owner, pot_slot, potential):
-    x_at, z_at = lax.axis_index("x"), lax.axis_index("z")
     vmem = pl.BlockSpec(memory_space=pltpu.VMEM)
     params = pltpu.CompilerParams(vmem_limit_bytes=32 * 2**20)
     struct = jax.ShapeDtypeStruct
@@ -399,21 +412,19 @@
     orb2 = orbitals.reshape(CELLS * WIDTH, NODES)
     src2 = adjoint_source.reshape(CELLS * WIDTH, NODES)
     owner1 = owner.reshape(CELLS)
-    first = jnp.stack([x_at * Z, z_at]) * HALF
-    place = jnp.broadcast_to(first.astype(F32)[:, None], (2, LANES))
-
     hbm = pl.BlockSpec(memory_space=pltpu.HBM)
-    to_mate, to_other, factor, eig, stiff = pl.pallas_call(
+    to_mate, to_other, ids, factor, eig, stiff = pl.pallas_call(
         pack_kernel,
         out_shape=(
             struct((HALO_ROWS, NODES), F32),
             struct((HALO_ROWS, NODES), F32),
+            struct((WIDTH, LANES), F32),
             struct((CELLS, LANES), F32),
             struct((WIDTH, LANES), F32),
             struct((NODES, NODES), BF16),
         ),
         in_specs=[hbm] * 9,
-        out_specs=(vmem,) * 5,
+        out_specs=(vmem,) * 6,
         scratch_shapes=[
             pltpu.SMEM((CELLS,), F32),
             pltpu.SMEM((CELLS,), jnp.int32),
@@ -432,6 +443,7 @@
 
     of_mate = lax.ppermute(to_mate, DOM, [(i, i ^ 1) for i in range(X * Z)])
     of_other = lax.ppermute(to_other, DOM, [(i, i + 1 if i % 2 else i - 1) for i in range(1, X * Z - 1)])
+    ids_of_x = lax.ppermute(ids, OUTER, [((i // COPIES + i) % X * COPIES + i % COPIES, i) for i in range(X * COPIES)])
 
     rows = CELLS * WIDTH
     inner = rows - 2 * HALO * WIDTH
@@ -462,12 +474,12 @@
         boundary_kernel,
         out_shape=(
             struct((rows, NODES), BF16),
-            struct((X * HALF, LANES), F32),
+            struct((2 * HALF, LANES), F32),
             struct((2 * WIDTH, NODES), F32),
             struct((HALO_ROWS, NODES), F32),
             struct((HALO_ROWS, NODES), F32),
         ),
-        in_specs=[vmem] * 12,
+        in_specs=[vmem] * 13,
         out_specs=(hbm, vmem, vmem, vmem, vmem),
         scratch_shapes=[pltpu.VMEM((strip_rows, NODES), F32)] * 4
         + [
@@ -477,24 +489,23 @@
             pltpu.SemaphoreType.DMA((3,)),
         ],
         compiler_params=params,
-    )(src2, orb2, base_potential, index, factor, eig, of_mate, of_other, stiff, restrict_t, adjoint_mid,
+    )(src2, orb2, base_potential, index, factor, eig, of_mate, of_other, ids_of_x, stiff, restrict_t, adjoint_mid,
       projected_mid)
 
     def exchanged(array, axes):
         return lax.all_to_all(array, axes, split_axis=0, concat_axis=0, tiled=True)
 
-    projected, place, x_at = lax.optimization_barrier((projected, place, x_at))
-    tiles = exchanged(projected.reshape(X * COPIES, WIDTH, LANES), OUTER)
-    tiles = jnp.sum(tiles.reshape(X, COPIES, WIDTH, LANES), axis=1)
-    mine = lax.dynamic_slice(tiles, (x_at, 0, 0), (1, WIDTH, LANES), allow_negative_indices=False)
-    gathered = exchanged(jnp.broadcast_to(mine, (Z, WIDTH, LANES)), ("z",))
+    tiles = jnp.sum(exchanged(projected.reshape(COPIES, 2 * WIDTH, LANES), ORB), axis=0)
+    mine = jnp.broadcast_to(tiles[None, :WIDTH], (Z, WIDTH, LANES))
+    mine, asking = lax.optimization_barrier((mine, tiles[WIDTH:]))
+    gathered = exchanged(mine, ("z",))
     columns = pl.pallas_call(
         sum_kernel,
         out_shape=struct((X * HALF, LANES), F32),
-        in_specs=[vmem] * 4,
+        in_specs=[vmem] * 3,
         out_specs=vmem,
         compiler_params=params,
-    )(place, gathered.reshape(Z * WIDTH, LANES), tiles.reshape(X * WIDTH, LANES), jnp.asarray(unpack_table(), BF16))
+    )(gathered.reshape(Z * WIDTH, LANES), asking, jnp.asarray(unpack_table(), BF16))
     columns = exchanged(columns.reshape(X * COPIES, WIDTH, LANES), OUTER)
     updated, applied2 = pl.pallas_call(
         apply_kernel,

time: 72.6 us -> 70.7 us (0.974)
  blocking collectives: 57.3 us -> 41.2 us
  starting transfers between devices: 5.04 us -> 19.2 us
    all_to_all x3, blocking collectives: 57.3 us -> 41.2 us  [exchanged(): return lax.all_to_all(array, axes, split_axis=0, concat_axis=0, tiled=True)]
    ppermute x0 -> x1, starting transfers between devices: none -> 14.2 us  [local(): lax.ppermute(ids, OUTER, [((i // COPIES + i) % X * COPIES + i % COPIES, i...]
  transfers between devices with their start and end apart: 2 -> 3, of which waited for: 0 -> 0; matrix products, arithmetic and copies ran while one was open for 0% -> 0% of each run, Pallas kernels for 5% -> 5%
where the time goes in v8:
time: 70.7 us; the launch traced here: 70.3 us
  blocking collectives  41.2 us (58%)
  starting transfers between devices  19.2 us (27%)
  Pallas kernels  9.02 us (13%)
  between operations  0.81 us (1%)
    all_to_all x3, blocking collectives, exchanged(): return lax.all_to_all(array, axes, split_axis=0, concat_axis=0, tiled=True)  41.2 us
    ppermute x1, starting transfers between devices, local(): lax.ppermute(ids, OUTER, [((i // COPIES + i) % X * COPIES + i % COPIES, i...  14.2 us
    ppermute x1, starting transfers between devices, local(): of_mate = lax.ppermute(to_mate, DOM, [(i, i ^ 1) for i in range(X * Z)])  4.38 us
    pallas_call x1, Pallas kernels, local(): pl.pallas_call(interior_kernel, out_shape=(struct((inner, NODES), BF16),...  3.56 us
    pallas_call x1, Pallas kernels, local(): pl.pallas_call(boundary_kernel, out_shape=(struct((rows, NODES), BF16), s...  2.13 us
  transfers between devices with their start and end apart: 3, of which 0 were waited for; matrix products, arithmetic and copies ran while one was open for 0% of the time, Pallas kernels for 5%

profile of v8, /device:TPU:1, one launch (start us, length us, event | category | flops | bytes accessed | tf_op | source)
XLA Modules:
  0.0 70.3 jit_solution(11296780458048575168)
XLA Ops:
  0.6 0.0 copy-start
  0.6 0.0 copy-start.1
  0.7 0.0 copy-start.2
  0.7 0.0 copy-start.5
  0.7 1.3 %shard_map.148 = (f32[48,512]{1,0:T(8,128)S(1)}, f32[48,512]{1,0:T(8,128)S(1)}, f32[8,128]{1,0:T(8,128)S(1)}, f32[48,128]{1,0:T(8,128)S(1)}, f32[8,128]{1,0:T(8,128)S(1)}, /*index=5*/bf16[512,512]{1,0:T(8,128)(2,1)S(1)}) custom-call(f32[48]{0:T(128)} %scale_hbm.1, s32[48]{0:T(128)} %bitcast.21, s32[48]{0:T(128)} %slot_hbm.3, bf16[384,512]{1,0:T(8,128)(2,1)} %bitcast.14, ...), custom_call_target="tpu_custom_call" | custom-call | tf_op jit(solution)/shard_map/pallas_call | solution.py:416
  2.0 4.4 %collective-permute-start = (f32[48,512]{1,0:T(8,128)S(1)}, f32[48,512]{1,0:T(8,128)S(1)}, u32[]{:S(2)}, u32[]{:S(2)}) collective-permute-start(f32[48,512]{1,0:T(8,128)S(1)} %get-tuple-element.27), channel_id=1, source_target_pairs={{0,8},{8,0},{16,24},{24,16},{32,40},{40,32},{48,56},{56,48},{64,72... | collective-permute-start | bytes 294920 | tf_op jit(solution)/shard_map/ppermute | solution.py:444
  6.4 0.7 collective-permute-start.1
  7.1 14.2 %collective-permute-start.2 = (f32[8,128]{1,0:T(8,128)S(1)}, f32[8,128]{1,0:T(8,128)S(1)}, u32[]{:S(2)}, u32[]{:S(2)}) collective-permute-start(f32[8,128]{1,0:T(8,128)S(1)} %get-tuple-element.29), channel_id=1, source_target_pairs={{0,0},{129,1},{258,2},{387,3},{4,4},{133,5},{262,6},{391,7},{128,1... | collective-permute-start | bytes 12296 | tf_op jit(solution)/shard_map/ppermute | solution.py:446
  21.3 0.0 copy-done
  21.3 0.0 copy-done.1
  21.3 0.0 copy-done.2
  21.3 3.6 %shard_map.149 = (bf16[320,512]{1,0:T(8,128)(2,1)S(1)}, f32[64,128]{1,0:T(8,128)S(1)}, f32[384,512]{1,0:T(8,128)S(1)}, s32[384,128]{1,0:T(8,128)S(1)}, bf16[64,512]{1,0:T(8,128)(2,1)S(1)}) custom-call(s32[48]{0:T(128)} %bitcast.22, s32[48]{0:T(128)} %slot_hbm.3, bf16[64,512]{1,0:T(8,128)(2,1)} %bitcast.25, f32[64,64]{1,0:T(8,128)} %potential_hbm.1, ...), custom_call_target="tpu_custom_call" | custom-call | flops 1006632960 | bytes 4194304 | tf_op jit(solution)/shard_map/pallas_call | solution.py:450
  24.9 0.0 collective-permute-done.2.ids_of_x
  24.9 0.0 collective-permute-done.of_mate
  24.9 0.0 collective-permute-done.1.of_other
  24.9 2.1 %shard_map.150 = (bf16[384,512]{1,0:T(8,128)(2,1)}, f32[128,128]{1,0:T(8,128)S(1)}, f32[16,512]{1,0:T(8,128)S(1)}, f32[48,512]{1,0:T(8,128)S(1)}, f32[48,512]{1,0:T(8,128)S(1)}) custom-call(bf16[384,512]{1,0:T(8,128)(2,1)S(1)} %bitcast.16, bf16[384,512]{1,0:T(8,128)(2,1)S(1)} %bitcast.12, f32[48,512]{1,0:T(8,128)S(1)} %copy-done.2, ...), custom_call_target="tpu_custom_call" | custom-call | tf_op jit(solution)/shard_map/pallas_call | solution.py:473
  27.1 10.4 %all_to_all.15 = f32[8,16,128]{2,1,0:T(8,128)S(1)} all-to-all(f32[8,16,128]{2,1,0:T(8,128)S(1)} %bitcast.20), channel_id=1, replica_groups=mesh['x'=4,'z'=16,'y'=4,'core'=2] {'y','core'}, dimensions={0} | all-to-all | bytes 131072 | tf_op jit(solution)/shard_map/all_to_all | solution.py:496
  37.5 0.0 copy-start.4
  37.5 17.4 %all_to_all.16 = f32[16,8,128]{2,1,0:T(8,128)S(1)} all-to-all(f32[16,8,128]{2,1,0:T(8,128)S(1)} %broadcast_in_dim.2), channel_id=1, replica_groups=mesh['x'=4,'z'=16,'y'=4,'core'=2] {'z'}, dimensions={0} | all-to-all | bytes 131072 | tf_op jit(solution)/shard_map/all_to_all | solution.py:496
  54.9 0.8 %shard_map.151 = f32[256,128]{1,0:T(8,128)S(1)} custom-call(f32[128,128]{1,0:T(8,128)S(1)} %bitcast.19, f32[8,128]{1,0:T(8,128)S(1)} %get-tuple-element.36.asking, bf16[128,128]{1,0:T(8,128)(2,1)S(1)} %copy-done.4), custom_call_target="tpu_custom_call" | custom-call | tf_op jit(solution)/shard_map/pallas_call | solution.py:502
  55.7 0.0 copy-start.3
  55.7 13.3 %all_to_all.17 = f32[32,8,128]{2,1,0:T(8,128)S(1)} all-to-all(f32[32,8,128]{2,1,0:T(8,128)S(1)} %bitcast.18), channel_id=1, replica_groups=mesh['x'=4,'z'=16,'y'=4,'core'=2] {'x','y','core'}, dimensions={0} | all-to-all | bytes 262144 | tf_op jit(solution)/shard_map/all_to_all | solution.py:496
  69.1 0.0 copy-done.3
  69.1 1.2 %shard_map.152 = (f32[64,64]{1,0:T(8,128)}, bf16[384,512]{1,0:T(8,128)(2,1)}) custom-call(f32[256,128]{1,0:T(8,128)S(1)} %bitcast.17, bf16[384,512]{1,0:T(8,128)(2,1)S(1)} %bitcast.13, f32[384,512]{1,0:T(8,128)S(1)} %get-tuple-element.37.linear, f32[16,512]{1,0:T(8,128)S(1)} %get-tuple-element.38.ghost, f32[48,512]{1,0:T(8,128)S(1)} %get-tuple-element.39.left, ...), custom_call_target="tpu_custom_call" | custom-call | tf_op jit(solution)/shard_map/pallas_call | solution.py:510
  (5 shorter events, 0.0 us)
Async XLA Ops:
  0.6 20.6 %copy-start = (bf16[48,8,512]{2,1,0:T(8,128)(2,1)S(1)}, bf16[48,8,512]{2,1,0:T(8,128)(2,1)}, u32[]{:S(2)}) copy-start(bf16[48,8,512]{2,1,0:T(8,128)(2,1)} %param.13) | copy-start | bytes 1179652
  0.6 20.6 %copy-start.1 = (bf16[48,8,512]{2,1,0:T(8,128)(2,1)S(1)}, bf16[48,8,512]{2,1,0:T(8,128)(2,1)}, u32[]{:S(2)}) copy-start(bf16[48,8,512]{2,1,0:T(8,128)(2,1)} %param.14) | copy-start | bytes 1179652
  0.7 20.6 %copy-start.2 = (f32[48,512]{1,0:T(8,128)S(1)}, f32[48,512]{1,0:T(8,128)}, u32[]{:S(2)}) copy-start(f32[48,512]{1,0:T(8,128)} %base.3) | copy-start | bytes 294916
  0.7 20.6 %copy-start.5 = (s32[48,64]{1,0:T(8,128)S(1)}, s32[48,64]{1,0:T(8,128)}, u32[]{:S(2)}) copy-start(s32[48,64]{1,0:T(8,128)} %perm.1) | copy-start | bytes 36868
  2.0 22.9 %collective-permute-start = (f32[48,512]{1,0:T(8,128)S(1)}, f32[48,512]{1,0:T(8,128)S(1)}, u32[]{:S(2)}, u32[]{:S(2)}) collective-permute-start(f32[48,512]{1,0:T(8,128)S(1)} %get-tuple-element.27), channel_id=1, source_target_pairs={{0,8},{8,0},{16,24},{24,16},{32,40},{40,32},{48,56},{56,48},{64,72... | collective-permute-start | bytes 294920 | tf_op jit(solution)/shard_map/ppermute | solution.py:444
  6.4 18.5 %collective-permute-start.1 = (f32[48,512]{1,0:T(8,128)S(1)}, f32[48,512]{1,0:T(8,128)S(1)}, u32[]{:S(2)}, u32[]{:S(2)}) collective-permute-start(f32[48,512]{1,0:T(8,128)S(1)} %get-tuple-element.28), channel_id=1, source_target_pairs={{8,16},{16,8},{24,32},{32,24},{40,48},{48,40},{56,64},{64,56},{72,... | collective-permute-start | bytes 294920 | tf_op jit(solution)/shard_map/ppermute | solution.py:445
  7.1 17.8 %collective-permute-start.2 = (f32[8,128]{1,0:T(8,128)S(1)}, f32[8,128]{1,0:T(8,128)S(1)}, u32[]{:S(2)}, u32[]{:S(2)}) collective-permute-start(f32[8,128]{1,0:T(8,128)S(1)} %get-tuple-element.29), channel_id=1, source_target_pairs={{0,0},{129,1},{258,2},{387,3},{4,4},{133,5},{262,6},{391,7},{128,1... | collective-permute-start | bytes 12296 | tf_op jit(solution)/shard_map/ppermute | solution.py:446
  37.5 17.4 %copy-start.4 = (bf16[128,128]{1,0:T(8,128)(2,1)S(1)}, bf16[128,128]{1,0:T(8,128)(2,1)}, u32[]{:S(2)}) copy-start(bf16[128,128]{1,0:T(8,128)(2,1)} %constant.4.clone.unpack) | copy-start | bytes 98308
  55.7 13.3 %copy-start.3 = (bf16[64,512]{1,0:T(8,128)(2,1)S(1)}, bf16[64,512]{1,0:T(8,128)(2,1)}, u32[]{:S(2)}) copy-start(bf16[64,512]{1,0:T(8,128)(2,1)} %prolong.1) | copy-start | bytes 196612

commit v9 on v8

--- a/solution.py
+++ b/solution.py
@@ -239,17 +239,11 @@
     )
 
 
-def boundary_kernel(src, orb, base, index_own, factor_own, eig, of_mate, of_other, ids_of_x, stiff, restrict_t, adjoint_mid,
-                    projected_mid, adjoint_out, projected_out, ghost_out, left, right,
-                    x, quarter, kin, shifted, factor, index, adjoint_ends, sems):
+def boundary_kernel(src, orb, base, index_own, factor_own, eig, of_mate, of_other, ids_of_x, stiff, restrict_t,
+                    projected_mid, adjoint_ends, projected_out, ghost_out, left, right,
+                    x, quarter, kin, shifted, factor, index):
     near, edge = 2 * HALO * WIDTH, HALO * WIDTH
     last = CELLS * WIDTH
-    copies = [
-        pltpu.make_async_copy(adjoint_mid, adjoint_out.at[edge : last - edge], sems.at[0]),
-        pltpu.make_async_copy(adjoint_ends.at[0], adjoint_out.at[0:edge], sems.at[1]),
-        pltpu.make_async_copy(adjoint_ends.at[1], adjoint_out.at[last - edge : last], sems.at[2]),
-    ]
-    copies[0].start()
     even = lax.axis_index("z") % 2 == 0
     left[...] = jnp.where(even, of_other[...], of_mate[...])
     right[...] = jnp.where(even, of_mate[...], of_other[...])
@@ -281,8 +275,6 @@
     low_cells, high_cells = x[edge : 2 * edge], x[4 * edge : 5 * edge]
     adjoint_ends[0] = low_cells.astype(BF16)
     adjoint_ends[1] = high_cells.astype(BF16)
-    copies[1].start()
-    copies[2].start()
     own_orb = jnp.concatenate([orb[0:edge], orb[last - edge :]], 0)
     own_x = jnp.concatenate([low_cells, high_cells], 0)
     added = projection(own_orb, own_x, group_of([*range(HALO), *range(CELLS - HALO, CELLS)]), restrict_t[...])
@@ -306,11 +298,17 @@
             ghost_out[tile(i), cols(t)] = (
                 factor[tile(e)] * ghost_kin[tile(i), cols(t)] + base_row[:, cols(t)] * ghosts[tile(i), cols(t)]
             )
+
+
+def sum_kernel(gathered, asking, unpack, adjoint_mid, adjoint_ends, out, adjoint_out, sems):
+    edge, last = HALO * WIDTH, CELLS * WIDTH
+    copies = [
+        pltpu.make_async_copy(adjoint_mid, adjoint_out.at[edge : last - edge], sems.at[0]),
+        pltpu.make_async_copy(adjoint_ends.at[0], adjoint_out.at[0:edge], sems.at[1]),
+        pltpu.make_async_copy(adjoint_ends.at[1], adjoint_out.at[last - edge : last], sems.at[2]),
+    ]
     for copy in copies:
-        copy.wait()
-
-
-def sum_kernel(gathered, asking, unpack, out):
+        copy.start()
     high, rest = split(gathered[...])
     ids = dot(high, unpack[...])
     row = lax.broadcasted_iota(jnp.int32, ids.shape, 0) % WIDTH
@@ -347,6 +345,8 @@
     for m in range(X):
         for i in range(COPIES):
             out[tile(m * COPIES + i)] = result[:, cols(m)]
+    for copy in copies:
+        copy.wait()
 
 
 def apply_kernel(columns, orb, linear, ghost, left, right, index, prolong, updated_out, applied_out):
@@ -470,26 +470,24 @@
     )(*map(in_hbm, (owner1, pot_slot, restrict.T, potential)), src2, orb2, base_potential, face_perm, factor, eig, stiff)
 
     strip_rows = 2 * STRIP * WIDTH
-    adjoint2, projected, ghost, left, right = pl.pallas_call(
+    adjoint_ends, projected, ghost, left, right = pl.pallas_call(
         boundary_kernel,
         out_shape=(
-            struct((rows, NODES), BF16),
+            struct((2, HALO * WIDTH, NODES), BF16),
             struct((2 * HALF, LANES), F32),
             struct((2 * WIDTH, NODES), F32),
             struct((HALO_ROWS, NODES), F32),
             struct((HALO_ROWS, NODES), F32),
         ),
-        in_specs=[vmem] * 13,
-        out_specs=(hbm, vmem, vmem, vmem, vmem),
+        in_specs=[vmem] * 12,
+        out_specs=(vmem,) * 5,
         scratch_shapes=[pltpu.VMEM((strip_rows, NODES), F32)] * 4
         + [
             pltpu.VMEM((strip_rows, LANES), F32),
             pltpu.VMEM((strip_rows, LANES), jnp.int32),
-            pltpu.VMEM((2, HALO * WIDTH, NODES), BF16),
-            pltpu.SemaphoreType.DMA((3,)),
         ],
         compiler_params=params,
-    )(src2, orb2, base_potential, index, factor, eig, of_mate, of_other, ids_of_x, stiff, restrict_t, adjoint_mid,
+    )(src2, orb2, base_potential, index, factor, eig, of_mate, of_other, ids_of_x, stiff, restrict_t,
       projected_mid)
 
     def exchanged(array, axes):
@@ -499,13 +497,15 @@
     mine = jnp.broadcast_to(tiles[None, :WIDTH], (Z, WIDTH, LANES))
     mine, asking = lax.optimization_barrier((mine, tiles[WIDTH:]))
     gathered = exchanged(mine, ("z",))
-    columns = pl.pallas_call(
+    columns, adjoint2 = pl.pallas_call(
         sum_kernel,
-        out_shape=struct((X * HALF, LANES), F32),
-        in_specs=[vmem] * 3,
-        out_specs=vmem,
+        out_shape=(struct((X * HALF, LANES), F32), struct((rows, NODES), BF16)),
+        in_specs=[vmem] * 5,
+        out_specs=(vmem, hbm),
+        scratch_shapes=[pltpu.SemaphoreType.DMA((3,))],
         compiler_params=params,
-    )(gathered.reshape(Z * WIDTH, LANES), asking, jnp.asarray(unpack_table(), BF16))
+    )(gathered.reshape(Z * WIDTH, LANES), asking, jnp.asarray(unpack_table(), BF16),
+      adjoint_mid, adjoint_ends)
     columns = exchanged(columns.reshape(X * COPIES, WIDTH, LANES), OUTER)
     updated, applied2 = pl.pallas_call(
         apply_kernel,

time: 70.7 us -> 70.1 us (level)
  no operation moved by 1% of the time
where the time goes in v9:
time: 70.1 us; the launch traced here: 69.7 us
  blocking collectives  41.2 us (59%)
  starting transfers between devices  19.2 us (27%)
  Pallas kernels  8.46 us (12%)
  between operations  0.81 us (1%)
    all_to_all x3, blocking collectives, exchanged(): return lax.all_to_all(array, axes, split_axis=0, concat_axis=0, tiled=True)  41.2 us
    ppermute x1, starting transfers between devices, local(): lax.ppermute(ids, OUTER, [((i // COPIES + i) % X * COPIES + i % COPIES, i...  14.2 us
    ppermute x1, starting transfers between devices, local(): of_mate = lax.ppermute(to_mate, DOM, [(i, i ^ 1) for i in range(X * Z)])  4.38 us
    pallas_call x1, Pallas kernels, local(): pl.pallas_call(interior_kernel, out_shape=(struct((inner, NODES), BF16),...  3.56 us
    pallas_call x1, Pallas kernels, local(): pl.pallas_call(boundary_kernel, out_shape=(struct((2, HALO * WIDTH, NODES...  1.54 us
  transfers between devices with their start and end apart: 3, of which 0 were waited for; matrix products, arithmetic and copies ran while one was open for 0% of the time, Pallas kernels for 5%

profile of v9, /device:TPU:1, one launch (start us, length us, event | category | flops | bytes accessed | tf_op | source)
XLA Modules:
  0.0 69.7 jit_solution(5876962461430323080)
XLA Ops:
  0.6 0.0 copy-start
  0.6 0.0 copy-start.1
  0.7 0.0 copy-start.2
  0.7 0.0 copy-start.5
  0.7 1.3 %shard_map.148 = (f32[48,512]{1,0:T(8,128)S(1)}, f32[48,512]{1,0:T(8,128)S(1)}, f32[8,128]{1,0:T(8,128)S(1)}, f32[48,128]{1,0:T(8,128)S(1)}, f32[8,128]{1,0:T(8,128)S(1)}, /*index=5*/bf16[512,512]{1,0:T(8,128)(2,1)S(1)}) custom-call(f32[48]{0:T(128)} %scale_hbm.1, s32[48]{0:T(128)} %bitcast.21, s32[48]{0:T(128)} %slot_hbm.3, bf16[384,512]{1,0:T(8,128)(2,1)} %bitcast.14, ...), custom_call_target="tpu_custom_call" | custom-call | tf_op jit(solution)/shard_map/pallas_call | solution.py:416
  2.0 4.4 %collective-permute-start = (f32[48,512]{1,0:T(8,128)S(1)}, f32[48,512]{1,0:T(8,128)S(1)}, u32[]{:S(2)}, u32[]{:S(2)}) collective-permute-start(f32[48,512]{1,0:T(8,128)S(1)} %get-tuple-element.29), channel_id=1, source_target_pairs={{0,8},{8,0},{16,24},{24,16},{32,40},{40,32},{48,56},{56,48},{64,72... | collective-permute-start | bytes 294920 | tf_op jit(solution)/shard_map/ppermute | solution.py:444
  6.4 0.7 collective-permute-start.1
  7.1 14.2 %collective-permute-start.2 = (f32[8,128]{1,0:T(8,128)S(1)}, f32[8,128]{1,0:T(8,128)S(1)}, u32[]{:S(2)}, u32[]{:S(2)}) collective-permute-start(f32[8,128]{1,0:T(8,128)S(1)} %get-tuple-element.31), channel_id=1, source_target_pairs={{0,0},{129,1},{258,2},{387,3},{4,4},{133,5},{262,6},{391,7},{128,1... | collective-permute-start | bytes 12296 | tf_op jit(solution)/shard_map/ppermute | solution.py:446
  21.3 0.0 copy-done
  21.3 0.0 copy-done.1
  21.3 0.0 copy-done.2
  21.3 3.6 %shard_map.149 = (bf16[320,512]{1,0:T(8,128)(2,1)S(1)}, f32[64,128]{1,0:T(8,128)S(1)}, f32[384,512]{1,0:T(8,128)S(1)}, s32[384,128]{1,0:T(8,128)S(1)}, bf16[64,512]{1,0:T(8,128)(2,1)S(1)}) custom-call(s32[48]{0:T(128)} %bitcast.22, s32[48]{0:T(128)} %slot_hbm.3, bf16[64,512]{1,0:T(8,128)(2,1)} %bitcast.25, f32[64,64]{1,0:T(8,128)} %potential_hbm.1, ...), custom_call_target="tpu_custom_call" | custom-call | flops 1006632960 | bytes 4194304 | tf_op jit(solution)/shard_map/pallas_call | solution.py:450
  24.9 0.0 collective-permute-done.2.ids_of_x
  24.9 0.0 collective-permute-done.of_mate
  24.9 0.0 collective-permute-done.1.of_other
  24.9 1.5 %shard_map.150 = (bf16[2,32,512]{2,1,0:T(8,128)(2,1)S(1)}, f32[128,128]{1,0:T(8,128)S(1)}, f32[16,512]{1,0:T(8,128)S(1)}, f32[48,512]{1,0:T(8,128)S(1)}, f32[48,512]{1,0:T(8,128)S(1)}) custom-call(bf16[384,512]{1,0:T(8,128)(2,1)S(1)} %bitcast.16, bf16[384,512]{1,0:T(8,128)(2,1)S(1)} %bitcast.12, f32[48,512]{1,0:T(8,128)S(1)} %copy-done.2, ...), custom_call_target="tpu_custom_call" | custom-call | tf_op jit(solution)/shard_map/pallas_call | solution.py:473
  26.5 10.4 %all_to_all.15 = f32[8,16,128]{2,1,0:T(8,128)S(1)} all-to-all(f32[8,16,128]{2,1,0:T(8,128)S(1)} %bitcast.20), channel_id=1, replica_groups=mesh['x'=4,'z'=16,'y'=4,'core'=2] {'y','core'}, dimensions={0} | all-to-all | bytes 131072 | tf_op jit(solution)/shard_map/all_to_all | solution.py:494
  36.9 0.0 copy-start.4
  36.9 17.4 %all_to_all.16 = f32[16,8,128]{2,1,0:T(8,128)S(1)} all-to-all(f32[16,8,128]{2,1,0:T(8,128)S(1)} %broadcast_in_dim.2), channel_id=1, replica_groups=mesh['x'=4,'z'=16,'y'=4,'core'=2] {'z'}, dimensions={0} | all-to-all | bytes 131072 | tf_op jit(solution)/shard_map/all_to_all | solution.py:494
  54.3 0.8 %shard_map.151 = (f32[256,128]{1,0:T(8,128)S(1)}, bf16[384,512]{1,0:T(8,128)(2,1)}) custom-call(f32[128,128]{1,0:T(8,128)S(1)} %bitcast.18, f32[8,128]{1,0:T(8,128)S(1)} %get-tuple-element.36.asking, bf16[128,128]{1,0:T(8,128)(2,1)S(1)} %copy-done.4, bf16[320,512]{1,0:T(8,128)(2,1)S(1)} %get-tuple-element.37.adjoint_mid, ...), custom_call_target="tpu_custom_call" | custom-call | tf_op jit(solution)/shard_map/pallas_call | solution.py:500
  55.2 0.0 copy-start.3
  55.2 13.3 %all_to_all.17 = f32[32,8,128]{2,1,0:T(8,128)S(1)} all-to-all(f32[32,8,128]{2,1,0:T(8,128)S(1)} %bitcast.19), channel_id=1, replica_groups=mesh['x'=4,'z'=16,'y'=4,'core'=2] {'x','y','core'}, dimensions={0} | all-to-all | bytes 262144 | tf_op jit(solution)/shard_map/all_to_all | solution.py:494
  68.5 0.0 copy-done.3
  68.5 1.2 %shard_map.152 = (f32[64,64]{1,0:T(8,128)}, bf16[384,512]{1,0:T(8,128)(2,1)}) custom-call(f32[256,128]{1,0:T(8,128)S(1)} %bitcast.17, bf16[384,512]{1,0:T(8,128)(2,1)S(1)} %bitcast.13, f32[384,512]{1,0:T(8,128)S(1)} %get-tuple-element.41.linear, f32[16,512]{1,0:T(8,128)S(1)} %get-tuple-element.42.ghost, f32[48,512]{1,0:T(8,128)S(1)} %get-tuple-element.43.left, ...), custom_call_target="tpu_custom_call" | custom-call | tf_op jit(solution)/shard_map/pallas_call | solution.py:510
  (5 shorter events, 0.0 us)
Async XLA Ops:
  0.6 20.6 %copy-start = (bf16[48,8,512]{2,1,0:T(8,128)(2,1)S(1)}, bf16[48,8,512]{2,1,0:T(8,128)(2,1)}, u32[]{:S(2)}) copy-start(bf16[48,8,512]{2,1,0:T(8,128)(2,1)} %param.13) | copy-start | bytes 1179652
  0.6 20.6 %copy-start.1 = (bf16[48,8,512]{2,1,0:T(8,128)(2,1)S(1)}, bf16[48,8,512]{2,1,0:T(8,128)(2,1)}, u32[]{:S(2)}) copy-start(bf16[48,8,512]{2,1,0:T(8,128)(2,1)} %param.14) | copy-start | bytes 1179652
  0.7 20.6 %copy-start.2 = (f32[48,512]{1,0:T(8,128)S(1)}, f32[48,512]{1,0:T(8,128)}, u32[]{:S(2)}) copy-start(f32[48,512]{1,0:T(8,128)} %base.3) | copy-start | bytes 294916
  0.7 20.6 %copy-start.5 = (s32[48,64]{1,0:T(8,128)S(1)}, s32[48,64]{1,0:T(8,128)}, u32[]{:S(2)}) copy-start(s32[48,64]{1,0:T(8,128)} %perm.1) | copy-start | bytes 36868
  2.0 22.9 %collective-permute-start = (f32[48,512]{1,0:T(8,128)S(1)}, f32[48,512]{1,0:T(8,128)S(1)}, u32[]{:S(2)}, u32[]{:S(2)}) collective-permute-start(f32[48,512]{1,0:T(8,128)S(1)} %get-tuple-element.29), channel_id=1, source_target_pairs={{0,8},{8,0},{16,24},{24,16},{32,40},{40,32},{48,56},{56,48},{64,72... | collective-permute-start | bytes 294920 | tf_op jit(solution)/shard_map/ppermute | solution.py:444
  6.4 18.5 %collective-permute-start.1 = (f32[48,512]{1,0:T(8,128)S(1)}, f32[48,512]{1,0:T(8,128)S(1)}, u32[]{:S(2)}, u32[]{:S(2)}) collective-permute-start(f32[48,512]{1,0:T(8,128)S(1)} %get-tuple-element.30), channel_id=1, source_target_pairs={{8,16},{16,8},{24,32},{32,24},{40,48},{48,40},{56,64},{64,56},{72,... | collective-permute-start | bytes 294920 | tf_op jit(solution)/shard_map/ppermute | solution.py:445
  7.1 17.8 %collective-permute-start.2 = (f32[8,128]{1,0:T(8,128)S(1)}, f32[8,128]{1,0:T(8,128)S(1)}, u32[]{:S(2)}, u32[]{:S(2)}) collective-permute-start(f32[8,128]{1,0:T(8,128)S(1)} %get-tuple-element.31), channel_id=1, source_target_pairs={{0,0},{129,1},{258,2},{387,3},{4,4},{133,5},{262,6},{391,7},{128,1... | collective-permute-start | bytes 12296 | tf_op jit(solution)/shard_map/ppermute | solution.py:446
  36.9 17.4 %copy-start.4 = (bf16[128,128]{1,0:T(8,128)(2,1)S(1)}, bf16[128,128]{1,0:T(8,128)(2,1)}, u32[]{:S(2)}) copy-start(bf16[128,128]{1,0:T(8,128)(2,1)} %constant.4.clone.unpack) | copy-start | bytes 98308
  55.2 13.4 %copy-start.3 = (bf16[64,512]{1,0:T(8,128)(2,1)S(1)}, bf16[64,512]{1,0:T(8,128)(2,1)}, u32[]{:S(2)}) copy-start(bf16[64,512]{1,0:T(8,128)(2,1)} %prolong.1) | copy-start | bytes 196612

commit v10 on v9

--- a/solution.py
+++ b/solution.py
@@ -125,8 +125,8 @@
             out[at, OWNER] = jnp.full((1, LANES), owner[edge_cell].astype(F32), F32)
             mark = slot[edge_cell].astype(F32) if i == end * (HALO - 1) else 1.0
             out[at, SLOT] = jnp.full((1, LANES), mark, F32)
-    lane = lax.broadcasted_iota(jnp.int32, (WIDTH, LANES), 1)
-    ids = [jnp.zeros((WIDTH, LANES), F32)] * 4
+    lane = lax.broadcasted_iota(jnp.int32, (1, LANES), 1)
+    ids = [jnp.zeros((1, LANES), F32)] * 4
     for c in range(CELLS):
         ids[c % 4] = jnp.where(lane == c, (owner[c] * HALF + slot[c]).astype(F32), ids[c % 4])
     for i, value in enumerate((owner[0], slot[0], owner[CELLS - 1], slot[CELLS - 1])):
@@ -283,7 +283,7 @@
     x_of_ids = (lax.axis_index("x") + member) % X
     row = lax.broadcasted_iota(jnp.int32, (WIDTH, LANES), 0)
     lane = lax.broadcasted_iota(jnp.int32, (WIDTH, LANES), 1)
-    ids = jnp.where(row == x_of_ids, ids_of_x[0:1] * (X / COPIES), 0.0)
+    ids = jnp.where(row == x_of_ids, ids_of_x[...] * (X / COPIES), 0.0)
     edges = jnp.where(lane >= EDGE_IDS, ids, 0.0)
     for i in range(COPIES):
         projected_out[tile(2 * i)] = whole[tile(i)] + edges
@@ -418,7 +418,7 @@
         out_shape=(
             struct((HALO_ROWS, NODES), F32),
             struct((HALO_ROWS, NODES), F32),
-            struct((WIDTH, LANES), F32),
+            struct((1, LANES), F32),
             struct((CELLS, LANES), F32),
             struct((WIDTH, LANES), F32),
             struct((NODES, NODES), BF16),

time: 70.1 us -> 70 us (level)
  no operation moved by 1% of the time
where the time goes in v10:
time: 70 us; the launch traced here: 69.7 us
  blocking collectives  41.1 us (59%)
  starting transfers between devices  19.2 us (27%)
  Pallas kernels  8.47 us (12%)
  between operations  0.81 us (1%)
    all_to_all x3, blocking collectives, exchanged(): return lax.all_to_all(array, axes, split_axis=0, concat_axis=0, tiled=True)  41.1 us
    ppermute x1, starting transfers between devices, local(): lax.ppermute(ids, OUTER, [((i // COPIES + i) % X * COPIES + i % COPIES, i...  14.2 us
    ppermute x1, starting transfers between devices, local(): of_mate = lax.ppermute(to_mate, DOM, [(i, i ^ 1) for i in range(X * Z)])  4.38 us
    pallas_call x1, Pallas kernels, local(): pl.pallas_call(interior_kernel, out_shape=(struct((inner, NODES), BF16),...  3.56 us
    pallas_call x1, Pallas kernels, local(): pl.pallas_call(boundary_kernel, out_shape=(struct((2, HALO * WIDTH, NODES...  1.54 us
  transfers between devices with their start and end apart: 3, of which 0 were waited for; matrix products, arithmetic and copies ran while one was open for 0% of the time, Pallas kernels for 5%

profile of v10, /device:TPU:1, one launch (start us, length us, event | category | flops | bytes accessed | tf_op | source)
XLA Modules:
  0.0 69.7 jit_solution(5965498362735643128)
XLA Ops:
  0.6 0.0 copy-start
  0.6 0.0 copy-start.1
  0.7 0.0 copy-start.2
  0.7 0.0 copy-start.5
  0.7 1.3 %shard_map.148 = (f32[48,512]{1,0:T(8,128)S(1)}, f32[48,512]{1,0:T(8,128)S(1)}, f32[1,128]{1,0:T(1,128)S(1)}, f32[48,128]{1,0:T(8,128)S(1)}, f32[8,128]{1,0:T(8,128)S(1)}, /*index=5*/bf16[512,512]{1,0:T(8,128)(2,1)S(1)}) custom-call(f32[48]{0:T(128)} %scale_hbm.1, s32[48]{0:T(128)} %bitcast.21, s32[48]{0:T(128)} %slot_hbm.3, bf16[384,512]{1,0:T(8,128)(2,1)} %bitcast.14, ...), custom_call_target="tpu_custom_call" | custom-call | tf_op jit(solution)/shard_map/pallas_call | solution.py:416
  2.0 4.4 %collective-permute-start = (f32[48,512]{1,0:T(8,128)S(1)}, f32[48,512]{1,0:T(8,128)S(1)}, u32[]{:S(2)}, u32[]{:S(2)}) collective-permute-start(f32[48,512]{1,0:T(8,128)S(1)} %get-tuple-element.29), channel_id=1, source_target_pairs={{0,8},{8,0},{16,24},{24,16},{32,40},{40,32},{48,56},{56,48},{64,72... | collective-permute-start | bytes 294920 | tf_op jit(solution)/shard_map/ppermute | solution.py:444
  6.4 0.7 collective-permute-start.1
  7.1 14.2 %collective-permute-start.2 = (f32[1,128]{1,0:T(1,128)S(1)}, f32[1,128]{1,0:T(1,128)S(1)}, u32[]{:S(2)}, u32[]{:S(2)}) collective-permute-start(f32[1,128]{1,0:T(1,128)S(1)} %get-tuple-element.31), channel_id=1, source_target_pairs={{0,0},{129,1},{258,2},{387,3},{4,4},{133,5},{262,6},{391,7},{128,1... | collective-permute-start | bytes 1544 | tf_op jit(solution)/shard_map/ppermute | solution.py:446
  21.3 0.0 copy-done
  21.3 0.0 copy-done.1
  21.3 0.0 copy-done.2
  21.3 3.6 %shard_map.149 = (bf16[320,512]{1,0:T(8,128)(2,1)S(1)}, f32[64,128]{1,0:T(8,128)S(1)}, f32[384,512]{1,0:T(8,128)S(1)}, s32[384,128]{1,0:T(8,128)S(1)}, bf16[64,512]{1,0:T(8,128)(2,1)S(1)}) custom-call(s32[48]{0:T(128)} %bitcast.22, s32[48]{0:T(128)} %slot_hbm.3, bf16[64,512]{1,0:T(8,128)(2,1)} %bitcast.25, f32[64,64]{1,0:T(8,128)} %potential_hbm.1, ...), custom_call_target="tpu_custom_call" | custom-call | flops 1006632960 | bytes 4194304 | tf_op jit(solution)/shard_map/pallas_call | solution.py:450
  24.9 0.0 collective-permute-done.2.ids_of_x
  24.9 0.0 collective-permute-done.of_mate
  24.9 0.0 collective-permute-done.1.of_other
  24.9 1.5 %shard_map.150 = (bf16[2,32,512]{2,1,0:T(8,128)(2,1)S(1)}, f32[128,128]{1,0:T(8,128)S(1)}, f32[16,512]{1,0:T(8,128)S(1)}, f32[48,512]{1,0:T(8,128)S(1)}, f32[48,512]{1,0:T(8,128)S(1)}) custom-call(bf16[384,512]{1,0:T(8,128)(2,1)S(1)} %bitcast.16, bf16[384,512]{1,0:T(8,128)(2,1)S(1)} %bitcast.12, f32[48,512]{1,0:T(8,128)S(1)} %copy-done.2, ...), custom_call_target="tpu_custom_call" | custom-call | tf_op jit(solution)/shard_map/pallas_call | solution.py:473
  26.5 10.4 %all_to_all.15 = f32[8,16,128]{2,1,0:T(8,128)S(1)} all-to-all(f32[8,16,128]{2,1,0:T(8,128)S(1)} %bitcast.20), channel_id=1, replica_groups=mesh['x'=4,'z'=16,'y'=4,'core'=2] {'y','core'}, dimensions={0} | all-to-all | bytes 131072 | tf_op jit(solution)/shard_map/all_to_all | solution.py:494
  36.9 0.0 copy-start.4
  36.9 17.4 %all_to_all.16 = f32[16,8,128]{2,1,0:T(8,128)S(1)} all-to-all(f32[16,8,128]{2,1,0:T(8,128)S(1)} %broadcast_in_dim.2), channel_id=1, replica_groups=mesh['x'=4,'z'=16,'y'=4,'core'=2] {'z'}, dimensions={0} | all-to-all | bytes 131072 | tf_op jit(solution)/shard_map/all_to_all | solution.py:494
  54.3 0.8 %shard_map.151 = (f32[256,128]{1,0:T(8,128)S(1)}, bf16[384,512]{1,0:T(8,128)(2,1)}) custom-call(f32[128,128]{1,0:T(8,128)S(1)} %bitcast.18, f32[8,128]{1,0:T(8,128)S(1)} %get-tuple-element.36.asking, bf16[128,128]{1,0:T(8,128)(2,1)S(1)} %copy-done.4, bf16[320,512]{1,0:T(8,128)(2,1)S(1)} %get-tuple-element.37.adjoint_mid, ...), custom_call_target="tpu_custom_call" | custom-call | tf_op jit(solution)/shard_map/pallas_call | solution.py:500
  55.1 0.0 copy-start.3
  55.2 13.3 %all_to_all.17 = f32[32,8,128]{2,1,0:T(8,128)S(1)} all-to-all(f32[32,8,128]{2,1,0:T(8,128)S(1)} %bitcast.19), channel_id=1, replica_groups=mesh['x'=4,'z'=16,'y'=4,'core'=2] {'x','y','core'}, dimensions={0} | all-to-all | bytes 262144 | tf_op jit(solution)/shard_map/all_to_all | solution.py:494
  68.4 0.0 copy-done.3
  68.4 1.2 %shard_map.152 = (f32[64,64]{1,0:T(8,128)}, bf16[384,512]{1,0:T(8,128)(2,1)}) custom-call(f32[256,128]{1,0:T(8,128)S(1)} %bitcast.17, bf16[384,512]{1,0:T(8,128)(2,1)S(1)} %bitcast.13, f32[384,512]{1,0:T(8,128)S(1)} %get-tuple-element.41.linear, f32[16,512]{1,0:T(8,128)S(1)} %get-tuple-element.42.ghost, f32[48,512]{1,0:T(8,128)S(1)} %get-tuple-element.43.left, ...), custom_call_target="tpu_custom_call" | custom-call | tf_op jit(solution)/shard_map/pallas_call | solution.py:510
  (5 shorter events, 0.0 us)
Async XLA Ops:
  0.6 20.6 %copy-start = (bf16[48,8,512]{2,1,0:T(8,128)(2,1)S(1)}, bf16[48,8,512]{2,1,0:T(8,128)(2,1)}, u32[]{:S(2)}) copy-start(bf16[48,8,512]{2,1,0:T(8,128)(2,1)} %param.13) | copy-start | bytes 1179652
  0.6 20.6 %copy-start.1 = (bf16[48,8,512]{2,1,0:T(8,128)(2,1)S(1)}, bf16[48,8,512]{2,1,0:T(8,128)(2,1)}, u32[]{:S(2)}) copy-start(bf16[48,8,512]{2,1,0:T(8,128)(2,1)} %param.14) | copy-start | bytes 1179652
  0.7 20.6 %copy-start.2 = (f32[48,512]{1,0:T(8,128)S(1)}, f32[48,512]{1,0:T(8,128)}, u32[]{:S(2)}) copy-start(f32[48,512]{1,0:T(8,128)} %base.3) | copy-start | bytes 294916
  0.7 20.6 %copy-start.5 = (s32[48,64]{1,0:T(8,128)S(1)}, s32[48,64]{1,0:T(8,128)}, u32[]{:S(2)}) copy-start(s32[48,64]{1,0:T(8,128)} %perm.1) | copy-start | bytes 36868
  2.0 22.9 %collective-permute-start = (f32[48,512]{1,0:T(8,128)S(1)}, f32[48,512]{1,0:T(8,128)S(1)}, u32[]{:S(2)}, u32[]{:S(2)}) collective-permute-start(f32[48,512]{1,0:T(8,128)S(1)} %get-tuple-element.29), channel_id=1, source_target_pairs={{0,8},{8,0},{16,24},{24,16},{32,40},{40,32},{48,56},{56,48},{64,72... | collective-permute-start | bytes 294920 | tf_op jit(solution)/shard_map/ppermute | solution.py:444
  6.4 18.5 %collective-permute-start.1 = (f32[48,512]{1,0:T(8,128)S(1)}, f32[48,512]{1,0:T(8,128)S(1)}, u32[]{:S(2)}, u32[]{:S(2)}) collective-permute-start(f32[48,512]{1,0:T(8,128)S(1)} %get-tuple-element.30), channel_id=1, source_target_pairs={{8,16},{16,8},{24,32},{32,24},{40,48},{48,40},{56,64},{64,56},{72,... | collective-permute-start | bytes 294920 | tf_op jit(solution)/shard_map/ppermute | solution.py:445
  7.1 17.8 %collective-permute-start.2 = (f32[1,128]{1,0:T(1,128)S(1)}, f32[1,128]{1,0:T(1,128)S(1)}, u32[]{:S(2)}, u32[]{:S(2)}) collective-permute-start(f32[1,128]{1,0:T(1,128)S(1)} %get-tuple-element.31), channel_id=1, source_target_pairs={{0,0},{129,1},{258,2},{387,3},{4,4},{133,5},{262,6},{391,7},{128,1... | collective-permute-start | bytes 1544 | tf_op jit(solution)/shard_map/ppermute | solution.py:446
  36.9 17.4 %copy-start.4 = (bf16[128,128]{1,0:T(8,128)(2,1)S(1)}, bf16[128,128]{1,0:T(8,128)(2,1)}, u32[]{:S(2)}) copy-start(bf16[128,128]{1,0:T(8,128)(2,1)} %constant.4.clone.unpack) | copy-start | bytes 98308
  55.1 13.3 %copy-start.3 = (bf16[64,512]{1,0:T(8,128)(2,1)S(1)}, bf16[64,512]{1,0:T(8,128)(2,1)}, u32[]{:S(2)}) copy-start(bf16[64,512]{1,0:T(8,128)(2,1)} %prolong.1) | copy-start | bytes 196612
